TPU v7x, 32 devices: a whole 2x2x4 slice. The times are simulated.
32 devices in a mesh: prow: 4 (over y, x), pcol: 8 (over z, core).
Axes of the slice: x: 2, y: 2, z: 4, core: 2. Of those that a mesh axis runs over, the one named last changes fastest.
Arguments:
- ancestor_inverse: bfloat16 [6144, 6144], P('pcol', 'prow'), may hold values from -6 to 6
- lower_panel: bfloat16 [6144, 1024], P(('prow', 'pcol')), may hold values from -0.3125 to 0.3125
- pivot_inverse: float32 [256, 1024], P('pcol', 'prow'), may hold values from -6 to 6
- struct_list: int32 [4, 12], replicated, may hold values from -1 to 23, as said below
Outputs:
- off_inverse: bfloat16 [6144, 1024], P('pcol', 'prow')
- diag_inverse: float32 [256, 1024], P('pcol', 'prow')
Inputs may be any that keep to these rules, and one draw needn't show every extreme that they name: `struct_list`: each row lists distinct ancestor supernodes first, all within 12 cyclically consecutive ancestor numbers, then entries -1; every row has at least one ancestor and some row lists 12.
All inputs are finite; a program needn't handle non-finite values.
Results may differ from a plain program's by a relative error of at most 0.001.
Values may be sent and summed in bfloat16 or wider, within the bound.
No kernel may reach another device: no remote copies, remote signals or barrier semaphores. Data moves between devices by JAX's collectives and lax.ppermute only.
A program may use at most 64 MiB of HBM per device.

v0:
```python
import jax
import jax.numpy as jnp
from jax import lax
from jax.sharding import PartitionSpec as P

B = 256
NK = 4


def from_root(value, axis, root):
    mine = lax.axis_index(axis) == root
    return lax.psum(jnp.where(mine, value, jnp.zeros_like(value)), axis)


def membership(struct_list, ancestor_ids):
    listed = struct_list[:, :, None] == ancestor_ids[None, None, :]
    return jnp.transpose(jnp.any(listed, axis=1))


def body(ancestor_inverse, lower_panel, pivot_inverse, struct_list):
    row_count = ancestor_inverse.shape[0] // B
    col_count = ancestor_inverse.shape[1] // B
    grid_rows = lax.axis_size("prow")
    prow_index = lax.axis_index("prow")
    pcol_index = lax.axis_index("pcol")
    col_share = NK * B // grid_rows
    gathered = lax.all_gather(lower_panel, "pcol", axis=0, tiled=True)
    col_ids = prow_index * col_count + jnp.arange(col_count, dtype=jnp.int32)
    row_ids = pcol_index * row_count + jnp.arange(row_count, dtype=jnp.int32)
    member_cols = membership(struct_list, col_ids)
    member_rows = membership(struct_list, row_ids)
    scaled = gathered.reshape(col_count, B, NK, B) * member_cols[:, None, :, None].astype(
        jnp.bfloat16
    )
    masked = scaled.reshape(col_count * B, NK * B)
    partial_value = -jnp.dot(ancestor_inverse, masked, preferred_element_type=jnp.float32)
    share_sum = lax.psum_scatter(partial_value, "prow", scatter_dimension=1, tiled=True)
    columns = prow_index * col_share + jnp.arange(col_share, dtype=jnp.int32)
    block_of = columns // B
    one_hot = block_of[:, None] == jnp.arange(NK, dtype=jnp.int32)[None, :]
    row_mask = jnp.any(member_rows[:, None, :] & one_hot[None, :, :], axis=2).astype(jnp.float32)
    off_share = (share_sum.reshape(row_count, B, col_share) * row_mask[:, None, :]).reshape(
        row_count * B, col_share
    )
    off_inverse = off_share.astype(jnp.bfloat16)
    block_count = max(col_share // B, 1)
    column_width = col_share // block_count
    offset_blocks = pcol_index * row_count % col_count
    root_row = pcol_index * row_count // col_count
    piece = lax.dynamic_slice_in_dim(masked, offset_blocks * B, row_count * B, 0)
    lower_rows = from_root(piece, "prow", root_row)
    first_block = prow_index * col_share // B
    lower_slice = lax.dynamic_slice_in_dim(lower_rows, first_block * B, block_count * B, 1)
    lower_blocks = lower_slice.astype(jnp.float32).reshape(row_count * B, block_count, B)
    off_blocks = off_share.reshape(row_count * B, block_count, column_width)
    diag_term = jnp.einsum(
        "ikr,ikc->rkc", lower_blocks, off_blocks, precision=lax.Precision.HIGHEST
    ).reshape(B, col_share)
    diag_share = lax.psum_scatter(diag_term, "pcol", scatter_dimension=0, tiled=True)
    diag_inverse = pivot_inverse - diag_share
    return (off_inverse, diag_inverse)


def solution(mesh):
    placed = (P("pcol", "prow"), P(("prow", "pcol"), None), P("pcol", "prow"), P())
    return jax.shard_map(
        body,
        mesh=mesh,
        in_specs=placed,
        out_specs=(P("pcol", "prow"), P("pcol", "prow")),
        check_vma=False,
    )
```

profile of v0, /device:TPU:0, one launch (start us, length us, event | category | flops | bytes accessed | tf_op | source)
XLA Modules:
  0.0 207.7 jit_solution(7479622725887524552)
XLA Ops:
  7.2 0.0 copy-start
  7.2 0.0 all-gather.2.cloned.1.call-start
  7.2 0.7 all-gather.2.cloned.1.call-update
  7.9 0.0 all-reduce.2.cloned.1.call-start
  8.0 0.9 compare_reduce_fusion
  8.9 0.9 mul.43
  9.8 2.5 %copy.26 = bf16[192,8,4,256]{3,1,2,0:T(8,128)(2,1)} copy(bf16[192,8,4,256]{3,2,1,0:T(4,128)(2,1)S(1)} %bitcast.18) | data formatting | bytes 6291456
  12.3 38.4 %all-gather.2.cloned.1.call-done = bf16[1536,1024]{1,0:T(8,128)(2,1)} async-done(((bf16[192,1024]{1,0:T(8,128)(2,1)}), bf16[1536,1024]{1,0:T(8,128)(2,1)}) %all-gather.2.cloned.1.call-update) | async-done | bytes 3145744 | tf_op jit(solution)/shard_map/all_gather | solution.py:27
  50.7 4.4 %mul.45 = bf16[1536,1024]{1,0:T(8,128)(2,1)S(1)} multiply(bf16[1536,1024]{1,0:T(8,128)(2,1)} %all-gather.2.cloned.1.call-done, bf16[1536,1024]{1,0:T(8,128)(2,1)} %bitcast.19) | non-fusion elementwise | flops 1572864 | bytes 9437184 | tf_op jit(solution)/shard_map/mul | solution.py:32
  55.0 0.0 copy-start.1
  55.1 1.7 copy-done.1
  56.7 1.6 dynamic-slice_select_fusion
  58.4 0.0 all-reduce.2.cloned.1.call-update
  58.4 0.0 reduce-scatter.5.cloned.1.call-start
  58.4 0.0 copy-done
  58.5 6.2 %negate_bitcast_fusion = f32[768,1024]{0,1:T(8,128)} fusion(bf16[1536,1024]{1,0:T(8,128)(2,1)} %copy-done.1, bf16[768,1536]{1,0:T(8,128)(2,1)S(1)} %copy-done), kind=kOutput, calls=%fused_computation | convolution fusion | flops 2416705536 | bytes 8650752 | tf_op jit(solution)/shard_map/dot_general | solution.py:36
  64.7 0.0 copy-start.3
  64.7 0.0 reduce-scatter.5.cloned.1.call-update
  64.7 0.0 copy-start.2
  64.7 0.0 reduce-scatter.7.cloned.1.call-start
  64.8 0.6 copy-done.3
  65.3 0.2 compare_reduce_fusion.1
  65.6 0.1 and_reduce_fusion
  65.7 0.9 mul.48
  66.6 1.4 copy.20
  68.0 50.3 %all-reduce.2.cloned.1.call-done = bf16[768,1024]{1,0:T(8,128)(2,1)} async-done(((bf16[768,1024]{1,0:T(8,128)(2,1)}), bf16[768,1024]{1,0:T(8,128)(2,1)}) %all-reduce.2.cloned.1.call-update) | async-done | bytes 1572880 | tf_op jit(solution)/shard_map/psum | solution.py:12
  118.3 47.3 %reduce-scatter.5.cloned.1.call-done = f32[768,256]{0,1:T(8,128)} async-done(((f32[768,1024]{0,1:T(8,128)}), f32[768,256]{0,1:T(8,128)}) %reduce-scatter.5.cloned.1.call-update) | async-done | bytes 786448 | tf_op jit(solution)/shard_map/reduce_scatter | solution.py:37
  165.6 1.8 convolution_bitcast_fusion
  167.3 0.8 copy.24
  168.2 0.0 reduce-scatter.7.cloned.1.call-update
  168.2 0.0 copy-done.2
  168.2 0.8 copy.21
  169.0 1.2 multiply_convert_fusion
  170.2 0.9 copy.22
  171.1 27.6 %reduce-scatter.7.cloned.1.call-done = f32[32,256]{1,0:T(8,128)} async-done(((f32[256,256]{1,0:T(8,128)}), f32[32,256]{1,0:T(8,128)}) %reduce-scatter.7.cloned.1.call-update) | async-done | bytes 32784
  198.7 0.9 copy.25
  199.6 0.9 sub.19
  200.5 0.7 copy.23
  (6 shorter events, 0.0 us)
Async XLA Ops:
  7.2 51.3 %copy-start = (bf16[768,1536]{1,0:T(8,128)(2,1)S(1)}, bf16[768,1536]{1,0:T(8,128)(2,1)}, u32[]{:S(2)}) copy-start(bf16[768,1536]{1,0:T(8,128)(2,1)} %param.4) | copy-start | bytes 7077892
  7.2 43.5 %all-gather.2.cloned.1.call-start = ((), (), s32[]{:S(2)}) async-start(), calls=%async_computation.2 | async-start | bytes 3538944 | tf_op jit(solution)/shard_map/all_gather | solution.py:27
  7.9 110.4 %all-reduce.2.cloned.1.call-start = ((), (), s32[]{:S(2)}) async-start(), calls=%async_computation.4 | async-start | bytes 3145728 | tf_op jit(solution)/shard_map/psum | solution.py:12
  55.0 1.7 copy-start.1
  58.4 107.2 %reduce-scatter.5.cloned.1.call-start = ((), (), s32[]{:S(2)}) async-start(), calls=%async_computation.3 | async-start | bytes 3932160 | tf_op jit(solution)/shard_map/reduce_scatter | solution.py:37
  64.7 0.7 copy-start.3
  64.7 103.5 %copy-start.2 = (f32[32,256]{1,0:T(8,128)S(1)}, f32[32,256]{1,0:T(8,128)}, u32[]{:S(2)}) copy-start(f32[32,256]{1,0:T(8,128)} %param.6) | copy-start | bytes 98308
  64.7 134.0 %reduce-scatter.7.cloned.1.call-start = ((), (), s32[]{:S(2)}) async-start(), calls=%async_computation.5 | async-start | bytes 294912
Sparse Core Ops, SparseCore 0:
  9.7 40.9 all-gather.1
  58.5 59.7 all-reduce.1
  121.6 43.9 reduce-scatter.4
  168.3 30.3 reduce-scatter.6
where the time goes:
time: 208 us
  waiting for transfers between devices  164 us (79%)
  between operations  13.9 us (7%)
  local copies, waits for them, and re-layouts  12 us (6%)
  other arithmetic  9.39 us (5%)
  matrix products  7.96 us (4%)
    psum x1, waiting for transfers between devices, from_root(): return lax.psum(jnp.where(mine, value, jnp.zeros_like(value)), axis)  50.3 us
    reduce_scatter x1, waiting for transfers between devices, body(): lax.psum_scatter(partial_value, 'prow', scatter_dimension=1, tiled=True)  47.3 us
    all_gather x1, waiting for transfers between devices, body(): gathered = lax.all_gather(lower_panel, 'pcol', axis=0, tiled=True)  38.4 us
    unnamed x5, waiting for transfers between devices  28.4 us
    unnamed x14, local copies, waits for them, and re-layouts  8.78 us
    dot_general x1, matrix products, body(): jnp.dot(ancestor_inverse, masked, preferred_element_type=jnp.float32)  6.21 us
    mul x1, other arithmetic, body(): gathered.reshape(col_count, B, NK, B)  4.37 us
  transfers between devices with their start and end apart: 4, of which 4 were waited for; matrix products, arithmetic and copies ran while one was open for 8% of the time, Pallas kernels for 0%

commit v1 on v0

--- a/solution.py
+++ b/solution.py
@@ -1,10 +1,17 @@
+import functools
+
 import jax
 import jax.numpy as jnp
 from jax import lax
+from jax.experimental import pallas as pl
+from jax.experimental.pallas import tpu as pltpu
 from jax.sharding import PartitionSpec as P
 
 B = 256
 NK = 4
+AXES = ("prow", "pcol")
+HALF = 128
+TAIL = 16
 
 
 def from_root(value, axis, root):
@@ -17,7 +24,7 @@
     return jnp.transpose(jnp.any(listed, axis=1))
 
 
-def body(ancestor_inverse, lower_panel, pivot_inverse, struct_list):
+def general_body(ancestor_inverse, lower_panel, pivot_inverse, struct_list):
     row_count = ancestor_inverse.shape[0] // B
     col_count = ancestor_inverse.shape[1] // B
     grid_rows = lax.axis_size("prow")
@@ -61,6 +68,394 @@
     return (off_inverse, diag_inverse)
 
 
+ANY = pl.BlockSpec(memory_space=pl.ANY)
+VM = pl.BlockSpec(memory_space=pltpu.VMEM)
+SM = pl.BlockSpec(memory_space=pltpu.SMEM)
+
+
+def place():
+    p = lax.axis_index("prow")
+    q = lax.axis_index("pcol")
+    return p, q // 2, q % 2
+
+
+def is_member(struct_ref, level, ancestor):
+    found = struct_ref[level, 0] == ancestor
+    for slot in range(1, struct_ref.shape[1]):
+        found = found | (struct_ref[level, slot] == ancestor)
+    return found
+
+
+def call(kernel, outs, specs, scratch, flops, moved, name):
+    return pl.pallas_call(
+        kernel,
+        out_shape=outs,
+        in_specs=specs,
+        out_specs=jax.tree.map(lambda _: VM, outs),
+        scratch_shapes=scratch,
+        compiler_params=pltpu.CompilerParams(vmem_limit_bytes=40 * 2**20),
+        cost_estimate=pl.CostEstimate(flops=flops, bytes_accessed=moved, transcendentals=0),
+        name=name,
+    )
+
+
+def split_kernel(struct_ref, lower_ref, across_ref, first_ref, second_ref, own_ref):
+    p, z, c = place()
+    shard = lower_ref.shape[0]
+    start = (p * 8 + 2 * z + c) * shard
+    ancestor = start // B
+    edge = (ancestor + 1) * B - start
+    row = lax.broadcasted_iota(jnp.int32, (shard, B), 0)
+
+    def masked(flip):
+        level = p ^ flip
+        value = lower_ref[:, pl.ds(pl.multiple_of(level * B, B), B)]
+        low = is_member(struct_ref, level, ancestor).astype(jnp.int32)
+        high = is_member(struct_ref, level, ancestor + 1).astype(jnp.int32)
+        keep = jnp.where(row < edge, low, high) > 0
+        return jnp.where(keep, value.astype(jnp.float32), 0.0).astype(jnp.bfloat16)
+
+    across_ref[...] = masked(3)
+    x_part = masked(1)
+    y_part = masked(2)
+    first_ref[:shard] = x_part[:, :HALF]
+    first_ref[shard:] = y_part[:, :HALF]
+    second_ref[:shard] = x_part[:, HALF:]
+    second_ref[shard:] = y_part[:, HALF:]
+    own_ref[...] = masked(0)
+
+
+def assemble(pieces, panel, sems, shard, halves):
+    _, z, c = place()
+    middle = (z == 1) | (z == 2)
+
+    def copies(ref, flip, core, index):
+        at = pl.multiple_of(((z ^ flip) * 2 + core) * shard, shard)
+        if halves:
+            return [
+                pltpu.make_async_copy(
+                    ref.at[pl.ds(h * shard, shard)],
+                    panel.at[pl.ds(at, shard), pl.ds(h * HALF, HALF)],
+                    sems.at[index, h],
+                )
+                for h in range(2)
+            ]
+        return [pltpu.make_async_copy(ref, panel.at[pl.ds(at, shard)], sems.at[index, 0])]
+
+    plan = []
+    for side in range(2):
+        core = c if side == 0 else 1 - c
+        for slot, flip in enumerate((0, 1, 2, 3, 3)):
+            cond = None if slot < 3 else (middle if slot == 3 else jnp.logical_not(middle))
+            plan.append((cond, copies(pieces[side * 5 + slot], flip, core, side * 5 + slot)))
+
+    def each(act):
+        for cond, items in plan:
+            def go(items=items):
+                for item in items:
+                    act(item)
+            if cond is None:
+                go()
+            else:
+                pl.when(cond)(go)
+
+    each(lambda item: item.start())
+    return lambda: each(lambda item: item.wait())
+
+
+def encode(value):
+    top = jnp.max(jnp.abs(value), axis=0, keepdims=True)
+    power = jnp.floor(jnp.log2(jnp.maximum(top, 2e-34))) + 1.0
+    scaled = jnp.round(value * jnp.exp2(15.0 - power))
+    code = jnp.clip(scaled, -32767.0, 32767.0).astype(jnp.int32).astype(jnp.int16)
+    return code, power
+
+
+def put_coded(ref, values, block):
+    code, power = encode(values)
+    ref[block * B : (block + 1) * B] = code
+    return power
+
+
+def put_tail(ref, powers):
+    rows = len(powers) * B
+    row = lax.broadcasted_iota(jnp.int32, (TAIL, HALF), 0)
+    tail = jnp.zeros((TAIL, HALF), jnp.float32)
+    for block, power in enumerate(powers):
+        tail = jnp.where(row == block, power, tail)
+    ref[rows : rows + TAIL] = tail.astype(jnp.int32).astype(jnp.int16)
+
+
+def decode(ref, block, blocks):
+    tail = ref[blocks * B : blocks * B + TAIL].astype(jnp.int32).astype(jnp.float32)
+    step = jnp.exp2(tail[block : block + 1] - 15.0)
+    code = ref[block * B : (block + 1) * B].astype(jnp.int32).astype(jnp.float32)
+    return code * step
+
+
+def start_rows(a_ref, a_buf, sems):
+    blocks = a_buf.shape[0] // B
+    items = [
+        pltpu.make_async_copy(a_ref.at[pl.ds(b * B, B)], a_buf.at[pl.ds(b * B, B)], sems.at[b])
+        for b in range(blocks)
+    ]
+    for item in items:
+        item.start()
+    return items
+
+
+def chunk_kernel(kind, shard, *refs):
+    pieces = refs[:10]
+    a_ref = refs[10]
+    at = 11
+    came = None
+    if kind != "across":
+        came = refs[11]
+        at = 12
+    left_ref, right_ref = refs[at : at + 2]
+    lower_refs = refs[at + 2 : len(refs) - 4]
+    panel, a_buf, piece_sems, row_sems = refs[len(refs) - 4 :]
+    _, _, c = place()
+    halves = kind != "across"
+    wait_pieces = assemble(pieces, panel, piece_sems, shard, halves)
+    rows = start_rows(a_ref, a_buf, row_sems)
+    wait_pieces()
+    blocks = len(rows)
+    left_powers, right_powers = [], []
+    for b in range(blocks):
+        rows[b].wait()
+        total = -jnp.dot(
+            a_buf[b * B : (b + 1) * B], panel[...], preferred_element_type=jnp.float32
+        )
+        left, right = total[:, :HALF], total[:, HALF:]
+        if kind == "first":
+            right = right + decode(came, b, blocks)
+        if kind == "second":
+            left = left + decode(came, b, blocks)
+        left_powers.append(put_coded(left_ref, left, b))
+        right_powers.append(put_coded(right_ref, right, b))
+    put_tail(left_ref, left_powers)
+    put_tail(right_ref, right_powers)
+    share = blocks * B
+    kept = panel[pl.ds(pl.multiple_of(c * share, share), share)]
+    if halves:
+        lower_refs[0][...] = kept[:, :HALF]
+        lower_refs[1][...] = kept[:, HALF:]
+    else:
+        lower_refs[0][...] = kept
+
+
+def last_kernel(shard, *refs):
+    pieces = refs[:10]
+    a_ref, struct_ref, xa, ya, xb, yb, l_across, l_xa, l_ya, l_xb, l_yb = refs[10:21]
+    off_ref, diag_ref = refs[21:23]
+    panel, a_buf, lower, piece_sems, row_sems, lower_sems = refs[23:]
+    p, z, c = place()
+    wait_pieces = assemble(pieces, panel, piece_sems, shard, False)
+    rows = start_rows(a_ref, a_buf, row_sems)
+    share = lower.shape[0]
+    flip = p ^ z
+
+    def lower_copies(flip):
+        if flip == 3:
+            return [pltpu.make_async_copy(l_across, lower, lower_sems.at[0])]
+        pair = (l_xa, l_xb) if flip == 1 else (l_ya, l_yb)
+        return [
+            pltpu.make_async_copy(pair[h], lower.at[:, pl.ds(h * HALF, HALF)], lower_sems.at[h])
+            for h in range(2)
+        ]
+
+    for known in (1, 2, 3):
+        @pl.when(flip == known)
+        def _(known=known):
+            for item in lower_copies(known):
+                item.start()
+
+    wait_pieces()
+
+    @pl.when(flip == 0)
+    def _():
+        lower[...] = panel[pl.ds(pl.multiple_of(c * share, share), share)]
+
+    for known in (1, 2, 3):
+        @pl.when(flip == known)
+        def _(known=known):
+            for item in lower_copies(known):
+                item.wait()
+
+    blocks = len(rows)
+    first = (2 * z + c) * blocks
+    diag = jnp.zeros((B, B), jnp.float32)
+    contract = (((0,), (0,)), ((), ()))
+    for b in range(blocks):
+        rows[b].wait()
+        total = -jnp.dot(
+            a_buf[b * B : (b + 1) * B], panel[...], preferred_element_type=jnp.float32
+        )
+        left = total[:, :HALF] + (decode(xa, b, blocks) + decode(ya, b, blocks))
+        right = total[:, HALF:] + (decode(xb, b, blocks) + decode(yb, b, blocks))
+        total = jnp.concatenate([left, right], axis=1)
+        keep = is_member(struct_ref, p, first + b).astype(jnp.float32)
+        total = total * keep
+        high = total.astype(jnp.bfloat16)
+        low = (total - high.astype(jnp.float32)).astype(jnp.bfloat16)
+        off_ref[b * B : (b + 1) * B] = high
+        factor = lower[b * B : (b + 1) * B]
+        for part in (high, low):
+            diag = diag + lax.dot_general(
+                factor, part, contract, preferred_element_type=jnp.float32
+            )
+    piece = B // 8
+    panel_diag = diag_ref
+    for place_of in range(8):
+        panel_diag[pl.ds(pl.multiple_of((place_of ^ (2 * z + c)) * piece, piece), piece)] = diag[
+            place_of * piece : (place_of + 1) * piece
+        ]
+
+
+def pairs(move):
+    found = []
+    for p in range(4):
+        for z in range(4):
+            for c in range(2):
+                to = move(p, z, c)
+                if to is not None:
+                    found.append((p * 8 + 2 * z + c, to[0] * 8 + 2 * to[1] + to[2]))
+    return found
+
+
+def send(value, move):
+    return lax.ppermute(value, AXES, pairs(move))
+
+
+def mids(z):
+    return z in (1, 2)
+
+
+def gather(own):
+    one = send(own, lambda p, z, c: (p, z ^ 1, c))
+    two = send(own, lambda p, z, c: (p, z ^ 2, c))
+    mid = send(own, lambda p, z, c: (p, z ^ 3, c) if mids(z) else None)
+    end = send(two, lambda p, z, c: (p, z ^ 1, c) if mids(z) else None)
+    kept = [own, one, two, mid, end]
+    swap = lambda p, z, c: (p, z, 1 - c)
+    others = [
+        send(own, swap),
+        send(one, swap),
+        send(two, swap),
+        send(mid, lambda p, z, c: (p, z, 1 - c) if mids(z) else None),
+        send(end, lambda p, z, c: None if mids(z) else (p, z, 1 - c)),
+    ]
+    return kept + others
+
+
+def to_flip(flip):
+    return lambda p, z, c: (p ^ flip, z, c)
+
+
+def from_home(flip):
+    return lambda p, z, c: (p ^ flip, z, c) if p == z else None
+
+
+def line_body(ancestor_inverse, lower_panel, pivot_inverse, struct_list):
+    rows, depth = ancestor_inverse.shape
+    shard = lower_panel.shape[0]
+    blocks = rows // B
+    bf16, f32 = jnp.bfloat16, jnp.float32
+    across, first, second, own = call(
+        split_kernel,
+        (
+            jax.ShapeDtypeStruct((shard, B), bf16),
+            jax.ShapeDtypeStruct((2 * shard, HALF), bf16),
+            jax.ShapeDtypeStruct((2 * shard, HALF), bf16),
+            jax.ShapeDtypeStruct((shard, B), bf16),
+        ),
+        [SM, VM],
+        [],
+        shard * NK * B,
+        4 * shard * NK * B,
+        "split_lower",
+    )(struct_list, lower_panel)
+
+    coded = jax.ShapeDtypeStruct((rows + TAIL, HALF), jnp.int16)
+    scratch = [
+        pltpu.VMEM((depth, B), bf16),
+        pltpu.VMEM((rows, depth), bf16),
+        pltpu.SemaphoreType.DMA((10, 2)),
+        pltpu.SemaphoreType.DMA((blocks,)),
+    ]
+    flops = 2 * rows * depth * B
+    moved = 2 * rows * depth
+
+    def chunk(kind, pieces, came):
+        if kind == "across":
+            lower = (jax.ShapeDtypeStruct((rows, B), bf16),)
+        else:
+            lower = (jax.ShapeDtypeStruct((rows, HALF), bf16),) * 2
+        extra = [] if came is None else [came]
+        return call(
+            functools.partial(chunk_kernel, kind, shard),
+            (coded, coded) + lower,
+            [ANY] * 11 + [VM] * len(extra),
+            scratch,
+            flops,
+            moved,
+            "chunk_" + kind,
+        )(*pieces, ancestor_inverse, *extra)
+
+    to_x, to_y, lower_a = chunk("across", gather(across), None)
+    by_x = send(to_x, to_flip(1))
+    by_y = send(to_y, to_flip(2))
+    l_across = send(lower_a, from_home(3))
+
+    xa, ya, l_xa, l_ya = chunk("first", gather(first), by_x)
+    xa = send(xa, to_flip(1))
+    ya = send(ya, to_flip(2))
+    l_xa = send(l_xa, from_home(1))
+    l_ya = send(l_ya, from_home(2))
+
+    xb, yb, l_xb, l_yb = chunk("second", gather(second), by_y)
+    xb = send(xb, to_flip(1))
+    yb = send(yb, to_flip(2))
+    l_xb = send(l_xb, from_home(1))
+    l_yb = send(l_yb, from_home(2))
+
+    off_inverse, diag = call(
+        functools.partial(last_kernel, shard),
+        (jax.ShapeDtypeStruct((rows, B), bf16), jax.ShapeDtypeStruct((B, B), f32)),
+        [ANY] * 11 + [SM] + [VM] * 4 + [ANY] * 5,
+        scratch[:2]
+        + [pltpu.VMEM((rows, B), bf16)]
+        + scratch[2:]
+        + [pltpu.SemaphoreType.DMA((2,))],
+        flops,
+        moved,
+        "chunk_own",
+    )(*gather(own), ancestor_inverse, struct_list, xa, ya, xb, yb, l_across, l_xa, l_ya, l_xb, l_yb)
+
+    piece = B // 8
+    total = diag[:piece]
+    for flip in range(1, 8):
+        part = diag[flip * piece : (flip + 1) * piece]
+        total = total + send(part, lambda p, z, c: (p, z ^ (flip >> 1), c ^ (flip & 1)))
+    return off_inverse, pivot_inverse - total
+
+
+def body(ancestor_inverse, lower_panel, pivot_inverse, struct_list):
+    rows, depth = ancestor_inverse.shape
+    shard = lower_panel.shape[0]
+    line = (
+        lax.axis_size("prow") == 4
+        and lax.axis_size("pcol") == 8
+        and depth == 8 * shard
+        and depth == 2 * rows
+        and shard % 64 == 0
+        and shard <= B
+    )
+    plan = line_body if line else general_body
+    return plan(ancestor_inverse, lower_panel, pivot_inverse, struct_list)
+
+
 def solution(mesh):
     placed = (P("pcol", "prow"), P(("prow", "pcol"), None), P("pcol", "prow"), P())
     return jax.shard_map(

time: 208 us -> 108 us (0.52)
  the two profiles are of different devices: /device:TPU:0 before, /device:TPU:3 now
where the time goes in v1:
time: 108 us
  starting transfers between devices  65.2 us (60%)
  waiting for transfers between devices  24 us (22%)
  Pallas kernels  13.5 us (12%)
  local copies, waits for them, and re-layouts  3.37 us (3%)
    ppermute x54, starting transfers between devices, send(): return lax.ppermute(value, AXES, pairs(move))  65.2 us
    ppermute x54, waiting for transfers between devices, send(): return lax.ppermute(value, AXES, pairs(move))  24 us
    pallas_call x3, Pallas kernels, chunk(): call(functools.partial(chunk_kernel, kind, shard), (coded, coded) + lower...  7.79 us
    pallas_call x1, Pallas kernels, line_body(): call(functools.partial(last_kernel, shard), (jax.ShapeDtypeStruct((rows,...  4.96 us
    unnamed x12, local copies, waits for them, and re-layouts  3.35 us
  transfers between devices with their start and end apart: 54, of which 11 were waited for; matrix products, arithmetic and copies ran while one was open for 0% of the time, Pallas kernels for 7%

profile of v1, /device:TPU:3, one launch (start us, length us, event | category | flops | bytes accessed | tf_op | source)
XLA Modules:
  0.0 107.7 jit_solution(9522776545545588933)
XLA Ops:
  0.6 1.0 copy-done.2
  1.6 0.7 copy-done.3
  2.3 0.7 split_lower.1
  3.0 2.4 %collective-permute-start.19 = (bf16[192,256]{1,0:T(8,128)(2,1)S(1)}, bf16[192,256]{1,0:T(8,128)(2,1)S(1)}, u32[]{:S(2)}, u32[]{:S(2)}) collective-permute-start(bf16[192,256]{1,0:T(8,128)(2,1)S(1)} %get-tuple-element.21.refs_0_), channel_id=1, source_target_pairs={{0,4},{1,5},{2,6},{3,7},{4,0},{5,1},{6,2},{7,3},{8,12},{9,13},{10,... | collective-permute-start | bytes 294920 | tf_op jit(solution)/shard_map/ppermute | solution.py:328
  5.4 1.3 %collective-permute-start.18 = (bf16[192,256]{1,0:T(8,128)(2,1)S(1)}, bf16[192,256]{1,0:T(8,128)(2,1)S(1)}, u32[]{:S(2)}, u32[]{:S(2)}) collective-permute-start(bf16[192,256]{1,0:T(8,128)(2,1)S(1)} %get-tuple-element.21.refs_0_), channel_id=1, source_target_pairs={{0,2},{1,3},{2,0},{3,1},{4,6},{5,7},{6,4},{7,5},{8,10},{9,11},{10,... | collective-permute-start | bytes 294920 | tf_op jit(solution)/shard_map/ppermute | solution.py:328
  6.7 0.7 collective-permute-start.20
  7.4 1.3 %collective-permute-start.22 = (bf16[192,256]{1,0:T(8,128)(2,1)S(1)}, bf16[192,256]{1,0:T(8,128)(2,1)S(1)}, u32[]{:S(2)}, u32[]{:S(2)}) collective-permute-start(bf16[192,256]{1,0:T(8,128)(2,1)S(1)} %get-tuple-element.21.refs_0_), channel_id=1, source_target_pairs={{0,1},{1,0},{2,3},{3,2},{4,5},{5,4},{6,7},{7,6},{8,9},{9,8},{10,11... | collective-permute-start | bytes 294920 | tf_op jit(solution)/shard_map/ppermute | solution.py:328
  8.7 2.9 %collective-permute-start.31 = (bf16[384,128]{1,0:T(8,128)(2,1)S(1)}, bf16[384,128]{1,0:T(8,128)(2,1)S(1)}, u32[]{:S(2)}, u32[]{:S(2)}) collective-permute-start(bf16[384,128]{1,0:T(8,128)(2,1)S(1)} %get-tuple-element.25.refs_0_), channel_id=1, source_target_pairs={{0,4},{1,5},{2,6},{3,7},{4,0},{5,1},{6,2},{7,3},{8,12},{9,13},{10,... | collective-permute-start | bytes 294920 | tf_op jit(solution)/shard_map/ppermute | solution.py:328
  11.6 0.7 collective-permute-start.32
  12.3 0.6 collective-permute-start.34
  12.8 4.9 %collective-permute-start.10 = (bf16[384,128]{1,0:T(8,128)(2,1)S(1)}, bf16[384,128]{1,0:T(8,128)(2,1)S(1)}, u32[]{:S(2)}, u32[]{:S(2)}) collective-permute-start(bf16[384,128]{1,0:T(8,128)(2,1)S(1)} %get-tuple-element.20.refs_0_), channel_id=1, source_target_pairs={{0,4},{1,5},{2,6},{3,7},{4,0},{5,1},{6,2},{7,3},{8,12},{9,13},{10,... | collective-permute-start | bytes 294920 | tf_op jit(solution)/shard_map/ppermute | solution.py:328
  17.8 0.7 collective-permute-start.11
  18.5 1.2 %collective-permute-start.13 = (bf16[384,128]{1,0:T(8,128)(2,1)S(1)}, bf16[384,128]{1,0:T(8,128)(2,1)S(1)}, u32[]{:S(2)}, u32[]{:S(2)}) collective-permute-start(bf16[384,128]{1,0:T(8,128)(2,1)S(1)} %get-tuple-element.20.refs_0_), channel_id=1, source_target_pairs={{0,1},{1,0},{2,3},{3,2},{4,5},{5,4},{6,7},{7,6},{8,9},{9,8},{10,11... | collective-permute-start | bytes 294920 | tf_op jit(solution)/shard_map/ppermute | solution.py:328
  19.7 5.2 %collective-permute-start.1 = (bf16[192,256]{1,0:T(8,128)(2,1)S(1)}, bf16[192,256]{1,0:T(8,128)(2,1)S(1)}, u32[]{:S(2)}, u32[]{:S(2)}) collective-permute-start(bf16[192,256]{1,0:T(8,128)(2,1)S(1)} %get-tuple-element.19.refs_0_), channel_id=1, source_target_pairs={{0,4},{1,5},{2,6},{3,7},{4,0},{5,1},{6,2},{7,3},{8,12},{9,13},{10,... | collective-permute-start | bytes 294920 | tf_op jit(solution)/shard_map/ppermute | solution.py:328
  24.9 0.7 collective-permute-start.2
  25.6 0.4 collective-permute-start.4
  26.1 1.3 %collective-permute-start.21 = (bf16[192,256]{1,0:T(8,128)(2,1)S(1)}, bf16[192,256]{1,0:T(8,128)(2,1)S(1)}, u32[]{:S(2)}, u32[]{:S(2)}) collective-permute-start(bf16[192,256]{1,0:T(8,128)(2,1)S(1)} %collective-permute-done.19.refs_2_), channel_id=1, source_target_pairs={{2,0},{3,1},{4,6},{5,7},{10,8},{11,9},{12,14},{13,15},{18,16},{19,... | collective-permute-start | bytes 294920 | tf_op jit(solution)/shard_map/ppermute | solution.py:328
  27.4 3.0 %collective-permute-done.1.refs_2_ = bf16[192,256]{1,0:T(8,128)(2,1)S(1)} collective-permute-done((bf16[192,256]{1,0:T(8,128)(2,1)S(1)}, bf16[192,256]{1,0:T(8,128)(2,1)S(1)}, u32[]{:S(2)}, u32[]{:S(2)}) %collective-permute-start.1) | collective-permute-done | bytes 98336 | tf_op jit(solution)/shard_map/ppermute | solution.py:328
  30.3 0.9 collective-permute-start.24
  31.3 0.7 collective-permute-start.25
  32.0 1.3 %collective-permute-start.33 = (bf16[384,128]{1,0:T(8,128)(2,1)S(1)}, bf16[384,128]{1,0:T(8,128)(2,1)S(1)}, u32[]{:S(2)}, u32[]{:S(2)}) collective-permute-start(bf16[384,128]{1,0:T(8,128)(2,1)S(1)} %collective-permute-done.31.refs_2_), channel_id=1, source_target_pairs={{2,0},{3,1},{4,6},{5,7},{10,8},{11,9},{12,14},{13,15},{18,16},{19,... | collective-permute-start | bytes 294920 | tf_op jit(solution)/shard_map/ppermute | solution.py:328
  33.3 2.1 %collective-permute-done.21.refs_4_ = bf16[192,256]{1,0:T(8,128)(2,1)S(1)} collective-permute-done((bf16[192,256]{1,0:T(8,128)(2,1)S(1)}, bf16[192,256]{1,0:T(8,128)(2,1)S(1)}, u32[]{:S(2)}, u32[]{:S(2)}) %collective-permute-start.21) | collective-permute-done | bytes 98336 | tf_op jit(solution)/shard_map/ppermute | solution.py:328
  35.3 0.6 collective-permute-start.36
  35.9 1.9 %collective-permute-start.26 = (bf16[192,256]{1,0:T(8,128)(2,1)S(1)}, bf16[192,256]{1,0:T(8,128)(2,1)S(1)}, u32[]{:S(2)}, u32[]{:S(2)}) collective-permute-start(bf16[192,256]{1,0:T(8,128)(2,1)S(1)} %collective-permute-done.21.refs_4_), channel_id=1, source_target_pairs={{0,1},{1,0},{6,7},{7,6},{8,9},{9,8},{14,15},{15,14},{16,17},{17,16... | collective-permute-start | bytes 294920 | tf_op jit(solution)/shard_map/ppermute | solution.py:328
  37.9 0.6 collective-permute-start.35
  38.4 0.7 collective-permute-start.37
  39.1 0.8 collective-permute-done.33.refs_4_
  39.9 1.3 %collective-permute-start.12 = (bf16[384,128]{1,0:T(8,128)(2,1)S(1)}, bf16[384,128]{1,0:T(8,128)(2,1)S(1)}, u32[]{:S(2)}, u32[]{:S(2)}) collective-permute-start(bf16[384,128]{1,0:T(8,128)(2,1)S(1)} %collective-permute-done.10.refs_2_), channel_id=1, source_target_pairs={{2,0},{3,1},{4,6},{5,7},{10,8},{11,9},{12,14},{13,15},{18,16},{19,... | collective-permute-start | bytes 294920 | tf_op jit(solution)/shard_map/ppermute | solution.py:328
  41.2 0.7 collective-permute-start.15
  42.0 1.7 %copy-done = bf16[768,1536]{1,0:T(8,128)(2,1)S(1)} copy-done((bf16[768,1536]{1,0:T(8,128)(2,1)S(1)}, bf16[768,1536]{1,0:T(8,128)(2,1)}, u32[]{:S(2)}) %copy-start) | copy-done | bytes 2359320
  43.6 3.2 %chunk_across.1 = (s16[784,128]{1,0:T(8,128)(2,1)S(1)}, s16[784,128]{1,0:T(8,128)(2,1)S(1)}, bf16[768,256]{1,0:T(8,128)(2,1)S(1)}) custom-call(bf16[192,256]{1,0:T(8,128)(2,1)S(1)} %get-tuple-element.21.refs_0_, bf16[192,256]{1,0:T(8,128)(2,1)S(1)} %collective-permute-done.18.refs_1_, bf16[192,256]{1,0:T(8,128)(2,1)S(1)} %collective-permute-done.19.refs_2_, ...), custom_call_target="tpu_custom_call" | custom-call | flops 603979776 | bytes 2359296 | tf_op jit(solution)/shard_map/chunk_across/pallas_call | solution.py:396
  46.8 1.3 %collective-permute-start.39 = (s16[784,128]{1,0:T(8,128)(2,1)S(1)}, s16[784,128]{1,0:T(8,128)(2,1)S(1)}, u32[]{:S(2)}, u32[]{:S(2)}) collective-permute-start(s16[784,128]{1,0:T(8,128)(2,1)S(1)} %get-tuple-element.26), channel_id=1, source_target_pairs={{0,16},{1,17},{2,18},{3,19},{4,20},{5,21},{6,22},{7,23},{8,24},{9,... | collective-permute-start | bytes 602120 | tf_op jit(solution)/shard_map/ppermute | solution.py:328
  48.1 0.7 collective-permute-start.16
  48.8 0.3 collective-permute-start.27
  49.1 1.3 %collective-permute-start.3 = (bf16[192,256]{1,0:T(8,128)(2,1)S(1)}, bf16[192,256]{1,0:T(8,128)(2,1)S(1)}, u32[]{:S(2)}, u32[]{:S(2)}) collective-permute-start(bf16[192,256]{1,0:T(8,128)(2,1)S(1)} %collective-permute-done.1.refs_2_), channel_id=1, source_target_pairs={{2,0},{3,1},{4,6},{5,7},{10,8},{11,9},{12,14},{13,15},{18,16},{19,... | collective-permute-start | bytes 294920 | tf_op jit(solution)/shard_map/ppermute | solution.py:328
  50.4 2.9 %collective-permute-start.38 = (bf16[384,128]{1,0:T(8,128)(2,1)S(1)}, bf16[384,128]{1,0:T(8,128)(2,1)S(1)}, u32[]{:S(2)}, u32[]{:S(2)}) collective-permute-start(bf16[384,128]{1,0:T(8,128)(2,1)S(1)} %collective-permute-done.33.refs_4_), channel_id=1, source_target_pairs={{0,1},{1,0},{6,7},{7,6},{8,9},{9,8},{14,15},{15,14},{16,17},{17,16... | collective-permute-start | bytes 294920 | tf_op jit(solution)/shard_map/ppermute | solution.py:328
  53.4 0.7 collective-permute-start.42
  54.0 3.6 %collective-permute-done.3.refs_4_ = bf16[192,256]{1,0:T(8,128)(2,1)S(1)} collective-permute-done((bf16[192,256]{1,0:T(8,128)(2,1)S(1)}, bf16[192,256]{1,0:T(8,128)(2,1)S(1)}, u32[]{:S(2)}, u32[]{:S(2)}) %collective-permute-start.3) | collective-permute-done | bytes 98336 | tf_op jit(solution)/shard_map/ppermute | solution.py:328
  57.7 0.8 collective-permute-start.6
  58.5 1.9 %collective-permute-start.17 = (bf16[384,128]{1,0:T(8,128)(2,1)S(1)}, bf16[384,128]{1,0:T(8,128)(2,1)S(1)}, u32[]{:S(2)}, u32[]{:S(2)}) collective-permute-start(bf16[384,128]{1,0:T(8,128)(2,1)S(1)} %collective-permute-done.12.refs_4_), channel_id=1, source_target_pairs={{0,1},{1,0},{6,7},{7,6},{8,9},{9,8},{14,15},{15,14},{16,17},{17,16... | collective-permute-start | bytes 294920 | tf_op jit(solution)/shard_map/ppermute | solution.py:328
  60.4 0.6 collective-permute-start.5
  61.0 2.3 %chunk_second.1 = (s16[784,128]{1,0:T(8,128)(2,1)S(1)}, s16[784,128]{1,0:T(8,128)(2,1)S(1)}, bf16[768,128]{1,0:T(8,128)(2,1)S(1)}, bf16[768,128]{1,0:T(8,128)(2,1)S(1)}) custom-call(bf16[384,128]{1,0:T(8,128)(2,1)S(1)} %get-tuple-element.25.refs_0_, bf16[384,128]{1,0:T(8,128)(2,1)S(1)} %collective-permute-done.30.refs_1_, ...), custom_call_target="tpu_custom_call" | custom-call | flops 603979776 | bytes 2359296 | tf_op jit(solution)/shard_map/chunk_second/pallas_call | solution.py:396
  63.3 0.7 collective-permute-start.7
  64.0 1.3 %collective-permute-start.45 = (bf16[768,128]{1,0:T(8,128)(2,1)S(1)}, bf16[768,128]{1,0:T(8,128)(2,1)S(1)}, u32[]{:S(2)}, u32[]{:S(2)}) collective-permute-start(bf16[768,128]{1,0:T(8,128)(2,1)S(1)} %get-tuple-element.32), channel_id=1, source_target_pairs={{0,8},{1,9},{10,2},{11,3},{20,28},{21,29},{30,22},{31,23}} | collective-permute-start | bytes 589832 | tf_op jit(solution)/shard_map/ppermute | solution.py:328
  65.3 0.7 collective-permute-start.46
  66.0 2.3 %chunk_first.1 = (s16[784,128]{1,0:T(8,128)(2,1)S(1)}, s16[784,128]{1,0:T(8,128)(2,1)S(1)}, bf16[768,128]{1,0:T(8,128)(2,1)S(1)}, bf16[768,128]{1,0:T(8,128)(2,1)S(1)}) custom-call(bf16[384,128]{1,0:T(8,128)(2,1)S(1)} %get-tuple-element.20.refs_0_, bf16[384,128]{1,0:T(8,128)(2,1)S(1)} %collective-permute-done.9.refs_1_, ...), custom_call_target="tpu_custom_call" | custom-call | flops 603979776 | bytes 2359296 | tf_op jit(solution)/shard_map/chunk_first/pallas_call | solution.py:396
  68.3 1.3 %collective-permute-start.43 = (bf16[768,128]{1,0:T(8,128)(2,1)S(1)}, bf16[768,128]{1,0:T(8,128)(2,1)S(1)}, u32[]{:S(2)}, u32[]{:S(2)}) collective-permute-start(bf16[768,128]{1,0:T(8,128)(2,1)S(1)} %get-tuple-element.30), channel_id=1, source_target_pairs={{0,8},{1,9},{10,2},{11,3},{20,28},{21,29},{30,22},{31,23}} | collective-permute-start | bytes 589832 | tf_op jit(solution)/shard_map/ppermute | solution.py:328
  69.6 1.9 %collective-permute-start.8 = (bf16[192,256]{1,0:T(8,128)(2,1)S(1)}, bf16[192,256]{1,0:T(8,128)(2,1)S(1)}, u32[]{:S(2)}, u32[]{:S(2)}) collective-permute-start(bf16[192,256]{1,0:T(8,128)(2,1)S(1)} %collective-permute-done.3.refs_4_), channel_id=1, source_target_pairs={{0,1},{1,0},{6,7},{7,6},{8,9},{9,8},{14,15},{15,14},{16,17},{17,16... | collective-permute-start | bytes 294920 | tf_op jit(solution)/shard_map/ppermute | solution.py:328
  71.5 1.2 %collective-permute-done.8.refs_9_ = bf16[192,256]{1,0:T(8,128)(2,1)S(1)} collective-permute-done((bf16[192,256]{1,0:T(8,128)(2,1)S(1)}, bf16[192,256]{1,0:T(8,128)(2,1)S(1)}, u32[]{:S(2)}, u32[]{:S(2)}) %collective-permute-start.8) | collective-permute-done | bytes 98336 | tf_op jit(solution)/shard_map/ppermute | solution.py:328
  72.8 2.7 %collective-permute-start.40 = (s16[784,128]{1,0:T(8,128)(2,1)S(1)}, s16[784,128]{1,0:T(8,128)(2,1)S(1)}, u32[]{:S(2)}, u32[]{:S(2)}) collective-permute-start(s16[784,128]{1,0:T(8,128)(2,1)S(1)} %get-tuple-element.27), channel_id=1, source_target_pairs={{0,8},{1,9},{2,10},{3,11},{4,12},{5,13},{6,14},{7,15},{8,0},{9,1},... | collective-permute-start | bytes 602120 | tf_op jit(solution)/shard_map/ppermute | solution.py:328
  75.6 1.4 %collective-permute-start.29 = (s16[784,128]{1,0:T(8,128)(2,1)S(1)}, s16[784,128]{1,0:T(8,128)(2,1)S(1)}, u32[]{:S(2)}, u32[]{:S(2)}) collective-permute-start(s16[784,128]{1,0:T(8,128)(2,1)S(1)} %get-tuple-element.24), channel_id=1, source_target_pairs={{0,16},{1,17},{2,18},{3,19},{4,20},{5,21},{6,22},{7,23},{8,24},{9,... | collective-permute-start | bytes 602120 | tf_op jit(solution)/shard_map/ppermute | solution.py:328
  77.3 0.8 collective-permute-start.44
  78.1 3.5 %collective-permute-done.40.refs_14_ = s16[784,128]{1,0:T(8,128)(2,1)S(1)} collective-permute-done((s16[784,128]{1,0:T(8,128)(2,1)S(1)}, s16[784,128]{1,0:T(8,128)(2,1)S(1)}, u32[]{:S(2)}, u32[]{:S(2)}) %collective-permute-start.40) | collective-permute-done | bytes 200736 | tf_op jit(solution)/shard_map/ppermute | solution.py:328
  81.6 4.3 %collective-permute-done.28.refs_12_ = s16[784,128]{1,0:T(8,128)(2,1)S(1)} collective-permute-done((s16[784,128]{1,0:T(8,128)(2,1)S(1)}, s16[784,128]{1,0:T(8,128)(2,1)S(1)}, u32[]{:S(2)}, u32[]{:S(2)}) %collective-permute-start.28) | collective-permute-done | bytes 200736 | tf_op jit(solution)/shard_map/ppermute | solution.py:328
  85.9 5.0 %chunk_own.1 = (bf16[768,256]{1,0:T(8,128)(2,1)}, f32[256,256]{1,0:T(8,128)S(1)}) custom-call(bf16[192,256]{1,0:T(8,128)(2,1)S(1)} %get-tuple-element.19.refs_0_, bf16[192,256]{1,0:T(8,128)(2,1)S(1)} %collective-permute-done.refs_1_, bf16[192,256]{1,0:T(8,128)(2,1)S(1)} %collective-permute-done.1.refs_2_, ...), custom_call_target="tpu_custom_call" | custom-call | flops 603979776 | bytes 2359296 | tf_op jit(solution)/shard_map/chunk_own/pallas_call | solution.py:423
  90.9 1.4 %collective-permute-start.47 = (f32[32,256]{1,0:T(8,128)S(1)}, f32[32,256]{1,0:T(8,128)S(1)}, u32[]{:S(2)}, u32[]{:S(2)}) collective-permute-start(f32[32,256]{1,0:T(8,128)S(1)} %get-tuple-element.36), channel_id=1, source_target_pairs={{0,1},{1,0},{2,3},{3,2},{4,5},{5,4},{6,7},{7,6},{8,9},{9,8},{10,11... | collective-permute-start | bytes 98312 | tf_op jit(solution)/shard_map/ppermute | solution.py:328
  92.3 1.7 %collective-permute-start.49 = (f32[32,256]{1,0:T(8,128)S(1)}, f32[32,256]{1,0:T(8,128)S(1)}, u32[]{:S(2)}, u32[]{:S(2)}) collective-permute-start(f32[32,256]{1,0:T(8,128)S(1)} %get-tuple-element.41), channel_id=1, source_target_pairs={{0,3},{1,2},{2,1},{3,0},{4,7},{5,6},{6,5},{7,4},{8,11},{9,10},{10,... | collective-permute-start | bytes 98312 | tf_op jit(solution)/shard_map/ppermute | solution.py:328
  94.0 3.9 %collective-permute-start.50 = (f32[32,256]{1,0:T(8,128)S(1)}, f32[32,256]{1,0:T(8,128)S(1)}, u32[]{:S(2)}, u32[]{:S(2)}) collective-permute-start(f32[32,256]{1,0:T(8,128)S(1)} %get-tuple-element.40), channel_id=1, source_target_pairs={{0,4},{1,5},{2,6},{3,7},{4,0},{5,1},{6,2},{7,3},{8,12},{9,13},{10,... | collective-permute-start | bytes 98312 | tf_op jit(solution)/shard_map/ppermute | solution.py:328
  97.9 0.3 collective-permute-start.51
  98.2 3.8 %collective-permute-start.52 = (f32[32,256]{1,0:T(8,128)S(1)}, f32[32,256]{1,0:T(8,128)S(1)}, u32[]{:S(2)}, u32[]{:S(2)}) collective-permute-start(f32[32,256]{1,0:T(8,128)S(1)} %get-tuple-element.38), channel_id=1, source_target_pairs={{0,6},{1,7},{2,4},{3,5},{4,2},{5,3},{6,0},{7,1},{8,14},{9,15},{10,... | collective-permute-start | bytes 98312 | tf_op jit(solution)/shard_map/ppermute | solution.py:328
  102.0 0.7 collective-permute-done.51
  102.7 1.7 %collective-permute-done.52 = f32[32,256]{1,0:T(8,128)S(1)} collective-permute-done((f32[32,256]{1,0:T(8,128)S(1)}, f32[32,256]{1,0:T(8,128)S(1)}, u32[]{:S(2)}, u32[]{:S(2)}) %collective-permute-start.52) | collective-permute-done | bytes 32800 | tf_op jit(solution)/shard_map/ppermute | solution.py:328
  104.4 2.7 %collective-permute-done.53 = f32[32,256]{1,0:T(8,128)S(1)} collective-permute-done((f32[32,256]{1,0:T(8,128)S(1)}, f32[32,256]{1,0:T(8,128)S(1)}, u32[]{:S(2)}, u32[]{:S(2)}) %collective-permute-start.53) | collective-permute-done | bytes 32800 | tf_op jit(solution)/shard_map/ppermute | solution.py:328
  107.1 0.6 add_subtract_fusion
  (63 shorter events, 0.7 us)
Async XLA Ops:
  0.6 1.0 copy-start.2
  1.6 0.7 copy-start.3
  3.0 8.5 %collective-permute-start.19 = (bf16[192,256]{1,0:T(8,128)(2,1)S(1)}, bf16[192,256]{1,0:T(8,128)(2,1)S(1)}, u32[]{:S(2)}, u32[]{:S(2)}) collective-permute-start(bf16[192,256]{1,0:T(8,128)(2,1)S(1)} %get-tuple-element.21.refs_0_), channel_id=1, source_target_pairs={{0,4},{1,5},{2,6},{3,7},{4,0},{5,1},{6,2},{7,3},{8,12},{9,13},{10,... | collective-permute-start | bytes 294920 | tf_op jit(solution)/shard_map/ppermute | solution.py:328
  5.4 6.2 %collective-permute-start.18 = (bf16[192,256]{1,0:T(8,128)(2,1)S(1)}, bf16[192,256]{1,0:T(8,128)(2,1)S(1)}, u32[]{:S(2)}, u32[]{:S(2)}) collective-permute-start(bf16[192,256]{1,0:T(8,128)(2,1)S(1)} %get-tuple-element.21.refs_0_), channel_id=1, source_target_pairs={{0,2},{1,3},{2,0},{3,1},{4,6},{5,7},{6,4},{7,5},{8,10},{9,11},{10,... | collective-permute-start | bytes 294920 | tf_op jit(solution)/shard_map/ppermute | solution.py:328
  6.7 5.5 %collective-permute-start.20 = (bf16[192,256]{1,0:T(8,128)(2,1)S(1)}, bf16[192,256]{1,0:T(8,128)(2,1)S(1)}, u32[]{:S(2)}, u32[]{:S(2)}) collective-permute-start(bf16[192,256]{1,0:T(8,128)(2,1)S(1)} %get-tuple-element.21.refs_0_), channel_id=1, source_target_pairs={{2,4},{3,5},{4,2},{5,3},{10,12},{11,13},{12,10},{13,11},{18,20},{1... | collective-permute-start | bytes 294920 | tf_op jit(solution)/shard_map/ppermute | solution.py:328
  7.4 5.5 %collective-permute-start.22 = (bf16[192,256]{1,0:T(8,128)(2,1)S(1)}, bf16[192,256]{1,0:T(8,128)(2,1)S(1)}, u32[]{:S(2)}, u32[]{:S(2)}) collective-permute-start(bf16[192,256]{1,0:T(8,128)(2,1)S(1)} %get-tuple-element.21.refs_0_), channel_id=1, source_target_pairs={{0,1},{1,0},{2,3},{3,2},{4,5},{5,4},{6,7},{7,6},{8,9},{9,8},{10,11... | collective-permute-start | bytes 294920 | tf_op jit(solution)/shard_map/ppermute | solution.py:328
  8.7 9.0 %collective-permute-start.31 = (bf16[384,128]{1,0:T(8,128)(2,1)S(1)}, bf16[384,128]{1,0:T(8,128)(2,1)S(1)}, u32[]{:S(2)}, u32[]{:S(2)}) collective-permute-start(bf16[384,128]{1,0:T(8,128)(2,1)S(1)} %get-tuple-element.25.refs_0_), channel_id=1, source_target_pairs={{0,4},{1,5},{2,6},{3,7},{4,0},{5,1},{6,2},{7,3},{8,12},{9,13},{10,... | collective-permute-start | bytes 294920 | tf_op jit(solution)/shard_map/ppermute | solution.py:328
  11.6 6.2 %collective-permute-start.30 = (bf16[384,128]{1,0:T(8,128)(2,1)S(1)}, bf16[384,128]{1,0:T(8,128)(2,1)S(1)}, u32[]{:S(2)}, u32[]{:S(2)}) collective-permute-start(bf16[384,128]{1,0:T(8,128)(2,1)S(1)} %get-tuple-element.25.refs_0_), channel_id=1, source_target_pairs={{0,2},{1,3},{2,0},{3,1},{4,6},{5,7},{6,4},{7,5},{8,10},{9,11},{10,... | collective-permute-start | bytes 294920 | tf_op jit(solution)/shard_map/ppermute | solution.py:328
  11.6 6.9 %collective-permute-start.32 = (bf16[384,128]{1,0:T(8,128)(2,1)S(1)}, bf16[384,128]{1,0:T(8,128)(2,1)S(1)}, u32[]{:S(2)}, u32[]{:S(2)}) collective-permute-start(bf16[384,128]{1,0:T(8,128)(2,1)S(1)} %get-tuple-element.25.refs_0_), channel_id=1, source_target_pairs={{2,4},{3,5},{4,2},{5,3},{10,12},{11,13},{12,10},{13,11},{18,20},{1... | collective-permute-start | bytes 294920 | tf_op jit(solution)/shard_map/ppermute | solution.py:328
  12.3 7.5 %collective-permute-start.34 = (bf16[384,128]{1,0:T(8,128)(2,1)S(1)}, bf16[384,128]{1,0:T(8,128)(2,1)S(1)}, u32[]{:S(2)}, u32[]{:S(2)}) collective-permute-start(bf16[384,128]{1,0:T(8,128)(2,1)S(1)} %get-tuple-element.25.refs_0_), channel_id=1, source_target_pairs={{0,1},{1,0},{2,3},{3,2},{4,5},{5,4},{6,7},{7,6},{8,9},{9,8},{10,11... | collective-permute-start | bytes 294920 | tf_op jit(solution)/shard_map/ppermute | solution.py:328
  12.8 12.1 %collective-permute-start.10 = (bf16[384,128]{1,0:T(8,128)(2,1)S(1)}, bf16[384,128]{1,0:T(8,128)(2,1)S(1)}, u32[]{:S(2)}, u32[]{:S(2)}) collective-permute-start(bf16[384,128]{1,0:T(8,128)(2,1)S(1)} %get-tuple-element.20.refs_0_), channel_id=1, source_target_pairs={{0,4},{1,5},{2,6},{3,7},{4,0},{5,1},{6,2},{7,3},{8,12},{9,13},{10,... | collective-permute-start | bytes 294920 | tf_op jit(solution)/shard_map/ppermute | solution.py:328
  17.7 7.2 %collective-permute-start.9 = (bf16[384,128]{1,0:T(8,128)(2,1)S(1)}, bf16[384,128]{1,0:T(8,128)(2,1)S(1)}, u32[]{:S(2)}, u32[]{:S(2)}) collective-permute-start(bf16[384,128]{1,0:T(8,128)(2,1)S(1)} %get-tuple-element.20.refs_0_), channel_id=1, source_target_pairs={{0,2},{1,3},{2,0},{3,1},{4,6},{5,7},{6,4},{7,5},{8,10},{9,11},{10,... | collective-permute-start | bytes 294920 | tf_op jit(solution)/shard_map/ppermute | solution.py:328
  17.8 7.8 %collective-permute-start.11 = (bf16[384,128]{1,0:T(8,128)(2,1)S(1)}, bf16[384,128]{1,0:T(8,128)(2,1)S(1)}, u32[]{:S(2)}, u32[]{:S(2)}) collective-permute-start(bf16[384,128]{1,0:T(8,128)(2,1)S(1)} %get-tuple-element.20.refs_0_), channel_id=1, source_target_pairs={{2,4},{3,5},{4,2},{5,3},{10,12},{11,13},{12,10},{13,11},{18,20},{1... | collective-permute-start | bytes 294920 | tf_op jit(solution)/shard_map/ppermute | solution.py:328
  18.5 7.6 %collective-permute-start.13 = (bf16[384,128]{1,0:T(8,128)(2,1)S(1)}, bf16[384,128]{1,0:T(8,128)(2,1)S(1)}, u32[]{:S(2)}, u32[]{:S(2)}) collective-permute-start(bf16[384,128]{1,0:T(8,128)(2,1)S(1)} %get-tuple-element.20.refs_0_), channel_id=1, source_target_pairs={{0,1},{1,0},{2,3},{3,2},{4,5},{5,4},{6,7},{7,6},{8,9},{9,8},{10,11... | collective-permute-start | bytes 294920 | tf_op jit(solution)/shard_map/ppermute | solution.py:328
  19.7 10.6 %collective-permute-start.1 = (bf16[192,256]{1,0:T(8,128)(2,1)S(1)}, bf16[192,256]{1,0:T(8,128)(2,1)S(1)}, u32[]{:S(2)}, u32[]{:S(2)}) collective-permute-start(bf16[192,256]{1,0:T(8,128)(2,1)S(1)} %get-tuple-element.19.refs_0_), channel_id=1, source_target_pairs={{0,4},{1,5},{2,6},{3,7},{4,0},{5,1},{6,2},{7,3},{8,12},{9,13},{10,... | collective-permute-start | bytes 294920 | tf_op jit(solution)/shard_map/ppermute | solution.py:328
  24.9 6.3 %collective-permute-start = (bf16[192,256]{1,0:T(8,128)(2,1)S(1)}, bf16[192,256]{1,0:T(8,128)(2,1)S(1)}, u32[]{:S(2)}, u32[]{:S(2)}) collective-permute-start(bf16[192,256]{1,0:T(8,128)(2,1)S(1)} %get-tuple-element.19.refs_0_), channel_id=1, source_target_pairs={{0,2},{1,3},{2,0},{3,1},{4,6},{5,7},{6,4},{7,5},{8,10},{9,11},{10,... | collective-permute-start | bytes 294920 | tf_op jit(solution)/shard_map/ppermute | solution.py:328
  24.9 6.3 %collective-permute-start.2 = (bf16[192,256]{1,0:T(8,128)(2,1)S(1)}, bf16[192,256]{1,0:T(8,128)(2,1)S(1)}, u32[]{:S(2)}, u32[]{:S(2)}) collective-permute-start(bf16[192,256]{1,0:T(8,128)(2,1)S(1)} %get-tuple-element.19.refs_0_), channel_id=1, source_target_pairs={{2,4},{3,5},{4,2},{5,3},{10,12},{11,13},{12,10},{13,11},{18,20},{1... | collective-permute-start | bytes 294920 | tf_op jit(solution)/shard_map/ppermute | solution.py:328
  25.6 6.3 %collective-permute-start.4 = (bf16[192,256]{1,0:T(8,128)(2,1)S(1)}, bf16[192,256]{1,0:T(8,128)(2,1)S(1)}, u32[]{:S(2)}, u32[]{:S(2)}) collective-permute-start(bf16[192,256]{1,0:T(8,128)(2,1)S(1)} %get-tuple-element.19.refs_0_), channel_id=1, source_target_pairs={{0,1},{1,0},{2,3},{3,2},{4,5},{5,4},{6,7},{7,6},{8,9},{9,8},{10,11... | collective-permute-start | bytes 294920 | tf_op jit(solution)/shard_map/ppermute | solution.py:328
  26.1 9.2 %collective-permute-start.21 = (bf16[192,256]{1,0:T(8,128)(2,1)S(1)}, bf16[192,256]{1,0:T(8,128)(2,1)S(1)}, u32[]{:S(2)}, u32[]{:S(2)}) collective-permute-start(bf16[192,256]{1,0:T(8,128)(2,1)S(1)} %collective-permute-done.19.refs_2_), channel_id=1, source_target_pairs={{2,0},{3,1},{4,6},{5,7},{10,8},{11,9},{12,14},{13,15},{18,16},{19,... | collective-permute-start | bytes 294920 | tf_op jit(solution)/shard_map/ppermute | solution.py:328
  30.3 5.6 %collective-permute-start.24 = (bf16[192,256]{1,0:T(8,128)(2,1)S(1)}, bf16[192,256]{1,0:T(8,128)(2,1)S(1)}, u32[]{:S(2)}, u32[]{:S(2)}) collective-permute-start(bf16[192,256]{1,0:T(8,128)(2,1)S(1)} %collective-permute-done.19.refs_2_), channel_id=1, source_target_pairs={{0,1},{1,0},{2,3},{3,2},{4,5},{5,4},{6,7},{7,6},{8,9},{9,8},{10,11... | collective-permute-start | bytes 294920 | tf_op jit(solution)/shard_map/ppermute | solution.py:328
  31.3 6.6 %collective-permute-start.23 = (bf16[192,256]{1,0:T(8,128)(2,1)S(1)}, bf16[192,256]{1,0:T(8,128)(2,1)S(1)}, u32[]{:S(2)}, u32[]{:S(2)}) collective-permute-start(bf16[192,256]{1,0:T(8,128)(2,1)S(1)} %collective-permute-done.18.refs_1_), channel_id=1, source_target_pairs={{0,1},{1,0},{2,3},{3,2},{4,5},{5,4},{6,7},{7,6},{8,9},{9,8},{10,11... | collective-permute-start | bytes 294920 | tf_op jit(solution)/shard_map/ppermute | solution.py:328
  31.3 7.2 %collective-permute-start.25 = (bf16[192,256]{1,0:T(8,128)(2,1)S(1)}, bf16[192,256]{1,0:T(8,128)(2,1)S(1)}, u32[]{:S(2)}, u32[]{:S(2)}) collective-permute-start(bf16[192,256]{1,0:T(8,128)(2,1)S(1)} %collective-permute-done.20.refs_3_), channel_id=1, source_target_pairs={{2,3},{3,2},{4,5},{5,4},{10,11},{11,10},{12,13},{13,12},{18,19},{1... | collective-permute-start | bytes 294920 | tf_op jit(solution)/shard_map/ppermute | solution.py:328
  32.0 8.0 %collective-permute-start.33 = (bf16[384,128]{1,0:T(8,128)(2,1)S(1)}, bf16[384,128]{1,0:T(8,128)(2,1)S(1)}, u32[]{:S(2)}, u32[]{:S(2)}) collective-permute-start(bf16[384,128]{1,0:T(8,128)(2,1)S(1)} %collective-permute-done.31.refs_2_), channel_id=1, source_target_pairs={{2,0},{3,1},{4,6},{5,7},{10,8},{11,9},{12,14},{13,15},{18,16},{19,... | collective-permute-start | bytes 294920 | tf_op jit(solution)/shard_map/ppermute | solution.py:328
  35.3 5.9 %collective-permute-start.36 = (bf16[384,128]{1,0:T(8,128)(2,1)S(1)}, bf16[384,128]{1,0:T(8,128)(2,1)S(1)}, u32[]{:S(2)}, u32[]{:S(2)}) collective-permute-start(bf16[384,128]{1,0:T(8,128)(2,1)S(1)} %collective-permute-done.31.refs_2_), channel_id=1, source_target_pairs={{0,1},{1,0},{2,3},{3,2},{4,5},{5,4},{6,7},{7,6},{8,9},{9,8},{10,11... | collective-permute-start | bytes 294920 | tf_op jit(solution)/shard_map/ppermute | solution.py:328
  35.9 5.9 %collective-permute-start.26 = (bf16[192,256]{1,0:T(8,128)(2,1)S(1)}, bf16[192,256]{1,0:T(8,128)(2,1)S(1)}, u32[]{:S(2)}, u32[]{:S(2)}) collective-permute-start(bf16[192,256]{1,0:T(8,128)(2,1)S(1)} %collective-permute-done.21.refs_4_), channel_id=1, source_target_pairs={{0,1},{1,0},{6,7},{7,6},{8,9},{9,8},{14,15},{15,14},{16,17},{17,16... | collective-permute-start | bytes 294920 | tf_op jit(solution)/shard_map/ppermute | solution.py:328
  37.9 9.0 %collective-permute-start.35 = (bf16[384,128]{1,0:T(8,128)(2,1)S(1)}, bf16[384,128]{1,0:T(8,128)(2,1)S(1)}, u32[]{:S(2)}, u32[]{:S(2)}) collective-permute-start(bf16[384,128]{1,0:T(8,128)(2,1)S(1)} %collective-permute-done.30.refs_1_), channel_id=1, source_target_pairs={{0,1},{1,0},{2,3},{3,2},{4,5},{5,4},{6,7},{7,6},{8,9},{9,8},{10,11... | collective-permute-start | bytes 294920 | tf_op jit(solution)/shard_map/ppermute | solution.py:328
  38.4 9.7 %collective-permute-start.37 = (bf16[384,128]{1,0:T(8,128)(2,1)S(1)}, bf16[384,128]{1,0:T(8,128)(2,1)S(1)}, u32[]{:S(2)}, u32[]{:S(2)}) collective-permute-start(bf16[384,128]{1,0:T(8,128)(2,1)S(1)} %collective-permute-done.32.refs_3_), channel_id=1, source_target_pairs={{2,3},{3,2},{4,5},{5,4},{10,11},{11,10},{12,13},{13,12},{18,19},{1... | collective-permute-start | bytes 294920 | tf_op jit(solution)/shard_map/ppermute | solution.py:328
  39.9 8.9 %collective-permute-start.12 = (bf16[384,128]{1,0:T(8,128)(2,1)S(1)}, bf16[384,128]{1,0:T(8,128)(2,1)S(1)}, u32[]{:S(2)}, u32[]{:S(2)}) collective-permute-start(bf16[384,128]{1,0:T(8,128)(2,1)S(1)} %collective-permute-done.10.refs_2_), channel_id=1, source_target_pairs={{2,0},{3,1},{4,6},{5,7},{10,8},{11,9},{12,14},{13,15},{18,16},{19,... | collective-permute-start | bytes 294920 | tf_op jit(solution)/shard_map/ppermute | solution.py:328
  41.2 7.9 %collective-permute-start.15 = (bf16[384,128]{1,0:T(8,128)(2,1)S(1)}, bf16[384,128]{1,0:T(8,128)(2,1)S(1)}, u32[]{:S(2)}, u32[]{:S(2)}) collective-permute-start(bf16[384,128]{1,0:T(8,128)(2,1)S(1)} %collective-permute-done.10.refs_2_), channel_id=1, source_target_pairs={{0,1},{1,0},{2,3},{3,2},{4,5},{5,4},{6,7},{7,6},{8,9},{9,8},{10,11... | collective-permute-start | bytes 294920 | tf_op jit(solution)/shard_map/ppermute | solution.py:328
  41.9 8.6 %collective-permute-start.14 = (bf16[384,128]{1,0:T(8,128)(2,1)S(1)}, bf16[384,128]{1,0:T(8,128)(2,1)S(1)}, u32[]{:S(2)}, u32[]{:S(2)}) collective-permute-start(bf16[384,128]{1,0:T(8,128)(2,1)S(1)} %collective-permute-done.9.refs_1_), channel_id=1, source_target_pairs={{0,1},{1,0},{2,3},{3,2},{4,5},{5,4},{6,7},{7,6},{8,9},{9,8},{10,11... | collective-permute-start | bytes 294920 | tf_op jit(solution)/shard_map/ppermute | solution.py:328
  42.0 1.7 %copy-start = (bf16[768,1536]{1,0:T(8,128)(2,1)S(1)}, bf16[768,1536]{1,0:T(8,128)(2,1)}, u32[]{:S(2)}) copy-start(bf16[768,1536]{1,0:T(8,128)(2,1)} %refs_10_.7) | copy-start | bytes 7077892
  43.6 17.3 %copy-start.1 = (bf16[768,1536]{1,0:T(8,128)(2,1)S(1)}, bf16[768,1536]{1,0:T(8,128)(2,1)}, u32[]{:S(2)}) copy-start(bf16[768,1536]{1,0:T(8,128)(2,1)} %refs_10_.7) | copy-start | bytes 7077892
  46.8 13.6 %collective-permute-start.39 = (s16[784,128]{1,0:T(8,128)(2,1)S(1)}, s16[784,128]{1,0:T(8,128)(2,1)S(1)}, u32[]{:S(2)}, u32[]{:S(2)}) collective-permute-start(s16[784,128]{1,0:T(8,128)(2,1)S(1)} %get-tuple-element.26), channel_id=1, source_target_pairs={{0,16},{1,17},{2,18},{3,19},{4,20},{5,21},{6,22},{7,23},{8,24},{9,... | collective-permute-start | bytes 602120 | tf_op jit(solution)/shard_map/ppermute | solution.py:328
  48.1 5.2 %collective-permute-start.16 = (bf16[384,128]{1,0:T(8,128)(2,1)S(1)}, bf16[384,128]{1,0:T(8,128)(2,1)S(1)}, u32[]{:S(2)}, u32[]{:S(2)}) collective-permute-start(bf16[384,128]{1,0:T(8,128)(2,1)S(1)} %collective-permute-done.11.refs_3_), channel_id=1, source_target_pairs={{2,3},{3,2},{4,5},{5,4},{10,11},{11,10},{12,13},{13,12},{18,19},{1... | collective-permute-start | bytes 294920 | tf_op jit(solution)/shard_map/ppermute | solution.py:328
  48.8 16.5 %collective-permute-start.27 = (s16[784,128]{1,0:T(8,128)(2,1)S(1)}, s16[784,128]{1,0:T(8,128)(2,1)S(1)}, u32[]{:S(2)}, u32[]{:S(2)}) collective-permute-start(s16[784,128]{1,0:T(8,128)(2,1)S(1)} %get-tuple-element.22), channel_id=1, source_target_pairs={{0,8},{1,9},{2,10},{3,11},{4,12},{5,13},{6,14},{7,15},{8,0},{9,1},... | collective-permute-start | bytes 602120 | tf_op jit(solution)/shard_map/ppermute | solution.py:328
  49.1 8.5 %collective-permute-start.3 = (bf16[192,256]{1,0:T(8,128)(2,1)S(1)}, bf16[192,256]{1,0:T(8,128)(2,1)S(1)}, u32[]{:S(2)}, u32[]{:S(2)}) collective-permute-start(bf16[192,256]{1,0:T(8,128)(2,1)S(1)} %collective-permute-done.1.refs_2_), channel_id=1, source_target_pairs={{2,0},{3,1},{4,6},{5,7},{10,8},{11,9},{12,14},{13,15},{18,16},{19,... | collective-permute-start | bytes 294920 | tf_op jit(solution)/shard_map/ppermute | solution.py:328
  50.4 8.0 %collective-permute-start.38 = (bf16[384,128]{1,0:T(8,128)(2,1)S(1)}, bf16[384,128]{1,0:T(8,128)(2,1)S(1)}, u32[]{:S(2)}, u32[]{:S(2)}) collective-permute-start(bf16[384,128]{1,0:T(8,128)(2,1)S(1)} %collective-permute-done.33.refs_4_), channel_id=1, source_target_pairs={{0,1},{1,0},{6,7},{7,6},{8,9},{9,8},{14,15},{15,14},{16,17},{17,16... | collective-permute-start | bytes 294920 | tf_op jit(solution)/shard_map/ppermute | solution.py:328
  53.4 22.2 %collective-permute-start.42 = (bf16[768,256]{1,0:T(8,128)(2,1)S(1)}, bf16[768,256]{1,0:T(8,128)(2,1)S(1)}, u32[]{:S(2)}, u32[]{:S(2)}) collective-permute-start(bf16[768,256]{1,0:T(8,128)(2,1)S(1)} %get-tuple-element.29), channel_id=1, source_target_pairs={{0,24},{1,25},{10,18},{11,19},{20,12},{21,13},{30,6},{31,7}} | collective-permute-start | bytes 1179656 | tf_op jit(solution)/shard_map/ppermute | solution.py:328
  57.7 5.6 %collective-permute-start.6 = (bf16[192,256]{1,0:T(8,128)(2,1)S(1)}, bf16[192,256]{1,0:T(8,128)(2,1)S(1)}, u32[]{:S(2)}, u32[]{:S(2)}) collective-permute-start(bf16[192,256]{1,0:T(8,128)(2,1)S(1)} %collective-permute-done.1.refs_2_), channel_id=1, source_target_pairs={{0,1},{1,0},{2,3},{3,2},{4,5},{5,4},{6,7},{7,6},{8,9},{9,8},{10,11... | collective-permute-start | bytes 294920 | tf_op jit(solution)/shard_map/ppermute | solution.py:328
  58.5 5.5 %collective-permute-start.17 = (bf16[384,128]{1,0:T(8,128)(2,1)S(1)}, bf16[384,128]{1,0:T(8,128)(2,1)S(1)}, u32[]{:S(2)}, u32[]{:S(2)}) collective-permute-start(bf16[384,128]{1,0:T(8,128)(2,1)S(1)} %collective-permute-done.12.refs_4_), channel_id=1, source_target_pairs={{0,1},{1,0},{6,7},{7,6},{8,9},{9,8},{14,15},{15,14},{16,17},{17,16... | collective-permute-start | bytes 294920 | tf_op jit(solution)/shard_map/ppermute | solution.py:328
  60.4 7.9 %collective-permute-start.5 = (bf16[192,256]{1,0:T(8,128)(2,1)S(1)}, bf16[192,256]{1,0:T(8,128)(2,1)S(1)}, u32[]{:S(2)}, u32[]{:S(2)}) collective-permute-start(bf16[192,256]{1,0:T(8,128)(2,1)S(1)} %collective-permute-done.refs_1_), channel_id=1, source_target_pairs={{0,1},{1,0},{2,3},{3,2},{4,5},{5,4},{6,7},{7,6},{8,9},{9,8},{10,11... | collective-permute-start | bytes 294920 | tf_op jit(solution)/shard_map/ppermute | solution.py:328
  63.3 22.7 %copy-start.4 = (s32[4,12]{1,0:T(4,128)S(1)}, s32[4,12]{1,0:T(4,128)}, u32[]{:S(2)}) copy-start(s32[4,12]{1,0:T(4,128)} %refs_11_.1) | copy-start | bytes 580
  63.3 6.3 %collective-permute-start.7 = (bf16[192,256]{1,0:T(8,128)(2,1)S(1)}, bf16[192,256]{1,0:T(8,128)(2,1)S(1)}, u32[]{:S(2)}, u32[]{:S(2)}) collective-permute-start(bf16[192,256]{1,0:T(8,128)(2,1)S(1)} %collective-permute-done.2.refs_3_), channel_id=1, source_target_pairs={{2,3},{3,2},{4,5},{5,4},{10,11},{11,10},{12,13},{13,12},{18,19},{1... | collective-permute-start | bytes 294920 | tf_op jit(solution)/shard_map/ppermute | solution.py:328
  64.0 11.6 %collective-permute-start.45 = (bf16[768,128]{1,0:T(8,128)(2,1)S(1)}, bf16[768,128]{1,0:T(8,128)(2,1)S(1)}, u32[]{:S(2)}, u32[]{:S(2)}) collective-permute-start(bf16[768,128]{1,0:T(8,128)(2,1)S(1)} %get-tuple-element.32), channel_id=1, source_target_pairs={{0,8},{1,9},{10,2},{11,3},{20,28},{21,29},{30,22},{31,23}} | collective-permute-start | bytes 589832 | tf_op jit(solution)/shard_map/ppermute | solution.py:328
  65.3 10.3 %collective-permute-start.46 = (bf16[768,128]{1,0:T(8,128)(2,1)S(1)}, bf16[768,128]{1,0:T(8,128)(2,1)S(1)}, u32[]{:S(2)}, u32[]{:S(2)}) collective-permute-start(bf16[768,128]{1,0:T(8,128)(2,1)S(1)} %get-tuple-element.33), channel_id=1, source_target_pairs={{0,16},{1,17},{10,26},{11,27},{20,4},{21,5},{30,14},{31,15}} | collective-permute-start | bytes 589832 | tf_op jit(solution)/shard_map/ppermute | solution.py:328
  68.3 9.0 %collective-permute-start.43 = (bf16[768,128]{1,0:T(8,128)(2,1)S(1)}, bf16[768,128]{1,0:T(8,128)(2,1)S(1)}, u32[]{:S(2)}, u32[]{:S(2)}) collective-permute-start(bf16[768,128]{1,0:T(8,128)(2,1)S(1)} %get-tuple-element.30), channel_id=1, source_target_pairs={{0,8},{1,9},{10,2},{11,3},{20,28},{21,29},{30,22},{31,23}} | collective-permute-start | bytes 589832 | tf_op jit(solution)/shard_map/ppermute | solution.py:328
  69.6 3.2 %collective-permute-start.8 = (bf16[192,256]{1,0:T(8,128)(2,1)S(1)}, bf16[192,256]{1,0:T(8,128)(2,1)S(1)}, u32[]{:S(2)}, u32[]{:S(2)}) collective-permute-start(bf16[192,256]{1,0:T(8,128)(2,1)S(1)} %collective-permute-done.3.refs_4_), channel_id=1, source_target_pairs={{0,1},{1,0},{6,7},{7,6},{8,9},{9,8},{14,15},{15,14},{16,17},{17,16... | collective-permute-start | bytes 294920 | tf_op jit(solution)/shard_map/ppermute | solution.py:328
  72.8 8.8 %collective-permute-start.40 = (s16[784,128]{1,0:T(8,128)(2,1)S(1)}, s16[784,128]{1,0:T(8,128)(2,1)S(1)}, u32[]{:S(2)}, u32[]{:S(2)}) collective-permute-start(s16[784,128]{1,0:T(8,128)(2,1)S(1)} %get-tuple-element.27), channel_id=1, source_target_pairs={{0,8},{1,9},{2,10},{3,11},{4,12},{5,13},{6,14},{7,15},{8,0},{9,1},... | collective-permute-start | bytes 602120 | tf_op jit(solution)/shard_map/ppermute | solution.py:328
  75.5 6.1 %collective-permute-start.41 = (s16[784,128]{1,0:T(8,128)(2,1)S(1)}, s16[784,128]{1,0:T(8,128)(2,1)S(1)}, u32[]{:S(2)}, u32[]{:S(2)}) collective-permute-start(s16[784,128]{1,0:T(8,128)(2,1)S(1)} %get-tuple-element.28), channel_id=1, source_target_pairs={{0,16},{1,17},{2,18},{3,19},{4,20},{5,21},{6,22},{7,23},{8,24},{9,... | collective-permute-start | bytes 602120 | tf_op jit(solution)/shard_map/ppermute | solution.py:328
  75.5 10.4 %collective-permute-start.28 = (s16[784,128]{1,0:T(8,128)(2,1)S(1)}, s16[784,128]{1,0:T(8,128)(2,1)S(1)}, u32[]{:S(2)}, u32[]{:S(2)}) collective-permute-start(s16[784,128]{1,0:T(8,128)(2,1)S(1)} %get-tuple-element.23), channel_id=1, source_target_pairs={{0,8},{1,9},{2,10},{3,11},{4,12},{5,13},{6,14},{7,15},{8,0},{9,1},... | collective-permute-start | bytes 602120 | tf_op jit(solution)/shard_map/ppermute | solution.py:328
  75.6 10.3 %collective-permute-start.29 = (s16[784,128]{1,0:T(8,128)(2,1)S(1)}, s16[784,128]{1,0:T(8,128)(2,1)S(1)}, u32[]{:S(2)}, u32[]{:S(2)}) collective-permute-start(s16[784,128]{1,0:T(8,128)(2,1)S(1)} %get-tuple-element.24), channel_id=1, source_target_pairs={{0,16},{1,17},{2,18},{3,19},{4,20},{5,21},{6,22},{7,23},{8,24},{9,... | collective-permute-start | bytes 602120 | tf_op jit(solution)/shard_map/ppermute | solution.py:328
  77.3 29.8 %copy-start.5 = (f32[32,256]{1,0:T(8,128)S(1)}, f32[32,256]{1,0:T(8,128)}, u32[]{:S(2)}) copy-start(f32[32,256]{1,0:T(8,128)} %param.6) | copy-start | bytes 98308
  77.3 0.8 collective-permute-start.44
  90.9 7.3 %collective-permute-start.47 = (f32[32,256]{1,0:T(8,128)S(1)}, f32[32,256]{1,0:T(8,128)S(1)}, u32[]{:S(2)}, u32[]{:S(2)}) collective-permute-start(f32[32,256]{1,0:T(8,128)S(1)} %get-tuple-element.36), channel_id=1, source_target_pairs={{0,1},{1,0},{2,3},{3,2},{4,5},{5,4},{6,7},{7,6},{8,9},{9,8},{10,11... | collective-permute-start | bytes 98312 | tf_op jit(solution)/shard_map/ppermute | solution.py:328
  92.3 9.7 %collective-permute-start.48 = (f32[32,256]{1,0:T(8,128)S(1)}, f32[32,256]{1,0:T(8,128)S(1)}, u32[]{:S(2)}, u32[]{:S(2)}) collective-permute-start(f32[32,256]{1,0:T(8,128)S(1)} %get-tuple-element.42), channel_id=1, source_target_pairs={{0,2},{1,3},{2,0},{3,1},{4,6},{5,7},{6,4},{7,5},{8,10},{9,11},{10,... | collective-permute-start | bytes 98312 | tf_op jit(solution)/shard_map/ppermute | solution.py:328
  92.3 9.7 %collective-permute-start.49 = (f32[32,256]{1,0:T(8,128)S(1)}, f32[32,256]{1,0:T(8,128)S(1)}, u32[]{:S(2)}, u32[]{:S(2)}) collective-permute-start(f32[32,256]{1,0:T(8,128)S(1)} %get-tuple-element.41), channel_id=1, source_target_pairs={{0,3},{1,2},{2,1},{3,0},{4,7},{5,6},{6,5},{7,4},{8,11},{9,10},{10,... | collective-permute-start | bytes 98312 | tf_op jit(solution)/shard_map/ppermute | solution.py:328
  94.0 8.0 %collective-permute-start.50 = (f32[32,256]{1,0:T(8,128)S(1)}, f32[32,256]{1,0:T(8,128)S(1)}, u32[]{:S(2)}, u32[]{:S(2)}) collective-permute-start(f32[32,256]{1,0:T(8,128)S(1)} %get-tuple-element.40), channel_id=1, source_target_pairs={{0,4},{1,5},{2,6},{3,7},{4,0},{5,1},{6,2},{7,3},{8,12},{9,13},{10,... | collective-permute-start | bytes 98312 | tf_op jit(solution)/shard_map/ppermute | solution.py:328
  97.9 4.8 %collective-permute-start.51 = (f32[32,256]{1,0:T(8,128)S(1)}, f32[32,256]{1,0:T(8,128)S(1)}, u32[]{:S(2)}, u32[]{:S(2)}) collective-permute-start(f32[32,256]{1,0:T(8,128)S(1)} %get-tuple-element.39), channel_id=1, source_target_pairs={{0,5},{1,4},{2,7},{3,6},{4,1},{5,0},{6,3},{7,2},{8,13},{9,12},{10,... | collective-permute-start | bytes 98312 | tf_op jit(solution)/shard_map/ppermute | solution.py:328
  98.2 6.2 %collective-permute-start.52 = (f32[32,256]{1,0:T(8,128)S(1)}, f32[32,256]{1,0:T(8,128)S(1)}, u32[]{:S(2)}, u32[]{:S(2)}) collective-permute-start(f32[32,256]{1,0:T(8,128)S(1)} %get-tuple-element.38), channel_id=1, source_target_pairs={{0,6},{1,7},{2,4},{3,5},{4,2},{5,3},{6,0},{7,1},{8,14},{9,15},{10,... | collective-permute-start | bytes 98312 | tf_op jit(solution)/shard_map/ppermute | solution.py:328
  102.0 5.1 %collective-permute-start.53 = (f32[32,256]{1,0:T(8,128)S(1)}, f32[32,256]{1,0:T(8,128)S(1)}, u32[]{:S(2)}, u32[]{:S(2)}) collective-permute-start(f32[32,256]{1,0:T(8,128)S(1)} %get-tuple-element.37), channel_id=1, source_target_pairs={{0,7},{1,6},{2,5},{3,4},{4,3},{5,2},{6,1},{7,0},{8,15},{9,14},{10,... | collective-permute-start | bytes 98312 | tf_op jit(solution)/shard_map/ppermute | solution.py:328

commit v2 on v0

--- a/solution.py
+++ b/solution.py
@@ -1,10 +1,17 @@
+import functools
+
 import jax
 import jax.numpy as jnp
 from jax import lax
+from jax.experimental import pallas as pl
+from jax.experimental.pallas import tpu as pltpu
 from jax.sharding import PartitionSpec as P
 
 B = 256
 NK = 4
+AXES = ("prow", "pcol")
+HALF = 128
+TAIL = 16
 
 
 def from_root(value, axis, root):
@@ -17,7 +24,7 @@
     return jnp.transpose(jnp.any(listed, axis=1))
 
 
-def body(ancestor_inverse, lower_panel, pivot_inverse, struct_list):
+def general_body(ancestor_inverse, lower_panel, pivot_inverse, struct_list):
     row_count = ancestor_inverse.shape[0] // B
     col_count = ancestor_inverse.shape[1] // B
     grid_rows = lax.axis_size("prow")
@@ -61,6 +68,365 @@
     return (off_inverse, diag_inverse)
 
 
+VM = pl.BlockSpec(memory_space=pltpu.VMEM)
+SM = pl.BlockSpec(memory_space=pltpu.SMEM)
+
+
+def place():
+    p = lax.axis_index("prow")
+    q = lax.axis_index("pcol")
+    return p, q // 2, q % 2
+
+
+def call(kernel, outs, specs, scratch, flops, moved, name):
+    return pl.pallas_call(
+        kernel,
+        out_shape=outs,
+        in_specs=specs,
+        out_specs=jax.tree.map(lambda _: VM, outs),
+        scratch_shapes=scratch,
+        compiler_params=pltpu.CompilerParams(vmem_limit_bytes=16 * 2**20),
+        cost_estimate=pl.CostEstimate(flops=flops, bytes_accessed=moved, transcendentals=0),
+        name=name,
+    )
+
+
+def split_kernel(lower_ref, near_ref, to_x, to_y, to_both, keep, sems):
+    p, _, _ = place()
+    shard = lower_ref.shape[0]
+    moves = []
+
+    def move(flip, start, width, out, slot, lane):
+        at = pl.multiple_of((p ^ flip) * B + start, HALF)
+        item = pltpu.make_async_copy(
+            lower_ref.at[:, pl.ds(at, width)],
+            out.at[pl.ds(slot * shard, shard), pl.ds(lane, width)],
+            sems.at[len(moves)],
+        )
+        item.start()
+        moves.append(item)
+
+    move(3, 0, B, near_ref, 0, 0)
+    move(1, 0, HALF, near_ref, 0, B)
+    move(2, HALF, HALF, near_ref, 0, B + HALF)
+    move(1, HALF, HALF, near_ref, 1, 0)
+    move(2, 0, HALF, near_ref, 1, HALF)
+    move(0, 0, B, near_ref, 1, B)
+    for flip, out in ((1, to_x), (2, to_y), (3, to_both), (0, keep)):
+        move(flip, 0, B, out, 0, 0)
+    for item in moves:
+        item.wait()
+
+
+def pair_kernel(own_ref, one_ref, out_ref):
+    shard = own_ref.shape[0] // 2
+    out_ref[:shard] = own_ref[shard:]
+    out_ref[shard : 2 * shard] = one_ref[shard:]
+
+
+def pack_kernel(*refs):
+    out_ref = refs[-1]
+    _, z, _ = place()
+    shard = out_ref.shape[0] // 4
+    parts = (
+        ((refs[0], 0), (refs[0], 1), (refs[1], 0), (refs[1], 1))
+        if len(refs) == 3
+        else tuple((ref, 0) for ref in refs[:4])
+    )
+    for flip, (ref, slot) in enumerate(parts):
+        out_ref[pl.ds(pl.multiple_of((z ^ flip) * shard, 64), shard)] = ref[
+            slot * shard : (slot + 1) * shard
+        ]
+
+
+def assemble(mine, theirs, panel, table_ref, parts):
+    p, _, c = place()
+    shard = panel.shape[0] // 8
+    for zz in range(4):
+        for ref, core in ((mine, c), (theirs, 1 - c)):
+            at = pl.multiple_of((2 * zz + core) * shard, 64)
+            panel[pl.ds(at, shard)] = ref[zz * shard : (zz + 1) * shard]
+    blocks = panel.shape[0] // B
+    for block in range(blocks):
+        for flip, lane, width in parts:
+            listed = table_ref[p ^ flip, p * blocks + block]
+
+            @pl.when(listed == 0)
+            def _(block=block, lane=lane, width=width):
+                panel[block * B : (block + 1) * B, lane : lane + width] = jnp.zeros(
+                    (B, width), jnp.bfloat16
+                )
+
+
+def encode(value):
+    top = jnp.max(jnp.abs(value), axis=0, keepdims=True)
+    power = jnp.floor(jnp.log2(jnp.maximum(top, 2e-34))) + 1.0
+    scaled = jnp.round(value * jnp.exp2(15.0 - power))
+    code = jnp.clip(scaled, -32767.0, 32767.0).astype(jnp.int32).astype(jnp.int16)
+    return code, power
+
+
+def put_coded(ref, values, block, first=0):
+    code, power = encode(values)
+    ref[first + block * B : first + (block + 1) * B] = code
+    return power
+
+
+def put_tail(ref, powers, first=0):
+    rows = first + len(powers) * B
+    row = lax.broadcasted_iota(jnp.int32, (TAIL, HALF), 0)
+    tail = jnp.zeros((TAIL, HALF), jnp.float32)
+    for block, power in enumerate(powers):
+        tail = jnp.where(row == block, power, tail)
+    ref[rows : rows + TAIL] = tail.astype(jnp.int32).astype(jnp.int16)
+
+
+def decode(ref, block, blocks, first=0):
+    last = first + blocks * B
+    tail = ref[last : last + TAIL].astype(jnp.int32).astype(jnp.float32)
+    step = jnp.exp2(tail[block : block + 1] - 15.0)
+    code = ref[first + block * B : first + (block + 1) * B]
+    return code.astype(jnp.int32).astype(jnp.float32) * step
+
+
+def first_kernel(table_ref, a_ref, mine, theirs, x_ref, y_ref, panel):
+    assemble(mine, theirs, panel, table_ref, ((3, 0, B), (1, B, HALF), (2, B + HALF, HALF)))
+    blocks = a_ref.shape[0] // B
+    share = blocks * B + TAIL
+    places = ((x_ref, 0), (y_ref, 0), (x_ref, share), (y_ref, share))
+    powers = [[], [], [], []]
+    for b in range(blocks):
+        total = -jnp.dot(
+            a_ref[b * B : (b + 1) * B], panel[...], preferred_element_type=jnp.float32
+        )
+        for i, (ref, first) in enumerate(places):
+            part = total[:, i * HALF : (i + 1) * HALF]
+            powers[i].append(put_coded(ref, part, b, first))
+    for (ref, first), power in zip(places, powers):
+        put_tail(ref, power, first)
+
+
+def second_kernel(
+    table_ref, a_ref, mine, theirs, by_x, by_y, x_ref, y_ref, own_ref, panel
+):
+    assemble(mine, theirs, panel, table_ref, ((1, 0, HALF), (2, HALF, HALF), (0, B, B)))
+    blocks = a_ref.shape[0] // B
+    x_powers, y_powers = [], []
+    for b in range(blocks):
+        rows = slice(b * B, (b + 1) * B)
+        total = -jnp.dot(a_ref[rows], panel[...], preferred_element_type=jnp.float32)
+        x_powers.append(put_coded(x_ref, total[:, :HALF] + decode(by_y, b, blocks), b))
+        y_powers.append(put_coded(y_ref, total[:, HALF:B] + decode(by_x, b, blocks), b))
+        own_ref[rows] = total[:, B:]
+    put_tail(x_ref, x_powers)
+    put_tail(y_ref, y_powers)
+
+
+def sum_kernel(table_ref, own_ref, x_first, y_first, x_second, y_second, off_ref, rest_ref):
+    p, z, c = place()
+    blocks = off_ref.shape[0] // B
+    share = blocks * B + TAIL
+    first = (2 * z + c) * blocks
+    for b in range(blocks):
+        rows = slice(b * B, (b + 1) * B)
+        left = decode(x_first, b, blocks, share) + decode(y_second, b, blocks)
+        right = decode(y_first, b, blocks, share) + decode(x_second, b, blocks)
+        total = own_ref[rows] + jnp.concatenate([left, right], axis=1)
+        total = jnp.where(table_ref[p, first + b] > 0, total, 0.0)
+        high = total.astype(jnp.bfloat16)
+        off_ref[rows] = high
+        rest_ref[rows] = (total - high.astype(jnp.float32)).astype(jnp.bfloat16)
+
+
+def route_kernel(own, x, y, both, *outs):
+    p, z, _ = place()
+    for flip, out in enumerate(outs):
+        for turn, ref in enumerate((own, x, y, both)):
+
+            @pl.when((p ^ z) == (turn ^ flip))
+            def _(ref=ref, out=out):
+                out[...] = ref[...]
+
+
+def share_kernel(own, one, two, three, keep_ref, give_ref):
+    _, z, c = place()
+    shard = own.shape[0]
+    for flip, ref in enumerate((own, one, two, three)):
+        chip = z ^ flip
+        at = pl.multiple_of((chip % 2) * shard, 64)
+
+        @pl.when(chip // 2 == c)
+        def _(ref=ref, at=at):
+            keep_ref[pl.ds(at, shard)] = ref[...]
+
+        @pl.when(chip // 2 != c)
+        def _(ref=ref, at=at):
+            give_ref[pl.ds(at, shard)] = ref[...]
+
+
+def diag_kernel(off_ref, rest_ref, keep, came, diag_ref, lower):
+    _, z, c = place()
+    shard = keep.shape[0] // 2
+    for half in range(2):
+        for ref, core in ((keep, c), (came, 1 - c)):
+            at = pl.multiple_of((2 * half + core) * shard, 64)
+            lower[pl.ds(at, shard)] = ref[half * shard : (half + 1) * shard]
+    contract = (((0,), (0,)), ((), ()))
+    diag = lax.dot_general(
+        lower[...], off_ref[...], contract, preferred_element_type=jnp.float32
+    ) + lax.dot_general(
+        lower[...], rest_ref[...], contract, preferred_element_type=jnp.float32
+    )
+    piece = B // 8
+    for zz in range(4):
+        for cc in range(2):
+            slot = (cc ^ c) * 4 + (zz ^ z)
+            at = (2 * zz + cc) * piece
+            diag_ref[pl.ds(pl.multiple_of(slot * piece, piece), piece)] = diag[at : at + piece]
+
+
+def send(value, move):
+    found = []
+    for p in range(4):
+        for z in range(4):
+            for c in range(2):
+                to = move(p, z, c)
+                found.append((p * 8 + 2 * z + c, to[0] * 8 + 2 * to[1] + to[2]))
+    return lax.ppermute(value, AXES, found)
+
+
+def chip_swap(p, z, c):
+    return (p, z, 1 - c)
+
+
+def along(flip):
+    return lambda p, z, c: (p, z ^ flip, c)
+
+
+def across(flip):
+    return lambda p, z, c: (p ^ flip, z, c)
+
+
+def after(value, *earlier):
+    return lax.optimization_barrier((value, *earlier))[0]
+
+
+def line_body(ancestor_inverse, lower_panel, pivot_inverse, struct_list):
+    rows, depth = ancestor_inverse.shape
+    shard = lower_panel.shape[0]
+    bf16, f32, i16 = jnp.bfloat16, jnp.float32, jnp.int16
+    shape = jax.ShapeDtypeStruct
+    wide = 2 * B
+    moved = 2 * rows * depth
+    flops = 2 * rows * depth * wide
+
+    def small(kernel, outs, name, *args, specs=None, scratch=()):
+        return call(
+            kernel, outs, specs or [VM] * len(args), list(scratch), shard * B, shard * B, name
+        )(*args)
+
+    piece = shape((shard, B), bf16)
+    near, to_x, to_y, to_both, keep = small(
+        split_kernel,
+        (shape((2 * shard, wide), bf16), piece, piece, piece, piece),
+        "split_lower",
+        lower_panel,
+        specs=[pl.BlockSpec(memory_space=pl.ANY)],
+        scratch=[pltpu.SemaphoreType.DMA((10,))],
+    )
+    names = jnp.arange(4 * depth // B, dtype=jnp.int32)
+    table = jnp.any(struct_list[:, :, None] == names, axis=1).astype(jnp.int32)
+
+    line = shape((4 * shard, wide), bf16)
+    panel = [pltpu.VMEM((depth, wide), bf16)]
+    coded = shape((rows + TAIL, HALF), i16)
+    coded_two = shape((2 * (rows + TAIL), HALF), i16)
+
+    own = near[:shard]
+    one = send(near, along(1))
+    two = send(own, along(2))
+    three = send(own, along(3))
+    rows_x = send(to_x, across(1))
+    rows_y = send(to_y, across(2))
+    rows_both = send(to_both, across(3))
+    mine = small(
+        pack_kernel, line, "pack_first", own, one[:shard], two, after(three, rows_x, rows_y, rows_both)
+    )
+    pair = small(pair_kernel, shape((2 * shard + TAIL, wide), bf16), "pair", near, one)
+    stay, to_one, to_two, to_three = small(
+        route_kernel, (piece,) * 4, "route", keep, rows_x, rows_y, rows_both
+    )
+
+    two = send(after(pair, mine), along(2))
+    from_one = send(after(to_one, mine), along(1))
+    theirs = send(mine, chip_swap)
+    x_first, y_first = call(
+        first_kernel, (coded_two, coded_two), [SM] + [VM] * 3, panel, flops, moved, "first"
+    )(table, ancestor_inverse, mine, theirs)
+    x_first = send(x_first, across(1))
+    y_first = send(y_first, across(2))
+    mine = small(pack_kernel, line, "pack_second", pair, after(two, x_first, y_first, from_one))
+
+    theirs = send(mine, chip_swap)
+    from_two = send(after(to_two, mine), along(2))
+    from_three = send(after(to_three, mine), along(3))
+    x_second, y_second, own = call(
+        second_kernel,
+        (coded, coded, shape((rows, B), f32)),
+        [SM] + [VM] * 5,
+        panel,
+        flops,
+        moved,
+        "second",
+    )(table, ancestor_inverse, mine, theirs, x_first, y_first)
+    x_second = send(x_second, across(1))
+    y_second = send(y_second, across(2))
+    off_inverse, rest = call(
+        sum_kernel,
+        (shape((rows, B), bf16),) * 2,
+        [SM] + [VM] * 5,
+        [],
+        8 * rows * B,
+        12 * rows * B,
+        "sum",
+    )(table, own, x_first, y_first, x_second, y_second)
+    half_rows = shape((2 * shard, B), bf16)
+    keep, give = small(
+        share_kernel, (half_rows, half_rows), "share", stay, from_one, from_two, from_three
+    )
+    came = send(give, chip_swap)
+    diag = call(
+        diag_kernel,
+        shape((B, B), f32),
+        [VM] * 4,
+        [pltpu.VMEM((rows, B), bf16)],
+        4 * rows * B * B,
+        moved,
+        "diag",
+    )(off_inverse, rest, keep, came)
+
+    half, part = B // 2, B // 8
+    total = diag[:half] + send(diag[half:], chip_swap)
+    total = total[: 2 * part] + send(total[2 * part :], along(2))
+    total = total[:part] + send(total[part:], along(1))
+    return off_inverse, pivot_inverse - total
+
+
+def body(ancestor_inverse, lower_panel, pivot_inverse, struct_list):
+    rows, depth = ancestor_inverse.shape
+    shard = lower_panel.shape[0]
+    line = (
+        lax.axis_size("prow") == 4
+        and lax.axis_size("pcol") == 8
+        and depth == 8 * shard
+        and depth == 2 * rows
+        and shard % 64 == 0
+        and shard <= B
+    )
+    plan = line_body if line else general_body
+    return plan(ancestor_inverse, lower_panel, pivot_inverse, struct_list)
+
+
 def solution(mesh):
     placed = (P("pcol", "prow"), P(("prow", "pcol"), None), P("pcol", "prow"), P())
     return jax.shard_map(

time: 208 us -> 77.7 us (0.37)
  waiting for transfers between devices: 164 us -> 44.8 us
  starting transfers between devices: 0.16 us -> 19.8 us
  between operations: 13.9 us -> 0.8 us
  local copies, waits for them, and re-layouts: 12 us -> 2.29 us
  Pallas kernels: 0 us -> 9.09 us
  other arithmetic: 9.39 us -> 0.75 us
  matrix products: 7.96 us -> 0 us
    psum x1 -> x0, waiting for transfers between devices: 50.3 us -> none  [from_root(): return lax.psum(jnp.where(mine, value, jnp.zeros_like(value)), axis)]
    reduce_scatter x1 -> x0, waiting for transfers between devices: 47.3 us -> none  [body(): lax.psum_scatter(partial_value, 'prow', scatter_dimension=1, tiled=True)]
    ppermute x0 -> x20, waiting for transfers between devices: none -> 44.8 us  [send(): return lax.ppermute(value, AXES, found)]
    all_gather x1 -> x0, waiting for transfers between devices: 38.4 us -> none  [body(): gathered = lax.all_gather(lower_panel, 'pcol', axis=0, tiled=True)]
    unnamed x5 -> x0, waiting for transfers between devices: 28.4 us -> none
    ppermute x0 -> x20, starting transfers between devices: none -> 19.8 us  [send(): return lax.ppermute(value, AXES, found)]
    pallas_call x0 -> x10, Pallas kernels: none -> 9.09 us  [the longest x1 3.26 us: line_body(): call(first_kernel, (coded_two, coded_two), [SM] + [VM] * 3, panel, flops,...]
    dot_general x2 -> x0, matrix products: 7.96 us -> none  [the longest x1 6.21 us: body(): jnp.dot(ancestor_inverse, masked, preferred_element_type=jnp.float32)]
  transfers between devices with their start and end apart: 4 -> 20, of which waited for: 4 -> 13; matrix products, arithmetic and copies ran while one was open for 8% -> 0% of each run, Pallas kernels for 0% -> 10%
where the time goes in v2:
time: 77.7 us; the launch traced here: 77.5 us
  waiting for transfers between devices  44.8 us (58%)
  starting transfers between devices  19.8 us (25%)
  Pallas kernels  9.09 us (12%)
  local copies, waits for them, and re-layouts  2.29 us (3%)
  between operations  0.8 us (1%)
    ppermute x20, waiting for transfers between devices, send(): return lax.ppermute(value, AXES, found)  44.8 us
    ppermute x20, starting transfers between devices, send(): return lax.ppermute(value, AXES, found)  19.8 us
    pallas_call x1, Pallas kernels, line_body(): call(first_kernel, (coded_two, coded_two), [SM] + [VM] * 3, panel, flops,...  3.26 us
    pallas_call x1, Pallas kernels, line_body(): call(second_kernel, (coded, coded, shape((rows, B), f32)), [SM] + [VM] *...  2.37 us
    unnamed x11, local copies, waits for them, and re-layouts  2.24 us
    pallas_call x1, Pallas kernels, line_body(): call(sum_kernel, (shape((rows, B), bf16),) * 2, [SM] + [VM] * 5, [], 8 *...  1.58 us
  transfers between devices with their start and end apart: 20, of which 13 were waited for; matrix products, arithmetic and copies ran while one was open for 0% of the time, Pallas kernels for 10%

profile of v2, /device:TPU:0, one launch (start us, length us, event | category | flops | bytes accessed | tf_op | source)
XLA Modules:
  0.0 77.5 jit_solution(12759648577689974225)
XLA Ops:
  0.6 0.0 copy-start
  0.6 0.0 copy-start.1
  0.6 1.1 %copy-done.1 = bf16[192,1024]{1,0:T(8,128)(2,1)S(1)} copy-done((bf16[192,1024]{1,0:T(8,128)(2,1)S(1)}, bf16[192,1024]{1,0:T(8,128)(2,1)}, u32[]{:S(2)}) %copy-start.1) | copy-done | bytes 393240
  1.8 0.0 copy-start.4
  1.8 0.2 split_lower.1
  2.0 3.1 %collective-permute-start = (bf16[384,512]{1,0:T(8,128)(2,1)S(1)}, bf16[384,512]{1,0:T(8,128)(2,1)S(1)}, u32[]{:S(2)}, u32[]{:S(2)}) collective-permute-start(bf16[384,512]{1,0:T(8,128)(2,1)S(1)} %get-tuple-element.26.own_ref), channel_id=1, source_target_pairs={{0,2},{1,3},{2,0},{3,1},{4,6},{5,7},{6,4},{7,5},{8,10},{9,11},{10,... | collective-permute-start | bytes 1179656 | tf_op jit(solution)/shard_map/ppermute | solution.py:295
  5.1 1.5 %collective-permute-start.3 = (bf16[192,256]{1,0:T(8,128)(2,1)S(1)}, bf16[192,256]{1,0:T(8,128)(2,1)S(1)}, u32[]{:S(2)}, u32[]{:S(2)}) collective-permute-start(bf16[192,256]{1,0:T(8,128)(2,1)S(1)} %get-tuple-element.27), channel_id=1, source_target_pairs={{0,8},{1,9},{2,10},{3,11},{4,12},{5,13},{6,14},{7,15},{8,0},{9,1},... | collective-permute-start | bytes 294920 | tf_op jit(solution)/shard_map/ppermute | solution.py:295
  6.6 2.5 %collective-permute-start.2 = (bf16[192,512]{1,0:T(8,128)(2,1)S(1)}, bf16[192,512]{1,0:T(8,128)(2,1)S(1)}, u32[]{:S(2)}, u32[]{:S(2)}) collective-permute-start(bf16[192,512]{1,0:T(8,128)(2,1)S(1)} %slice.24.refs_0_), channel_id=1, source_target_pairs={{0,6},{1,7},{2,4},{3,5},{4,2},{5,3},{6,0},{7,1},{8,14},{9,15},{10,... | collective-permute-start | bytes 589832 | tf_op jit(solution)/shard_map/ppermute | solution.py:295
  9.2 0.2 collective-permute-start.1
  9.4 1.5 %collective-permute-start.4 = (bf16[192,256]{1,0:T(8,128)(2,1)S(1)}, bf16[192,256]{1,0:T(8,128)(2,1)S(1)}, u32[]{:S(2)}, u32[]{:S(2)}) collective-permute-start(bf16[192,256]{1,0:T(8,128)(2,1)S(1)} %get-tuple-element.28), channel_id=1, source_target_pairs={{0,16},{1,17},{2,18},{3,19},{4,20},{5,21},{6,22},{7,23},{8,24},{9,... | collective-permute-start | bytes 294920 | tf_op jit(solution)/shard_map/ppermute | solution.py:295
  10.9 0.0 collective-permute-done.3.x
  10.9 1.3 %collective-permute-start.5 = (bf16[192,256]{1,0:T(8,128)(2,1)S(1)}, bf16[192,256]{1,0:T(8,128)(2,1)S(1)}, u32[]{:S(2)}, u32[]{:S(2)}) collective-permute-start(bf16[192,256]{1,0:T(8,128)(2,1)S(1)} %get-tuple-element.29), channel_id=1, source_target_pairs={{0,24},{1,25},{2,26},{3,27},{4,28},{5,29},{6,30},{7,31},{8,16},{9,... | collective-permute-start | bytes 294920 | tf_op jit(solution)/shard_map/ppermute | solution.py:295
  12.2 2.8 %collective-permute-done.4.y = bf16[192,256]{1,0:T(8,128)(2,1)S(1)} collective-permute-done((bf16[192,256]{1,0:T(8,128)(2,1)S(1)}, bf16[192,256]{1,0:T(8,128)(2,1)S(1)}, u32[]{:S(2)}, u32[]{:S(2)}) %collective-permute-start.4) | collective-permute-done | bytes 98336 | tf_op jit(solution)/shard_map/ppermute | solution.py:295
  15.0 1.4 %collective-permute-done.5.both = bf16[192,256]{1,0:T(8,128)(2,1)S(1)} collective-permute-done((bf16[192,256]{1,0:T(8,128)(2,1)S(1)}, bf16[192,256]{1,0:T(8,128)(2,1)S(1)}, u32[]{:S(2)}, u32[]{:S(2)}) %collective-permute-start.5) | collective-permute-done | bytes 98336 | tf_op jit(solution)/shard_map/ppermute | solution.py:295
  16.4 5.4 %collective-permute-done.2.refs_3_ = bf16[192,512]{1,0:T(8,128)(2,1)S(1)} collective-permute-done((bf16[192,512]{1,0:T(8,128)(2,1)S(1)}, bf16[192,512]{1,0:T(8,128)(2,1)S(1)}, u32[]{:S(2)}, u32[]{:S(2)}) %collective-permute-start.2) | collective-permute-done | bytes 196640 | tf_op jit(solution)/shard_map/ppermute | solution.py:295
  21.8 0.0 collective-permute-done.one_ref
  21.8 4.5 %collective-permute-done.1.refs_2_ = bf16[192,512]{1,0:T(8,128)(2,1)S(1)} collective-permute-done((bf16[192,512]{1,0:T(8,128)(2,1)S(1)}, bf16[192,512]{1,0:T(8,128)(2,1)S(1)}, u32[]{:S(2)}, u32[]{:S(2)}) %collective-permute-start.1) | collective-permute-done | bytes 196640 | tf_op jit(solution)/shard_map/ppermute | solution.py:295
  26.3 1.0 %pack_first.1.mine = bf16[768,512]{1,0:T(8,128)(2,1)} custom-call(bf16[192,512]{1,0:T(8,128)(2,1)S(1)} %slice.24.refs_0_, bf16[192,512]{1,0:T(8,128)(2,1)S(1)} %slice.32.refs_1_, bf16[192,512]{1,0:T(8,128)(2,1)S(1)} %collective-permute-done.1.refs_2_, bf16[192,512]{1,0:T(8,128)(2,1)S(1)} %collective-permute-done.2.refs_3_), custom_call_target="tpu_custom_call" | custom-call | flops 49152 | bytes 49152 | tf_op jit(solution)/shard_map/pack_first/pallas_call | solution.py:324
  27.3 0.0 collective-permute-start.7
  27.3 0.0 copy-done.4
  27.3 0.1 copy.6
  27.4 0.1 fusion.1
  27.5 0.1 collective-permute-start.6
  27.6 2.3 %collective-permute-done.7.theirs = bf16[768,512]{1,0:T(8,128)(2,1)} collective-permute-done((bf16[768,512]{1,0:T(8,128)(2,1)}, bf16[768,512]{1,0:T(8,128)(2,1)}, u32[]{:S(2)}, u32[]{:S(2)}) %collective-permute-start.7) | collective-permute-done | bytes 786464 | tf_op jit(solution)/shard_map/ppermute | solution.py:295
  29.9 0.0 copy-done
  29.9 3.3 %first.1 = (s16[1568,128]{1,0:T(8,128)(2,1)S(1)}, s16[1568,128]{1,0:T(8,128)(2,1)S(1)}) custom-call(s32[4,24]{1,0:T(4,128)S(1)} %convert_element_type.3.table_ref, bf16[768,1536]{1,0:T(8,128)(2,1)S(1)} %copy-done, bf16[768,512]{1,0:T(8,128)(2,1)} %pack_first.1.mine, bf16[768,512]{1,0:T(8,128)(2,1)} %collective-permute-done.7.theirs), custom_call_target="tpu_custom_call" | custom-call | flops 1207959552 | bytes 2359296 | tf_op jit(solution)/shard_map/first/pallas_call | solution.py:363
  33.2 0.6 collective-permute-start.8
  33.8 1.5 %collective-permute-start.9 = (s16[1568,128]{1,0:T(8,128)(2,1)S(1)}, s16[1568,128]{1,0:T(8,128)(2,1)S(1)}, u32[]{:S(2)}, u32[]{:S(2)}) collective-permute-start(s16[1568,128]{1,0:T(8,128)(2,1)S(1)} %get-tuple-element.33), channel_id=1, source_target_pairs={{0,16},{1,17},{2,18},{3,19},{4,20},{5,21},{6,22},{7,23},{8,24},{9,... | collective-permute-start | bytes 1204232 | tf_op jit(solution)/shard_map/ppermute | solution.py:295
  35.4 0.9 %collective-permute-start.10 = (bf16[192,256]{1,0:T(8,128)(2,1)S(1)}, bf16[192,256]{1,0:T(8,128)(2,1)S(1)}, u32[]{:S(2)}, u32[]{:S(2)}) collective-permute-start(bf16[192,256]{1,0:T(8,128)(2,1)S(1)} %get-tuple-element.36), channel_id=1, source_target_pairs={{0,2},{1,3},{2,0},{3,1},{4,6},{5,7},{6,4},{7,5},{8,10},{9,11},{10,... | collective-permute-start | bytes 294920 | tf_op jit(solution)/shard_map/ppermute | solution.py:295
  36.3 3.8 %collective-permute-done.10.one = bf16[192,256]{1,0:T(8,128)(2,1)S(1)} collective-permute-done((bf16[192,256]{1,0:T(8,128)(2,1)S(1)}, bf16[192,256]{1,0:T(8,128)(2,1)S(1)}, u32[]{:S(2)}, u32[]{:S(2)}) %collective-permute-start.10) | collective-permute-done | bytes 98336 | tf_op jit(solution)/shard_map/ppermute | solution.py:295
  40.0 9.1 %collective-permute-done.6.refs_1_ = bf16[400,512]{1,0:T(8,128)(2,1)S(1)} collective-permute-done((bf16[400,512]{1,0:T(8,128)(2,1)S(1)}, bf16[400,512]{1,0:T(8,128)(2,1)S(1)}, u32[]{:S(2)}, u32[]{:S(2)}) %collective-permute-start.6) | collective-permute-done | bytes 409632 | tf_op jit(solution)/shard_map/ppermute | solution.py:295
  49.1 0.0 collective-permute-done.8.by_x.x_first
  49.1 0.0 collective-permute-done.9.by_y.y_first
  49.1 0.1 pack_second.1.mine
  49.2 0.1 collective-permute-start.11
  49.3 0.3 collective-permute-start.14
  49.6 2.0 %collective-permute-start.15 = (bf16[192,256]{1,0:T(8,128)(2,1)S(1)}, bf16[192,256]{1,0:T(8,128)(2,1)S(1)}, u32[]{:S(2)}, u32[]{:S(2)}) collective-permute-start(bf16[192,256]{1,0:T(8,128)(2,1)S(1)} %get-tuple-element.47), channel_id=1, source_target_pairs={{0,6},{1,7},{2,4},{3,5},{4,2},{5,3},{6,0},{7,1},{8,14},{9,15},{10,... | collective-permute-start | bytes 294920 | tf_op jit(solution)/shard_map/ppermute | solution.py:295
  51.6 0.0 collective-permute-done.11.theirs
  51.6 2.4 %second.1 = (s16[784,128]{1,0:T(8,128)(2,1)S(1)}, s16[784,128]{1,0:T(8,128)(2,1)S(1)}, f32[768,256]{1,0:T(8,128)S(1)}) custom-call(s32[4,24]{1,0:T(4,128)S(1)} %convert_element_type.3.table_ref, bf16[768,1536]{1,0:T(8,128)(2,1)S(1)} %copy-done, bf16[768,512]{1,0:T(8,128)(2,1)S(1)} %pack_second.1.mine, bf16[768,512]{1,0:T(8,128)(2,1)S(1)} %collective-permute-done.11.theirs, ...), custom_call_target="tpu_custom_call" | custom-call | flops 1207959552 | bytes 2359296 | tf_op jit(solution)/shard_map/second/pallas_call | solution.py:373
  54.0 1.2 %collective-permute-start.12 = (s16[784,128]{1,0:T(8,128)(2,1)S(1)}, s16[784,128]{1,0:T(8,128)(2,1)S(1)}, u32[]{:S(2)}, u32[]{:S(2)}) collective-permute-start(s16[784,128]{1,0:T(8,128)(2,1)S(1)} %get-tuple-element.39), channel_id=1, source_target_pairs={{0,8},{1,9},{2,10},{3,11},{4,12},{5,13},{6,14},{7,15},{8,0},{9,1},... | collective-permute-start | bytes 602120 | tf_op jit(solution)/shard_map/ppermute | solution.py:295
  55.2 0.9 %collective-permute-start.13 = (s16[784,128]{1,0:T(8,128)(2,1)S(1)}, s16[784,128]{1,0:T(8,128)(2,1)S(1)}, u32[]{:S(2)}, u32[]{:S(2)}) collective-permute-start(s16[784,128]{1,0:T(8,128)(2,1)S(1)} %get-tuple-element.40), channel_id=1, source_target_pairs={{0,16},{1,17},{2,18},{3,19},{4,20},{5,21},{6,22},{7,23},{8,24},{9,... | collective-permute-start | bytes 602120 | tf_op jit(solution)/shard_map/ppermute | solution.py:295
  56.1 3.1 %collective-permute-done.14.two = bf16[192,256]{1,0:T(8,128)(2,1)S(1)} collective-permute-done((bf16[192,256]{1,0:T(8,128)(2,1)S(1)}, bf16[192,256]{1,0:T(8,128)(2,1)S(1)}, u32[]{:S(2)}, u32[]{:S(2)}) %collective-permute-start.14) | collective-permute-done | bytes 98336 | tf_op jit(solution)/shard_map/ppermute | solution.py:295
  59.2 0.0 collective-permute-done.15.three
  59.2 0.0 copy-start.3
  59.2 0.1 share.1
  59.3 0.1 collective-permute-start.16
  59.3 1.7 %collective-permute-done.12.x_second = s16[784,128]{1,0:T(8,128)(2,1)S(1)} collective-permute-done((s16[784,128]{1,0:T(8,128)(2,1)S(1)}, s16[784,128]{1,0:T(8,128)(2,1)S(1)}, u32[]{:S(2)}, u32[]{:S(2)}) %collective-permute-start.12) | collective-permute-done | bytes 200736 | tf_op jit(solution)/shard_map/ppermute | solution.py:295
  61.0 0.9 %collective-permute-done.13.y_second = s16[784,128]{1,0:T(8,128)(2,1)S(1)} collective-permute-done((s16[784,128]{1,0:T(8,128)(2,1)S(1)}, s16[784,128]{1,0:T(8,128)(2,1)S(1)}, u32[]{:S(2)}, u32[]{:S(2)}) %collective-permute-start.13) | collective-permute-done | bytes 200736 | tf_op jit(solution)/shard_map/ppermute | solution.py:295
  61.9 1.6 %sum.1 = (bf16[768,256]{1,0:T(8,128)(2,1)}, bf16[768,256]{1,0:T(8,128)(2,1)S(1)}) custom-call(s32[4,24]{1,0:T(4,128)S(1)} %convert_element_type.3.table_ref, f32[768,256]{1,0:T(8,128)S(1)} %get-tuple-element.38.own_ref, s16[1568,128]{1,0:T(8,128)(2,1)S(1)} %collective-permute-done.8.by_x.x_first, s16[1568,128]{1,0:T(8,128)(2,1)S(1)} %collective-permute-done.9.by_y.y_first, ...), custom_call_target="tpu_custom_call" | custom-call | flops 1572864 | bytes 2359296 | tf_op jit(solution)/shard_map/sum/pallas_call | solution.py:384
  63.5 0.0 collective-permute-done.16.came
  63.5 0.0 copy-start.2
  63.5 1.0 %copy-done.2 = bf16[768,256]{1,0:T(8,128)(2,1)S(1)} copy-done((bf16[768,256]{1,0:T(8,128)(2,1)S(1)}, bf16[768,256]{1,0:T(8,128)(2,1)}, u32[]{:S(2)}) %copy-start.2) | copy-done | bytes 393240
  64.5 0.4 diag.1
  64.9 0.1 collective-permute-start.17
  65.0 1.3 %collective-permute-done.17 = f32[128,256]{1,0:T(8,128)S(1)} collective-permute-done((f32[128,256]{1,0:T(8,128)S(1)}, f32[128,256]{1,0:T(8,128)S(1)}, u32[]{:S(2)}, u32[]{:S(2)}) %collective-permute-start.17) | collective-permute-done | bytes 131104 | tf_op jit(solution)/shard_map/ppermute | solution.py:295
  66.4 1.8 %collective-permute-start.18 = (f32[64,256]{1,0:T(8,128)S(1)}, f32[64,256]{1,0:T(8,128)S(1)}, u32[]{:S(2)}, u32[]{:S(2)}) collective-permute-start(f32[64,256]{1,0:T(8,128)S(1)} %slice.36), channel_id=1, source_target_pairs={{0,4},{1,5},{2,6},{3,7},{4,0},{5,1},{6,2},{7,3},{8,12},{9,13},{10,... | collective-permute-start | bytes 196616 | tf_op jit(solution)/shard_map/ppermute | solution.py:295
  68.2 4.7 %collective-permute-done.18 = f32[64,256]{1,0:T(8,128)S(1)} collective-permute-done((f32[64,256]{1,0:T(8,128)S(1)}, f32[64,256]{1,0:T(8,128)S(1)}, u32[]{:S(2)}, u32[]{:S(2)}) %collective-permute-start.18) | collective-permute-done | bytes 65568 | tf_op jit(solution)/shard_map/ppermute | solution.py:295
  72.9 0.1 collective-permute-start.19
  73.0 3.9 %collective-permute-done.19 = f32[32,256]{1,0:T(8,128)S(1)} collective-permute-done((f32[32,256]{1,0:T(8,128)S(1)}, f32[32,256]{1,0:T(8,128)S(1)}, u32[]{:S(2)}, u32[]{:S(2)}) %collective-permute-start.19) | collective-permute-done | bytes 32800 | tf_op jit(solution)/shard_map/ppermute | solution.py:295
  76.9 0.0 copy-done.3
  76.9 0.6 fusion
  (10 shorter events, 0.2 us)
Async XLA Ops:
  0.6 29.3 %copy-start = (bf16[768,1536]{1,0:T(8,128)(2,1)S(1)}, bf16[768,1536]{1,0:T(8,128)(2,1)}, u32[]{:S(2)}) copy-start(bf16[768,1536]{1,0:T(8,128)(2,1)} %a_ref.3) | copy-start | bytes 7077892
  0.6 1.1 %copy-start.1 = (bf16[192,1024]{1,0:T(8,128)(2,1)S(1)}, bf16[192,1024]{1,0:T(8,128)(2,1)}, u32[]{:S(2)}) copy-start(bf16[192,1024]{1,0:T(8,128)(2,1)} %lower_ref.1) | copy-start | bytes 1179652
  1.8 25.5 %copy-start.4 = (s32[4,12]{1,0:T(4,128)S(1)}, s32[4,12]{1,0:T(4,128)}, u32[]{:S(2)}) copy-start(s32[4,12]{1,0:T(4,128)} %param.7) | copy-start | bytes 580
  2.0 19.8 %collective-permute-start = (bf16[384,512]{1,0:T(8,128)(2,1)S(1)}, bf16[384,512]{1,0:T(8,128)(2,1)S(1)}, u32[]{:S(2)}, u32[]{:S(2)}) collective-permute-start(bf16[384,512]{1,0:T(8,128)(2,1)S(1)} %get-tuple-element.26.own_ref), channel_id=1, source_target_pairs={{0,2},{1,3},{2,0},{3,1},{4,6},{5,7},{6,4},{7,5},{8,10},{9,11},{10,... | collective-permute-start | bytes 1179656 | tf_op jit(solution)/shard_map/ppermute | solution.py:295
  5.1 5.8 %collective-permute-start.3 = (bf16[192,256]{1,0:T(8,128)(2,1)S(1)}, bf16[192,256]{1,0:T(8,128)(2,1)S(1)}, u32[]{:S(2)}, u32[]{:S(2)}) collective-permute-start(bf16[192,256]{1,0:T(8,128)(2,1)S(1)} %get-tuple-element.27), channel_id=1, source_target_pairs={{0,8},{1,9},{2,10},{3,11},{4,12},{5,13},{6,14},{7,15},{8,0},{9,1},... | collective-permute-start | bytes 294920 | tf_op jit(solution)/shard_map/ppermute | solution.py:295
  6.6 15.2 %collective-permute-start.2 = (bf16[192,512]{1,0:T(8,128)(2,1)S(1)}, bf16[192,512]{1,0:T(8,128)(2,1)S(1)}, u32[]{:S(2)}, u32[]{:S(2)}) collective-permute-start(bf16[192,512]{1,0:T(8,128)(2,1)S(1)} %slice.24.refs_0_), channel_id=1, source_target_pairs={{0,6},{1,7},{2,4},{3,5},{4,2},{5,3},{6,0},{7,1},{8,14},{9,15},{10,... | collective-permute-start | bytes 589832 | tf_op jit(solution)/shard_map/ppermute | solution.py:295
  9.2 17.1 %collective-permute-start.1 = (bf16[192,512]{1,0:T(8,128)(2,1)S(1)}, bf16[192,512]{1,0:T(8,128)(2,1)S(1)}, u32[]{:S(2)}, u32[]{:S(2)}) collective-permute-start(bf16[192,512]{1,0:T(8,128)(2,1)S(1)} %slice.24.refs_0_), channel_id=1, source_target_pairs={{0,4},{1,5},{2,6},{3,7},{4,0},{5,1},{6,2},{7,3},{8,12},{9,13},{10,... | collective-permute-start | bytes 589832 | tf_op jit(solution)/shard_map/ppermute | solution.py:295
  9.4 5.7 %collective-permute-start.4 = (bf16[192,256]{1,0:T(8,128)(2,1)S(1)}, bf16[192,256]{1,0:T(8,128)(2,1)S(1)}, u32[]{:S(2)}, u32[]{:S(2)}) collective-permute-start(bf16[192,256]{1,0:T(8,128)(2,1)S(1)} %get-tuple-element.28), channel_id=1, source_target_pairs={{0,16},{1,17},{2,18},{3,19},{4,20},{5,21},{6,22},{7,23},{8,24},{9,... | collective-permute-start | bytes 294920 | tf_op jit(solution)/shard_map/ppermute | solution.py:295
  10.9 5.5 %collective-permute-start.5 = (bf16[192,256]{1,0:T(8,128)(2,1)S(1)}, bf16[192,256]{1,0:T(8,128)(2,1)S(1)}, u32[]{:S(2)}, u32[]{:S(2)}) collective-permute-start(bf16[192,256]{1,0:T(8,128)(2,1)S(1)} %get-tuple-element.29), channel_id=1, source_target_pairs={{0,24},{1,25},{2,26},{3,27},{4,28},{5,29},{6,30},{7,31},{8,16},{9,... | collective-permute-start | bytes 294920 | tf_op jit(solution)/shard_map/ppermute | solution.py:295
  27.3 2.6 %collective-permute-start.7 = (bf16[768,512]{1,0:T(8,128)(2,1)}, bf16[768,512]{1,0:T(8,128)(2,1)}, u32[]{:S(2)}, u32[]{:S(2)}) collective-permute-start(bf16[768,512]{1,0:T(8,128)(2,1)} %pack_first.1.mine), channel_id=1, source_target_pairs={{0,1},{1,0},{2,3},{3,2},{4,5},{5,4},{6,7},{7,6},{8,9},{9,8},{10,11... | collective-permute-start | bytes 2359304 | tf_op jit(solution)/shard_map/ppermute | solution.py:295
  27.5 21.6 %collective-permute-start.6 = (bf16[400,512]{1,0:T(8,128)(2,1)S(1)}, bf16[400,512]{1,0:T(8,128)(2,1)S(1)}, u32[]{:S(2)}, u32[]{:S(2)}) collective-permute-start(bf16[400,512]{1,0:T(8,128)(2,1)S(1)} %pair.1.refs_0_), channel_id=1, source_target_pairs={{0,4},{1,5},{2,6},{3,7},{4,0},{5,1},{6,2},{7,3},{8,12},{9,13},{10,... | collective-permute-start | bytes 1228808 | tf_op jit(solution)/shard_map/ppermute | solution.py:295
  33.2 15.9 %collective-permute-start.8 = (s16[1568,128]{1,0:T(8,128)(2,1)S(1)}, s16[1568,128]{1,0:T(8,128)(2,1)S(1)}, u32[]{:S(2)}, u32[]{:S(2)}) collective-permute-start(s16[1568,128]{1,0:T(8,128)(2,1)S(1)} %get-tuple-element.32), channel_id=1, source_target_pairs={{0,8},{1,9},{2,10},{3,11},{4,12},{5,13},{6,14},{7,15},{8,0},{9,1},... | collective-permute-start | bytes 1204232 | tf_op jit(solution)/shard_map/ppermute | solution.py:295
  33.8 15.3 %collective-permute-start.9 = (s16[1568,128]{1,0:T(8,128)(2,1)S(1)}, s16[1568,128]{1,0:T(8,128)(2,1)S(1)}, u32[]{:S(2)}, u32[]{:S(2)}) collective-permute-start(s16[1568,128]{1,0:T(8,128)(2,1)S(1)} %get-tuple-element.33), channel_id=1, source_target_pairs={{0,16},{1,17},{2,18},{3,19},{4,20},{5,21},{6,22},{7,23},{8,24},{9,... | collective-permute-start | bytes 1204232 | tf_op jit(solution)/shard_map/ppermute | solution.py:295
  35.4 4.7 %collective-permute-start.10 = (bf16[192,256]{1,0:T(8,128)(2,1)S(1)}, bf16[192,256]{1,0:T(8,128)(2,1)S(1)}, u32[]{:S(2)}, u32[]{:S(2)}) collective-permute-start(bf16[192,256]{1,0:T(8,128)(2,1)S(1)} %get-tuple-element.36), channel_id=1, source_target_pairs={{0,2},{1,3},{2,0},{3,1},{4,6},{5,7},{6,4},{7,5},{8,10},{9,11},{10,... | collective-permute-start | bytes 294920 | tf_op jit(solution)/shard_map/ppermute | solution.py:295
  49.2 2.4 %collective-permute-start.11 = (bf16[768,512]{1,0:T(8,128)(2,1)S(1)}, bf16[768,512]{1,0:T(8,128)(2,1)S(1)}, u32[]{:S(2)}, u32[]{:S(2)}) collective-permute-start(bf16[768,512]{1,0:T(8,128)(2,1)S(1)} %pack_second.1.mine), channel_id=1, source_target_pairs={{0,1},{1,0},{2,3},{3,2},{4,5},{5,4},{6,7},{7,6},{8,9},{9,8},{10,11... | collective-permute-start | bytes 2359304 | tf_op jit(solution)/shard_map/ppermute | solution.py:295
  49.3 9.8 %collective-permute-start.14 = (bf16[192,256]{1,0:T(8,128)(2,1)S(1)}, bf16[192,256]{1,0:T(8,128)(2,1)S(1)}, u32[]{:S(2)}, u32[]{:S(2)}) collective-permute-start(bf16[192,256]{1,0:T(8,128)(2,1)S(1)} %get-tuple-element.45), channel_id=1, source_target_pairs={{0,4},{1,5},{2,6},{3,7},{4,0},{5,1},{6,2},{7,3},{8,12},{9,13},{10,... | collective-permute-start | bytes 294920 | tf_op jit(solution)/shard_map/ppermute | solution.py:295
  49.6 9.6 %collective-permute-start.15 = (bf16[192,256]{1,0:T(8,128)(2,1)S(1)}, bf16[192,256]{1,0:T(8,128)(2,1)S(1)}, u32[]{:S(2)}, u32[]{:S(2)}) collective-permute-start(bf16[192,256]{1,0:T(8,128)(2,1)S(1)} %get-tuple-element.47), channel_id=1, source_target_pairs={{0,6},{1,7},{2,4},{3,5},{4,2},{5,3},{6,0},{7,1},{8,14},{9,15},{10,... | collective-permute-start | bytes 294920 | tf_op jit(solution)/shard_map/ppermute | solution.py:295
  54.0 7.0 %collective-permute-start.12 = (s16[784,128]{1,0:T(8,128)(2,1)S(1)}, s16[784,128]{1,0:T(8,128)(2,1)S(1)}, u32[]{:S(2)}, u32[]{:S(2)}) collective-permute-start(s16[784,128]{1,0:T(8,128)(2,1)S(1)} %get-tuple-element.39), channel_id=1, source_target_pairs={{0,8},{1,9},{2,10},{3,11},{4,12},{5,13},{6,14},{7,15},{8,0},{9,1},... | collective-permute-start | bytes 602120 | tf_op jit(solution)/shard_map/ppermute | solution.py:295
  55.2 6.7 %collective-permute-start.13 = (s16[784,128]{1,0:T(8,128)(2,1)S(1)}, s16[784,128]{1,0:T(8,128)(2,1)S(1)}, u32[]{:S(2)}, u32[]{:S(2)}) collective-permute-start(s16[784,128]{1,0:T(8,128)(2,1)S(1)} %get-tuple-element.40), channel_id=1, source_target_pairs={{0,16},{1,17},{2,18},{3,19},{4,20},{5,21},{6,22},{7,23},{8,24},{9,... | collective-permute-start | bytes 602120 | tf_op jit(solution)/shard_map/ppermute | solution.py:295
  59.2 17.7 %copy-start.3 = (f32[32,256]{1,0:T(8,128)S(1)}, f32[32,256]{1,0:T(8,128)}, u32[]{:S(2)}) copy-start(f32[32,256]{1,0:T(8,128)} %param.6) | copy-start | bytes 98308
  59.3 4.2 %collective-permute-start.16 = (bf16[384,256]{1,0:T(8,128)(2,1)S(1)}, bf16[384,256]{1,0:T(8,128)(2,1)S(1)}, u32[]{:S(2)}, u32[]{:S(2)}) collective-permute-start(bf16[384,256]{1,0:T(8,128)(2,1)S(1)} %get-tuple-element.49), channel_id=1, source_target_pairs={{0,1},{1,0},{2,3},{3,2},{4,5},{5,4},{6,7},{7,6},{8,9},{9,8},{10,11... | collective-permute-start | bytes 589832 | tf_op jit(solution)/shard_map/ppermute | solution.py:295
  63.5 1.0 %copy-start.2 = (bf16[768,256]{1,0:T(8,128)(2,1)S(1)}, bf16[768,256]{1,0:T(8,128)(2,1)}, u32[]{:S(2)}) copy-start(bf16[768,256]{1,0:T(8,128)(2,1)} %get-tuple-element.24.off_ref) | copy-start | bytes 1179652
  64.9 1.4 %collective-permute-start.17 = (f32[128,256]{1,0:T(8,128)S(1)}, f32[128,256]{1,0:T(8,128)S(1)}, u32[]{:S(2)}, u32[]{:S(2)}) collective-permute-start(f32[128,256]{1,0:T(8,128)S(1)} %slice.34), channel_id=1, source_target_pairs={{0,1},{1,0},{2,3},{3,2},{4,5},{5,4},{6,7},{7,6},{8,9},{9,8},{10,11... | collective-permute-start | bytes 393224 | tf_op jit(solution)/shard_map/ppermute | solution.py:295
  66.4 6.5 %collective-permute-start.18 = (f32[64,256]{1,0:T(8,128)S(1)}, f32[64,256]{1,0:T(8,128)S(1)}, u32[]{:S(2)}, u32[]{:S(2)}) collective-permute-start(f32[64,256]{1,0:T(8,128)S(1)} %slice.36), channel_id=1, source_target_pairs={{0,4},{1,5},{2,6},{3,7},{4,0},{5,1},{6,2},{7,3},{8,12},{9,13},{10,... | collective-permute-start | bytes 196616 | tf_op jit(solution)/shard_map/ppermute | solution.py:295
  72.9 4.0 %collective-permute-start.19 = (f32[32,256]{1,0:T(8,128)S(1)}, f32[32,256]{1,0:T(8,128)S(1)}, u32[]{:S(2)}, u32[]{:S(2)}) collective-permute-start(f32[32,256]{1,0:T(8,128)S(1)} %slice.38), channel_id=1, source_target_pairs={{0,2},{1,3},{2,0},{3,1},{4,6},{5,7},{6,4},{7,5},{8,10},{9,11},{10,... | collective-permute-start | bytes 98312 | tf_op jit(solution)/shard_map/ppermute | solution.py:295

commit v3 on v0

--- a/solution.py
+++ b/solution.py
@@ -1,10 +1,16 @@
+import functools
+
 import jax
 import jax.numpy as jnp
 from jax import lax
+from jax.experimental import pallas as pl
+from jax.experimental.pallas import tpu as pltpu
 from jax.sharding import PartitionSpec as P
 
 B = 256
 NK = 4
+AXES = ("prow", "pcol")
+TAIL = 16
 
 
 def from_root(value, axis, root):
@@ -17,7 +23,7 @@
     return jnp.transpose(jnp.any(listed, axis=1))
 
 
-def body(ancestor_inverse, lower_panel, pivot_inverse, struct_list):
+def general_body(ancestor_inverse, lower_panel, pivot_inverse, struct_list):
     row_count = ancestor_inverse.shape[0] // B
     col_count = ancestor_inverse.shape[1] // B
     grid_rows = lax.axis_size("prow")
@@ -61,6 +67,322 @@
     return (off_inverse, diag_inverse)
 
 
+VM = pl.BlockSpec(memory_space=pltpu.VMEM)
+SM = pl.BlockSpec(memory_space=pltpu.SMEM)
+FINE = 64
+FILL = 0.9999
+
+
+def place():
+    p = lax.axis_index("prow")
+    q = lax.axis_index("pcol")
+    return p, q // 2, q % 2
+
+
+def call(kernel, outs, specs, scratch, flops, moved, name, room=2**23):
+    return pl.pallas_call(
+        kernel,
+        out_shape=outs,
+        in_specs=specs,
+        out_specs=jax.tree.map(lambda _: VM, outs),
+        scratch_shapes=scratch,
+        compiler_params=pltpu.CompilerParams(vmem_limit_bytes=room),
+        cost_estimate=pl.CostEstimate(flops=flops, bytes_accessed=moved, transcendentals=0),
+        name=name,
+    )
+
+
+def is_member(struct_ref, level, ancestor):
+    found = struct_ref[level, 0] == ancestor
+    for slot in range(1, struct_ref.shape[1]):
+        found = found | (struct_ref[level, slot] == ancestor)
+    return found
+
+
+def column_power(value):
+    top = jnp.maximum(jnp.max(jnp.abs(value), axis=0, keepdims=True), 2e-34)
+    power = jnp.floor(jnp.log2(top)) + 1.0
+    return jnp.where(top >= jnp.exp2(power), power + 1.0, power)
+
+
+def put_tail(ref, powers, rows):
+    row = lax.broadcasted_iota(jnp.int32, (TAIL, ref.shape[1]), 0)
+    tail = jnp.zeros((TAIL, ref.shape[1]), jnp.float32)
+    for block, power in enumerate(powers):
+        tail = jnp.where(row == block, power, tail)
+    ref[rows : rows + TAIL] = tail.astype(jnp.int32).astype(jnp.int16)
+
+
+def to_code(value):
+    return jnp.round(value).astype(jnp.int32).astype(jnp.int16)
+
+
+def from_code(code):
+    return code.astype(jnp.int32).astype(jnp.float32)
+
+
+def code_kernel(lower_ref, code_ref, own, to_x, to_y, to_both):
+    p, _, _ = place()
+    shard = lower_ref.shape[0]
+
+    def level(k):
+        return lower_ref[:, pl.ds(pl.multiple_of(k * B, B), B)]
+
+    for flip, out in enumerate((own, to_x, to_y, to_both)):
+        out[...] = level(p ^ flip)
+    powers = [[] for _ in range(shard // FINE)]
+    for slot, flip in enumerate((3, 1, 2, 0)):
+        value = level(p ^ flip).astype(jnp.float32)
+        for i in range(shard // FINE):
+            rows = slice(i * FINE, (i + 1) * FINE)
+            power = column_power(value[rows])
+            code_ref[rows, slot * B : (slot + 1) * B] = to_code(
+                value[rows] * jnp.exp2(15.0 - power)
+            )
+            powers[i].append(power)
+    put_tail(code_ref, [jnp.concatenate(power, axis=1) for power in powers], shard)
+
+
+def load_panel(code_ref, panel, struct_ref, slots):
+    p, _, _ = place()
+    span = code_ref.shape[0] // 8
+    shard = span - TAIL
+    blocks = panel.shape[0] // B
+    for at, (slot, flip) in enumerate(slots):
+        lanes = slice(slot * B, (slot + 1) * B)
+        for s in range(8):
+            last = s * span + shard
+            step = jnp.exp2(from_code(code_ref[last : last + TAIL, lanes]) - 15.0)
+            for i in range(shard // FINE):
+                first = s * span + i * FINE
+                value = from_code(code_ref[first : first + FINE, lanes]) * step[i : i + 1]
+                row = s * shard + i * FINE
+                panel[row : row + FINE, at * B : (at + 1) * B] = value.astype(jnp.bfloat16)
+        for block in range(blocks):
+
+            @pl.when(jnp.logical_not(is_member(struct_ref, p ^ flip, p * blocks + block)))
+            def _(block=block, at=at):
+                panel[block * B : (block + 1) * B, at * B : (at + 1) * B] = jnp.zeros(
+                    (B, B), jnp.bfloat16
+                )
+
+
+def sums_kernel(slots, struct_ref, a_ref, code_ref, *refs):
+    outs, panel = refs[:-1], refs[-1]
+    load_panel(code_ref, panel, struct_ref, slots)
+    blocks = a_ref.shape[0] // B
+    powers = [[] for _ in outs]
+    for b in range(blocks):
+        rows = slice(b * B, (b + 1) * B)
+        total = -jnp.dot(a_ref[rows], panel[...], preferred_element_type=jnp.float32)
+        for i, ref in enumerate(outs):
+            part = total[:, i * B : (i + 1) * B]
+            power = column_power(part)
+            ref[rows] = to_code(part * (jnp.exp2(15.0 - power) * FILL))
+            powers[i].append(power)
+    for ref, power in zip(outs, powers):
+        put_tail(ref, power, blocks * B)
+
+
+def own_kernel(struct_ref, a_ref, code_ref, own_ref, panel):
+    load_panel(code_ref, panel, struct_ref, ((3, 0),))
+    own_ref[...] = -jnp.dot(a_ref[...], panel[...], preferred_element_type=jnp.float32)
+
+
+def route_kernel(own, x, y, both, *outs):
+    p, z, _ = place()
+    for flip, out in enumerate(outs):
+        for turn, ref in enumerate((own, x, y, both)):
+
+            @pl.when((p ^ z) == (turn ^ flip))
+            def _(ref=ref, out=out):
+                out[...] = ref[...]
+
+
+def share_kernel(own, one, two, three, keep_ref, give_ref):
+    _, z, c = place()
+    shard = own.shape[0]
+    for flip, ref in enumerate((own, one, two, three)):
+        chip = z ^ flip
+        at = pl.multiple_of((chip % 2) * shard, 64)
+
+        @pl.when(chip // 2 == c)
+        def _(ref=ref, at=at):
+            keep_ref[pl.ds(at, shard)] = ref[...]
+
+        @pl.when(chip // 2 != c)
+        def _(ref=ref, at=at):
+            give_ref[pl.ds(at, shard)] = ref[...]
+
+
+def turn_kernel(keep, came, out_ref, lower):
+    _, _, c = place()
+    shard = keep.shape[0] // 2
+    for half in range(2):
+        for ref, core in ((keep, c), (came, 1 - c)):
+            at = pl.multiple_of((2 * half + core) * shard, FINE)
+            lower[pl.ds(at, shard)] = ref[half * shard : (half + 1) * shard]
+    out_ref[...] = jnp.transpose(lower[...])
+
+
+def last_kernel(
+    struct_ref, own_ref, came_d, came_x, came_y, lower, off_ref, diag_ref, both
+):
+    p, z, c = place()
+    blocks = off_ref.shape[0] // B
+    first = (2 * z + c) * blocks
+    steps = [
+        jnp.exp2(from_code(ref[blocks * B : blocks * B + TAIL]) - 15.0) * (1.0 / FILL)
+        for ref in (came_d, came_x, came_y)
+    ]
+    for b in range(blocks):
+        rows = slice(b * B, (b + 1) * B)
+        total = own_ref[rows]
+        for ref, step in zip((came_d, came_x, came_y), steps):
+            total = total + from_code(ref[rows]) * step[b : b + 1]
+        total = jnp.where(is_member(struct_ref, p, first + b), total, 0.0)
+        high = total.astype(jnp.bfloat16)
+        off_ref[rows] = high
+        both[rows, :B] = high
+        both[rows, B:] = (total - high.astype(jnp.float32)).astype(jnp.bfloat16)
+    diag = jnp.dot(lower[...], both[...], preferred_element_type=jnp.float32)
+    diag = diag[:, :B] + diag[:, B:]
+    piece = B // 8
+    for zz in range(4):
+        for cc in range(2):
+            slot = (cc ^ c) * 4 + (zz ^ z)
+            at = (2 * zz + cc) * piece
+            diag_ref[pl.ds(pl.multiple_of(slot * piece, piece), piece)] = diag[at : at + piece]
+
+
+def send(value, move):
+    found = []
+    for p in range(4):
+        for z in range(4):
+            for c in range(2):
+                to = move(p, z, c)
+                found.append((p * 8 + 2 * z + c, to[0] * 8 + 2 * to[1] + to[2]))
+    return lax.ppermute(value, AXES, found)
+
+
+def chip_swap(p, z, c):
+    return (p, z, 1 - c)
+
+
+def along(flip):
+    return lambda p, z, c: (p, z ^ flip, c)
+
+
+def across(flip):
+    return lambda p, z, c: (p ^ flip, z, c)
+
+
+def after(value, *earlier):
+    return lax.optimization_barrier((value, *earlier))[0]
+
+
+def line_body(ancestor_inverse, lower_panel, pivot_inverse, struct_list):
+    rows, depth = ancestor_inverse.shape
+    shard = lower_panel.shape[0]
+    bf16, f32, i16 = jnp.bfloat16, jnp.float32, jnp.int16
+    shape = jax.ShapeDtypeStruct
+    piece = shape((shard, B), bf16)
+    code, keep, to_x, to_y, to_both = call(
+        code_kernel,
+        (shape((shard + TAIL, NK * B), i16),) + (piece,) * 4,
+        [VM],
+        [],
+        8 * shard * NK * B,
+        4 * shard * NK * B,
+        "code",
+    )(lower_panel)
+    rows_x = send(to_x, across(1))
+    rows_y = send(to_y, across(2))
+    rows_both = send(to_both, across(3))
+    gathered = lax.all_gather(code, "pcol", axis=0, tiled=True)
+
+    coded = shape((rows + TAIL, B), i16)
+
+    def sums(slots, outs, name, *args):
+        return call(
+            functools.partial(sums_kernel, slots),
+            (coded,) * outs,
+            [SM, VM, VM],
+            [pltpu.VMEM((depth, outs * B), bf16)],
+            1,
+            1,
+            name,
+        )(*args)
+
+    (part_d,) = sums(((0, 3),), 1, "sums_d", struct_list, ancestor_inverse, gathered)
+    came_d = send(part_d, across(3))
+    part_x, part_y = sums(
+        ((1, 1), (2, 2)), 2, "sums_xy", after(struct_list, part_d), ancestor_inverse, gathered
+    )
+    came_x = send(part_x, across(1))
+    came_y = send(part_y, across(2))
+    def small(kernel, outs, name, *args):
+        return call(kernel, outs, [VM] * len(args), [], 1, 1, name, room=2**21)(*args)
+
+    stay, to_one, to_two, to_three = small(
+        route_kernel, (piece,) * 4, "route", keep, rows_x, rows_y, rows_both
+    )
+    from_one = send(to_one, along(1))
+    from_two = send(to_two, along(2))
+    from_three = send(to_three, along(3))
+    half_rows = shape((2 * shard, B), bf16)
+    keep, give = small(
+        share_kernel, (half_rows, half_rows), "share", stay, from_one, from_two, from_three
+    )
+    lower = call(
+        turn_kernel,
+        shape((B, rows), bf16),
+        [VM, VM],
+        [pltpu.VMEM((rows, B), bf16)],
+        1,
+        1,
+        "turn",
+    )(keep, send(give, chip_swap))
+    own = call(
+        own_kernel,
+        shape((rows, B), f32),
+        [SM, VM, VM],
+        [pltpu.VMEM((depth, B), bf16)],
+        1,
+        1,
+        "own",
+    )(after(struct_list, part_x), ancestor_inverse, gathered)
+    off_inverse, diag = call(
+        last_kernel,
+        (shape((rows, B), bf16), shape((B, B), f32)),
+        [SM] + [VM] * 5,
+        [pltpu.VMEM((rows, 2 * B), bf16)],
+        4 * rows * B * B,
+        8 * rows * B,
+        "last",
+    )(struct_list, own, came_d, came_x, came_y, lower)
+
+    half, part = B // 2, B // 8
+    total = diag[:half] + send(diag[half:], chip_swap)
+    near = [send(total[i * part : (i + 1) * part], along(i)) for i in (1, 2, 3)]
+    return off_inverse, pivot_inverse - (total[:part] + near[0] + near[1] + near[2])
+
+
+def body(ancestor_inverse, lower_panel, pivot_inverse, struct_list):
+    rows, depth = ancestor_inverse.shape
+    shard = lower_panel.shape[0]
+    line = (
+        lax.axis_size("prow") == 4
+        and lax.axis_size("pcol") == 8
+        and depth == 8 * shard
+        and depth == 2 * rows
+        and shard % 64 == 0
+        and shard <= B
+    )
+    plan = line_body if line else general_body
+    return plan(ancestor_inverse, lower_panel, pivot_inverse, struct_list)
+
+
 def solution(mesh):
     placed = (P("pcol", "prow"), P(("prow", "pcol"), None), P("pcol", "prow"), P())
     return jax.shard_map(

time: 208 us -> 75 us (0.36)
  waiting for transfers between devices: 164 us -> 12.4 us
  blocking collectives: 0 us -> 33.8 us
  starting transfers between devices: 0.16 us -> 17.5 us
  between operations: 13.9 us -> 0.76 us
  local copies, waits for them, and re-layouts: 12 us -> 1.17 us
  other arithmetic: 9.39 us -> 0.64 us
  Pallas kernels: 0 us -> 8.48 us
  matrix products: 7.96 us -> 0 us
    psum x1 -> x0, waiting for transfers between devices: 50.3 us -> none  [from_root(): return lax.psum(jnp.where(mine, value, jnp.zeros_like(value)), axis)]
    reduce_scatter x1 -> x0, waiting for transfers between devices: 47.3 us -> none  [body(): lax.psum_scatter(partial_value, 'prow', scatter_dimension=1, tiled=True)]
    all_gather x1 -> x0, waiting for transfers between devices: 38.4 us -> none  [body(): gathered = lax.all_gather(lower_panel, 'pcol', axis=0, tiled=True)]
    all_gather x0 -> x1, blocking collectives: none -> 33.8 us  [line_body(): gathered = lax.all_gather(code, 'pcol', axis=0, tiled=True)]
    unnamed x5 -> x0, waiting for transfers between devices: 28.4 us -> none
    ppermute x0 -> x14, starting transfers between devices: none -> 17.5 us  [send(): return lax.ppermute(value, AXES, found)]
    ppermute x0 -> x14, waiting for transfers between devices: none -> 12.4 us  [send(): return lax.ppermute(value, AXES, found)]
    pallas_call x0 -> x8, Pallas kernels: none -> 8.48 us  [the longest x2 4.49 us: sums(): call(functools.partial(sums_kernel, slots), (coded,) * outs, [SM, VM, VM]...]
  transfers between devices with their start and end apart: 4 -> 14, of which waited for: 4 -> 9; matrix products, arithmetic and copies ran while one was open for 8% -> 0% of each run, Pallas kernels for 0% -> 9%
where the time goes in v3:
time: 75 us; the launch traced here: 74.8 us
  blocking collectives  33.8 us (45%)
  starting transfers between devices  17.5 us (23%)
  waiting for transfers between devices  12.4 us (17%)
  Pallas kernels  8.48 us (11%)
  local copies, waits for them, and re-layouts  1.17 us (2%)
  between operations  0.76 us (1%)
    all_gather x1, blocking collectives, line_body(): gathered = lax.all_gather(code, 'pcol', axis=0, tiled=True)  33.8 us
    ppermute x14, starting transfers between devices, send(): return lax.ppermute(value, AXES, found)  17.5 us
    ppermute x14, waiting for transfers between devices, send(): return lax.ppermute(value, AXES, found)  12.4 us
    pallas_call x2, Pallas kernels, sums(): call(functools.partial(sums_kernel, slots), (coded,) * outs, [SM, VM, VM]...  4.49 us
    pallas_call x1, Pallas kernels, line_body(): call(last_kernel, (shape((rows, B), bf16), shape((B, B), f32)), [SM] + [V...  1.8 us
    pallas_call x1, Pallas kernels, line_body(): call(own_kernel, shape((rows, B), f32), [SM, VM, VM], [pltpu.VMEM((depth,...  1.65 us
  transfers between devices with their start and end apart: 14, of which 9 were waited for; matrix products, arithmetic and copies ran while one was open for 0% of the time, Pallas kernels for 9%

profile of v3, /device:TPU:0, one launch (start us, length us, event | category | flops | bytes accessed | tf_op | source)
XLA Modules:
  0.0 74.8 jit_solution(1005300148653368433)
XLA Ops:
  0.6 0.0 copy-start
  0.6 0.0 copy-start.1
  0.6 1.1 %copy-done.1 = bf16[192,1024]{1,0:T(8,128)(2,1)S(1)} copy-done((bf16[192,1024]{1,0:T(8,128)(2,1)S(1)}, bf16[192,1024]{1,0:T(8,128)(2,1)}, u32[]{:S(2)}) %copy-start.1) | copy-done | bytes 393240
  1.8 0.0 copy-start.2
  1.8 0.2 code.1
  2.0 3.0 %collective-permute-start.3 = (bf16[192,256]{1,0:T(8,128)(2,1)S(1)}, bf16[192,256]{1,0:T(8,128)(2,1)S(1)}, u32[]{:S(2)}, u32[]{:S(2)}) collective-permute-start(bf16[192,256]{1,0:T(8,128)(2,1)S(1)} %get-tuple-element.25), channel_id=1, source_target_pairs={{0,8},{1,9},{2,10},{3,11},{4,12},{5,13},{6,14},{7,15},{8,0},{9,1},... | collective-permute-start | bytes 294920 | tf_op jit(solution)/shard_map/ppermute | solution.py:265
  5.0 1.5 %collective-permute-start.4 = (bf16[192,256]{1,0:T(8,128)(2,1)S(1)}, bf16[192,256]{1,0:T(8,128)(2,1)S(1)}, u32[]{:S(2)}, u32[]{:S(2)}) collective-permute-start(bf16[192,256]{1,0:T(8,128)(2,1)S(1)} %get-tuple-element.26), channel_id=1, source_target_pairs={{0,16},{1,17},{2,18},{3,19},{4,20},{5,21},{6,22},{7,23},{8,24},{9,... | collective-permute-start | bytes 294920 | tf_op jit(solution)/shard_map/ppermute | solution.py:265
  6.5 0.0 collective-permute-start.5
  6.5 33.8 %all-gather.1.code_ref = s16[1664,1024]{1,0:T(8,128)(2,1)S(1)} all-gather(s16[208,1024]{1,0:T(8,128)(2,1)S(1)} %get-tuple-element.19), channel_id=1, replica_groups=mesh['prow'=4,'pcol'=8] {'pcol'}, dimensions={0}, use_global_device_ids=true | all-gather | bytes 3833856 | tf_op jit(solution)/shard_map/all_gather | solution.py:302
  40.4 0.0 copy-done
  40.4 0.0 copy-done.2
  40.4 1.8 %sums_d.1 = s16[784,256]{1,0:T(8,128)(2,1)S(1)} custom-call(s32[4,12]{1,0:T(4,128)S(1)} %copy-done.2, bf16[768,1536]{1,0:T(8,128)(2,1)S(1)} %copy-done, s16[1664,1024]{1,0:T(8,128)(2,1)S(1)} %all-gather.1.code_ref), custom_call_target="tpu_custom_call" | custom-call | flops 1 | bytes 1 | tf_op jit(solution)/shard_map/sums_d/pallas_call | solution.py:307
  42.1 2.5 %collective-permute-start = (s16[784,256]{1,0:T(8,128)(2,1)S(1)}, s16[784,256]{1,0:T(8,128)(2,1)S(1)}, u32[]{:S(2)}, u32[]{:S(2)}) collective-permute-start(s16[784,256]{1,0:T(8,128)(2,1)S(1)} %sums_d.1), channel_id=1, source_target_pairs={{0,24},{1,25},{2,26},{3,27},{4,28},{5,29},{6,30},{7,31},{8,16},{9,... | collective-permute-start | bytes 1204232 | tf_op jit(solution)/shard_map/ppermute | solution.py:265
  44.6 2.7 %sums_xy.1 = (s16[784,256]{1,0:T(8,128)(2,1)S(1)}, s16[784,256]{1,0:T(8,128)(2,1)S(1)}) custom-call(s32[4,12]{1,0:T(4,128)S(1)} %copy-done.2, bf16[768,1536]{1,0:T(8,128)(2,1)S(1)} %copy-done, s16[1664,1024]{1,0:T(8,128)(2,1)S(1)} %all-gather.1.code_ref), custom_call_target="tpu_custom_call" | custom-call | flops 1 | bytes 1 | tf_op jit(solution)/shard_map/sums_xy/pallas_call | solution.py:307
  47.4 0.6 collective-permute-start.2
  48.0 0.0 collective-permute-done.3.x
  48.0 0.6 collective-permute-start.1
  48.5 0.0 collective-permute-done.4.y
  48.5 0.0 collective-permute-done.5.both
  48.5 0.1 route.1
  48.6 0.3 collective-permute-start.6
  48.9 2.9 %collective-permute-start.7 = (bf16[192,256]{1,0:T(8,128)(2,1)S(1)}, bf16[192,256]{1,0:T(8,128)(2,1)S(1)}, u32[]{:S(2)}, u32[]{:S(2)}) collective-permute-start(bf16[192,256]{1,0:T(8,128)(2,1)S(1)} %get-tuple-element.30), channel_id=1, source_target_pairs={{0,4},{1,5},{2,6},{3,7},{4,0},{5,1},{6,2},{7,3},{8,12},{9,13},{10,... | collective-permute-start | bytes 294920 | tf_op jit(solution)/shard_map/ppermute | solution.py:265
  51.8 2.7 %collective-permute-done.6.one = bf16[192,256]{1,0:T(8,128)(2,1)S(1)} collective-permute-done((bf16[192,256]{1,0:T(8,128)(2,1)S(1)}, bf16[192,256]{1,0:T(8,128)(2,1)S(1)}, u32[]{:S(2)}, u32[]{:S(2)}) %collective-permute-start.6) | collective-permute-done | bytes 98336 | tf_op jit(solution)/shard_map/ppermute | solution.py:265
  54.5 2.3 %collective-permute-start.8 = (bf16[192,256]{1,0:T(8,128)(2,1)S(1)}, bf16[192,256]{1,0:T(8,128)(2,1)S(1)}, u32[]{:S(2)}, u32[]{:S(2)}) collective-permute-start(bf16[192,256]{1,0:T(8,128)(2,1)S(1)} %get-tuple-element.31), channel_id=1, source_target_pairs={{0,6},{1,7},{2,4},{3,5},{4,2},{5,3},{6,0},{7,1},{8,14},{9,15},{10,... | collective-permute-start | bytes 294920 | tf_op jit(solution)/shard_map/ppermute | solution.py:265
  56.8 1.2 %collective-permute-done.7.two = bf16[192,256]{1,0:T(8,128)(2,1)S(1)} collective-permute-done((bf16[192,256]{1,0:T(8,128)(2,1)S(1)}, bf16[192,256]{1,0:T(8,128)(2,1)S(1)}, u32[]{:S(2)}, u32[]{:S(2)}) %collective-permute-start.7) | collective-permute-done | bytes 98336 | tf_op jit(solution)/shard_map/ppermute | solution.py:265
  57.9 3.0 %collective-permute-done.8.three = bf16[192,256]{1,0:T(8,128)(2,1)S(1)} collective-permute-done((bf16[192,256]{1,0:T(8,128)(2,1)S(1)}, bf16[192,256]{1,0:T(8,128)(2,1)S(1)}, u32[]{:S(2)}, u32[]{:S(2)}) %collective-permute-start.8) | collective-permute-done | bytes 98336 | tf_op jit(solution)/shard_map/ppermute | solution.py:265
  60.9 0.1 share.1
  61.0 0.1 collective-permute-start.9
  61.1 1.6 %own.1.own_ref = f32[768,256]{1,0:T(8,128)S(1)} custom-call(s32[4,12]{1,0:T(4,128)S(1)} %copy-done.2, bf16[768,1536]{1,0:T(8,128)(2,1)S(1)} %copy-done, s16[1664,1024]{1,0:T(8,128)(2,1)S(1)} %all-gather.1.code_ref), custom_call_target="tpu_custom_call" | custom-call | flops 1 | bytes 1 | tf_op jit(solution)/shard_map/own/pallas_call | solution.py:346
  62.7 0.0 copy-start.3
  62.7 0.0 collective-permute-done.9.came
  62.8 0.2 turn.1.lower
  63.0 0.0 collective-permute-done.came_d
  63.0 0.3 collective-permute-done.2.came_y
  63.3 0.1 collective-permute-done.1.came_x
  63.3 1.8 %last.1 = (bf16[768,256]{1,0:T(8,128)(2,1)}, f32[256,256]{1,0:T(8,128)S(1)}) custom-call(s32[4,12]{1,0:T(4,128)S(1)} %copy-done.2, f32[768,256]{1,0:T(8,128)S(1)} %own.1.own_ref, s16[784,256]{1,0:T(8,128)(2,1)S(1)} %collective-permute-done.came_d, s16[784,256]{1,0:T(8,128)(2,1)S(1)} %collective-permute-done.1.came_x, ...), custom_call_target="tpu_custom_call" | custom-call | flops 201326592 | bytes 1572864 | tf_op jit(solution)/shard_map/last/pallas_call | solution.py:355
  65.2 0.2 collective-permute-start.10
  65.4 1.2 %collective-permute-done.10 = f32[128,256]{1,0:T(8,128)S(1)} collective-permute-done((f32[128,256]{1,0:T(8,128)S(1)}, f32[128,256]{1,0:T(8,128)S(1)}, u32[]{:S(2)}, u32[]{:S(2)}) %collective-permute-start.10) | collective-permute-done | bytes 131104 | tf_op jit(solution)/shard_map/ppermute | solution.py:265
  66.6 0.3 collective-permute-start.11
  66.9 2.4 %collective-permute-start.13 = (f32[32,256]{1,0:T(8,128)S(1)}, f32[32,256]{1,0:T(8,128)S(1)}, u32[]{:S(2)}, u32[]{:S(2)}) collective-permute-start(f32[32,256]{1,0:T(8,128)S(1)} %get-tuple-element.37), channel_id=1, source_target_pairs={{0,6},{1,7},{2,4},{3,5},{4,2},{5,3},{6,0},{7,1},{8,14},{9,15},{10,... | collective-permute-start | bytes 98312 | tf_op jit(solution)/shard_map/ppermute | solution.py:265
  69.4 0.8 %collective-permute-start.12 = (f32[32,256]{1,0:T(8,128)S(1)}, f32[32,256]{1,0:T(8,128)S(1)}, u32[]{:S(2)}, u32[]{:S(2)}) collective-permute-start(f32[32,256]{1,0:T(8,128)S(1)} %get-tuple-element.38), channel_id=1, source_target_pairs={{0,4},{1,5},{2,6},{3,7},{4,0},{5,1},{6,2},{7,3},{8,12},{9,13},{10,... | collective-permute-start | bytes 98312 | tf_op jit(solution)/shard_map/ppermute | solution.py:265
  70.2 0.4 collective-permute-done.11
  70.6 2.0 %collective-permute-done.13 = f32[32,256]{1,0:T(8,128)S(1)} collective-permute-done((f32[32,256]{1,0:T(8,128)S(1)}, f32[32,256]{1,0:T(8,128)S(1)}, u32[]{:S(2)}, u32[]{:S(2)}) %collective-permute-start.13) | collective-permute-done | bytes 32800 | tf_op jit(solution)/shard_map/ppermute | solution.py:265
  72.6 1.5 %collective-permute-done.12 = f32[32,256]{1,0:T(8,128)S(1)} collective-permute-done((f32[32,256]{1,0:T(8,128)S(1)}, f32[32,256]{1,0:T(8,128)S(1)}, u32[]{:S(2)}, u32[]{:S(2)}) %collective-permute-start.12) | collective-permute-done | bytes 32800 | tf_op jit(solution)/shard_map/ppermute | solution.py:265
  74.2 0.0 copy-done.3
  74.2 0.6 fusion.2
  (3 shorter events, 0.0 us)
Async XLA Ops:
  0.6 39.7 %copy-start = (bf16[768,1536]{1,0:T(8,128)(2,1)S(1)}, bf16[768,1536]{1,0:T(8,128)(2,1)}, u32[]{:S(2)}) copy-start(bf16[768,1536]{1,0:T(8,128)(2,1)} %a_ref.5) | copy-start | bytes 7077892
  0.6 1.1 %copy-start.1 = (bf16[192,1024]{1,0:T(8,128)(2,1)S(1)}, bf16[192,1024]{1,0:T(8,128)(2,1)}, u32[]{:S(2)}) copy-start(bf16[192,1024]{1,0:T(8,128)(2,1)} %lower_ref.1) | copy-start | bytes 1179652
  1.8 38.6 %copy-start.2 = (s32[4,12]{1,0:T(4,128)S(1)}, s32[4,12]{1,0:T(4,128)}, u32[]{:S(2)}) copy-start(s32[4,12]{1,0:T(4,128)} %struct_ref.5) | copy-start | bytes 580
  2.0 46.0 %collective-permute-start.3 = (bf16[192,256]{1,0:T(8,128)(2,1)S(1)}, bf16[192,256]{1,0:T(8,128)(2,1)S(1)}, u32[]{:S(2)}, u32[]{:S(2)}) collective-permute-start(bf16[192,256]{1,0:T(8,128)(2,1)S(1)} %get-tuple-element.25), channel_id=1, source_target_pairs={{0,8},{1,9},{2,10},{3,11},{4,12},{5,13},{6,14},{7,15},{8,0},{9,1},... | collective-permute-start | bytes 294920 | tf_op jit(solution)/shard_map/ppermute | solution.py:265
  5.0 43.5 %collective-permute-start.4 = (bf16[192,256]{1,0:T(8,128)(2,1)S(1)}, bf16[192,256]{1,0:T(8,128)(2,1)S(1)}, u32[]{:S(2)}, u32[]{:S(2)}) collective-permute-start(bf16[192,256]{1,0:T(8,128)(2,1)S(1)} %get-tuple-element.26), channel_id=1, source_target_pairs={{0,16},{1,17},{2,18},{3,19},{4,20},{5,21},{6,22},{7,23},{8,24},{9,... | collective-permute-start | bytes 294920 | tf_op jit(solution)/shard_map/ppermute | solution.py:265
  6.5 42.0 %collective-permute-start.5 = (bf16[192,256]{1,0:T(8,128)(2,1)S(1)}, bf16[192,256]{1,0:T(8,128)(2,1)S(1)}, u32[]{:S(2)}, u32[]{:S(2)}) collective-permute-start(bf16[192,256]{1,0:T(8,128)(2,1)S(1)} %get-tuple-element.27), channel_id=1, source_target_pairs={{0,24},{1,25},{2,26},{3,27},{4,28},{5,29},{6,30},{7,31},{8,16},{9,... | collective-permute-start | bytes 294920 | tf_op jit(solution)/shard_map/ppermute | solution.py:265
  42.1 20.8 %collective-permute-start = (s16[784,256]{1,0:T(8,128)(2,1)S(1)}, s16[784,256]{1,0:T(8,128)(2,1)S(1)}, u32[]{:S(2)}, u32[]{:S(2)}) collective-permute-start(s16[784,256]{1,0:T(8,128)(2,1)S(1)} %sums_d.1), channel_id=1, source_target_pairs={{0,24},{1,25},{2,26},{3,27},{4,28},{5,29},{6,30},{7,31},{8,16},{9,... | collective-permute-start | bytes 1204232 | tf_op jit(solution)/shard_map/ppermute | solution.py:265
  47.4 15.9 %collective-permute-start.2 = (s16[784,256]{1,0:T(8,128)(2,1)S(1)}, s16[784,256]{1,0:T(8,128)(2,1)S(1)}, u32[]{:S(2)}, u32[]{:S(2)}) collective-permute-start(s16[784,256]{1,0:T(8,128)(2,1)S(1)} %get-tuple-element.23), channel_id=1, source_target_pairs={{0,16},{1,17},{2,18},{3,19},{4,20},{5,21},{6,22},{7,23},{8,24},{9,... | collective-permute-start | bytes 1204232 | tf_op jit(solution)/shard_map/ppermute | solution.py:265
  48.0 15.4 %collective-permute-start.1 = (s16[784,256]{1,0:T(8,128)(2,1)S(1)}, s16[784,256]{1,0:T(8,128)(2,1)S(1)}, u32[]{:S(2)}, u32[]{:S(2)}) collective-permute-start(s16[784,256]{1,0:T(8,128)(2,1)S(1)} %get-tuple-element.21), channel_id=1, source_target_pairs={{0,8},{1,9},{2,10},{3,11},{4,12},{5,13},{6,14},{7,15},{8,0},{9,1},... | collective-permute-start | bytes 1204232 | tf_op jit(solution)/shard_map/ppermute | solution.py:265
  48.6 5.9 %collective-permute-start.6 = (bf16[192,256]{1,0:T(8,128)(2,1)S(1)}, bf16[192,256]{1,0:T(8,128)(2,1)S(1)}, u32[]{:S(2)}, u32[]{:S(2)}) collective-permute-start(bf16[192,256]{1,0:T(8,128)(2,1)S(1)} %get-tuple-element.29), channel_id=1, source_target_pairs={{0,2},{1,3},{2,0},{3,1},{4,6},{5,7},{6,4},{7,5},{8,10},{9,11},{10,... | collective-permute-start | bytes 294920 | tf_op jit(solution)/shard_map/ppermute | solution.py:265
  48.9 9.0 %collective-permute-start.7 = (bf16[192,256]{1,0:T(8,128)(2,1)S(1)}, bf16[192,256]{1,0:T(8,128)(2,1)S(1)}, u32[]{:S(2)}, u32[]{:S(2)}) collective-permute-start(bf16[192,256]{1,0:T(8,128)(2,1)S(1)} %get-tuple-element.30), channel_id=1, source_target_pairs={{0,4},{1,5},{2,6},{3,7},{4,0},{5,1},{6,2},{7,3},{8,12},{9,13},{10,... | collective-permute-start | bytes 294920 | tf_op jit(solution)/shard_map/ppermute | solution.py:265
  54.5 6.4 %collective-permute-start.8 = (bf16[192,256]{1,0:T(8,128)(2,1)S(1)}, bf16[192,256]{1,0:T(8,128)(2,1)S(1)}, u32[]{:S(2)}, u32[]{:S(2)}) collective-permute-start(bf16[192,256]{1,0:T(8,128)(2,1)S(1)} %get-tuple-element.31), channel_id=1, source_target_pairs={{0,6},{1,7},{2,4},{3,5},{4,2},{5,3},{6,0},{7,1},{8,14},{9,15},{10,... | collective-permute-start | bytes 294920 | tf_op jit(solution)/shard_map/ppermute | solution.py:265
  61.0 1.7 %collective-permute-start.9 = (bf16[384,256]{1,0:T(8,128)(2,1)S(1)}, bf16[384,256]{1,0:T(8,128)(2,1)S(1)}, u32[]{:S(2)}, u32[]{:S(2)}) collective-permute-start(bf16[384,256]{1,0:T(8,128)(2,1)S(1)} %get-tuple-element.33), channel_id=1, source_target_pairs={{0,1},{1,0},{2,3},{3,2},{4,5},{5,4},{6,7},{7,6},{8,9},{9,8},{10,11... | collective-permute-start | bytes 589832 | tf_op jit(solution)/shard_map/ppermute | solution.py:265
  62.7 11.4 %copy-start.3 = (f32[32,256]{1,0:T(8,128)S(1)}, f32[32,256]{1,0:T(8,128)}, u32[]{:S(2)}) copy-start(f32[32,256]{1,0:T(8,128)} %param.6) | copy-start | bytes 98308
  65.2 1.4 %collective-permute-start.10 = (f32[128,256]{1,0:T(8,128)S(1)}, f32[128,256]{1,0:T(8,128)S(1)}, u32[]{:S(2)}, u32[]{:S(2)}) collective-permute-start(f32[128,256]{1,0:T(8,128)S(1)} %slice.19), channel_id=1, source_target_pairs={{0,1},{1,0},{2,3},{3,2},{4,5},{5,4},{6,7},{7,6},{8,9},{9,8},{10,11... | collective-permute-start | bytes 393224 | tf_op jit(solution)/shard_map/ppermute | solution.py:265
  66.6 4.0 %collective-permute-start.11 = (f32[32,256]{1,0:T(8,128)S(1)}, f32[32,256]{1,0:T(8,128)S(1)}, u32[]{:S(2)}, u32[]{:S(2)}) collective-permute-start(f32[32,256]{1,0:T(8,128)S(1)} %get-tuple-element.36), channel_id=1, source_target_pairs={{0,2},{1,3},{2,0},{3,1},{4,6},{5,7},{6,4},{7,5},{8,10},{9,11},{10,... | collective-permute-start | bytes 98312 | tf_op jit(solution)/shard_map/ppermute | solution.py:265
  66.9 5.7 %collective-permute-start.13 = (f32[32,256]{1,0:T(8,128)S(1)}, f32[32,256]{1,0:T(8,128)S(1)}, u32[]{:S(2)}, u32[]{:S(2)}) collective-permute-start(f32[32,256]{1,0:T(8,128)S(1)} %get-tuple-element.37), channel_id=1, source_target_pairs={{0,6},{1,7},{2,4},{3,5},{4,2},{5,3},{6,0},{7,1},{8,14},{9,15},{10,... | collective-permute-start | bytes 98312 | tf_op jit(solution)/shard_map/ppermute | solution.py:265
  69.4 4.8 %collective-permute-start.12 = (f32[32,256]{1,0:T(8,128)S(1)}, f32[32,256]{1,0:T(8,128)S(1)}, u32[]{:S(2)}, u32[]{:S(2)}) collective-permute-start(f32[32,256]{1,0:T(8,128)S(1)} %get-tuple-element.38), channel_id=1, source_target_pairs={{0,4},{1,5},{2,6},{3,7},{4,0},{5,1},{6,2},{7,3},{8,12},{9,13},{10,... | collective-permute-start | bytes 98312 | tf_op jit(solution)/shard_map/ppermute | solution.py:265

commit v4 on v3

--- a/solution.py
+++ b/solution.py
@@ -70,6 +70,7 @@
 VM = pl.BlockSpec(memory_space=pltpu.VMEM)
 SM = pl.BlockSpec(memory_space=pltpu.SMEM)
 FINE = 64
+TINY = 2.0**-100
 FILL = 0.9999
 
 
@@ -123,48 +124,42 @@
 
 def code_kernel(lower_ref, code_ref, own, to_x, to_y, to_both):
     p, _, _ = place()
-    shard = lower_ref.shape[0]
 
     def level(k):
         return lower_ref[:, pl.ds(pl.multiple_of(k * B, B), B)]
 
     for flip, out in enumerate((own, to_x, to_y, to_both)):
         out[...] = level(p ^ flip)
-    powers = [[] for _ in range(shard // FINE)]
     for slot, flip in enumerate((3, 1, 2, 0)):
         value = level(p ^ flip).astype(jnp.float32)
-        for i in range(shard // FINE):
-            rows = slice(i * FINE, (i + 1) * FINE)
-            power = column_power(value[rows])
-            code_ref[rows, slot * B : (slot + 1) * B] = to_code(
-                value[rows] * jnp.exp2(15.0 - power)
-            )
-            powers[i].append(power)
-    put_tail(code_ref, [jnp.concatenate(power, axis=1) for power in powers], shard)
+        size = jnp.abs(value)
+        power = jnp.floor(jnp.log2(jnp.maximum(size, TINY)))
+        code = jnp.round(size * jnp.exp2(7.0 - power)) + (power + 126.0) * 128.0
+        code = jnp.where(size < TINY, 0.0, jnp.where(value < 0.0, -code, code))
+        code_ref[:, slot * B : (slot + 1) * B] = code.astype(jnp.int32).astype(jnp.int16)
 
 
 def load_panel(code_ref, panel, struct_ref, slots):
     p, _, _ = place()
-    span = code_ref.shape[0] // 8
-    shard = span - TAIL
     blocks = panel.shape[0] // B
     for at, (slot, flip) in enumerate(slots):
-        lanes = slice(slot * B, (slot + 1) * B)
-        for s in range(8):
-            last = s * span + shard
-            step = jnp.exp2(from_code(code_ref[last : last + TAIL, lanes]) - 15.0)
-            for i in range(shard // FINE):
-                first = s * span + i * FINE
-                value = from_code(code_ref[first : first + FINE, lanes]) * step[i : i + 1]
-                row = s * shard + i * FINE
-                panel[row : row + FINE, at * B : (at + 1) * B] = value.astype(jnp.bfloat16)
         for block in range(blocks):
-
-            @pl.when(jnp.logical_not(is_member(struct_ref, p ^ flip, p * blocks + block)))
-            def _(block=block, at=at):
-                panel[block * B : (block + 1) * B, at * B : (at + 1) * B] = jnp.zeros(
-                    (B, B), jnp.bfloat16
+            rows = slice(block * B, (block + 1) * B)
+            listed = is_member(struct_ref, p ^ flip, p * blocks + block)
+
+            @pl.when(listed)
+            def _(rows=rows, at=at, slot=slot):
+                code = code_ref[rows, slot * B : (slot + 1) * B].astype(jnp.int32)
+                size = jnp.abs(code)
+                power = jnp.exp2(((size >> 7) - 134).astype(jnp.float32))
+                value = ((size & 127) + 128).astype(jnp.float32) * power
+                panel[rows, at * B : (at + 1) * B] = jnp.where(code < 0, -value, value).astype(
+                    jnp.bfloat16
                 )
+
+            @pl.when(jnp.logical_not(listed))
+            def _(rows=rows, at=at):
+                panel[rows, at * B : (at + 1) * B] = jnp.zeros((B, B), jnp.bfloat16)
 
 
 def sums_kernel(slots, struct_ref, a_ref, code_ref, *refs):
@@ -184,9 +179,19 @@
         put_tail(ref, power, blocks * B)
 
 
-def own_kernel(struct_ref, a_ref, code_ref, own_ref, panel):
+def came_step(ref, blocks):
+    return jnp.exp2(from_code(ref[blocks * B : blocks * B + TAIL]) - 15.0) * (1.0 / FILL)
+
+
+def own_kernel(struct_ref, a_ref, code_ref, came_d, own_ref, panel):
     load_panel(code_ref, panel, struct_ref, ((3, 0),))
-    own_ref[...] = -jnp.dot(a_ref[...], panel[...], preferred_element_type=jnp.float32)
+    blocks = own_ref.shape[0] // B
+    step = came_step(came_d, blocks)
+    for b in range(blocks):
+        rows = slice(b * B, (b + 1) * B)
+        own_ref[rows] = from_code(came_d[rows]) * step[b : b + 1] - jnp.dot(
+            a_ref[rows], panel[...], preferred_element_type=jnp.float32
+        )
 
 
 def route_kernel(own, x, y, both, *outs):
@@ -226,19 +231,16 @@
 
 
 def last_kernel(
-    struct_ref, own_ref, came_d, came_x, came_y, lower, off_ref, diag_ref, both
+    struct_ref, own_ref, came_x, came_y, lower, off_ref, diag_ref, both
 ):
     p, z, c = place()
     blocks = off_ref.shape[0] // B
     first = (2 * z + c) * blocks
-    steps = [
-        jnp.exp2(from_code(ref[blocks * B : blocks * B + TAIL]) - 15.0) * (1.0 / FILL)
-        for ref in (came_d, came_x, came_y)
-    ]
+    steps = [came_step(ref, blocks) for ref in (came_x, came_y)]
     for b in range(blocks):
         rows = slice(b * B, (b + 1) * B)
         total = own_ref[rows]
-        for ref, step in zip((came_d, came_x, came_y), steps):
+        for ref, step in zip((came_x, came_y), steps):
             total = total + from_code(ref[rows]) * step[b : b + 1]
         total = jnp.where(is_member(struct_ref, p, first + b), total, 0.0)
         high = total.astype(jnp.bfloat16)
@@ -289,7 +291,7 @@
     piece = shape((shard, B), bf16)
     code, keep, to_x, to_y, to_both = call(
         code_kernel,
-        (shape((shard + TAIL, NK * B), i16),) + (piece,) * 4,
+        (shape((shard, NK * B), i16),) + (piece,) * 4,
         [VM],
         [],
         8 * shard * NK * B,
@@ -321,15 +323,24 @@
     )
     came_x = send(part_x, across(1))
     came_y = send(part_y, across(2))
-    def small(kernel, outs, name, *args):
-        return call(kernel, outs, [VM] * len(args), [], 1, 1, name, room=2**21)(*args)
+    def small(kernel, outs, name, *args, flops=1):
+        return call(kernel, outs, [VM] * len(args), [], flops, 1, name, room=2**21)(*args)
 
     stay, to_one, to_two, to_three = small(
-        route_kernel, (piece,) * 4, "route", keep, rows_x, rows_y, rows_both
+        route_kernel, (piece,) * 4, "route", keep, rows_x, rows_y, rows_both, flops=1
     )
     from_one = send(to_one, along(1))
     from_two = send(to_two, along(2))
-    from_three = send(to_three, along(3))
+    from_three = send(after(to_three, from_one), along(3))
+    own = call(
+        own_kernel,
+        shape((rows, B), f32),
+        [SM, VM, VM, VM],
+        [pltpu.VMEM((depth, B), bf16)],
+        1,
+        1,
+        "own",
+    )(struct_list, ancestor_inverse, gathered, came_d)
     half_rows = shape((2 * shard, B), bf16)
     keep, give = small(
         share_kernel, (half_rows, half_rows), "share", stay, from_one, from_two, from_three
@@ -343,24 +354,15 @@
         1,
         "turn",
     )(keep, send(give, chip_swap))
-    own = call(
-        own_kernel,
-        shape((rows, B), f32),
-        [SM, VM, VM],
-        [pltpu.VMEM((depth, B), bf16)],
-        1,
-        1,
-        "own",
-    )(after(struct_list, part_x), ancestor_inverse, gathered)
     off_inverse, diag = call(
         last_kernel,
         (shape((rows, B), bf16), shape((B, B), f32)),
-        [SM] + [VM] * 5,
+        [SM] + [VM] * 4,
         [pltpu.VMEM((rows, 2 * B), bf16)],
         4 * rows * B * B,
         8 * rows * B,
         "last",
-    )(struct_list, own, came_d, came_x, came_y, lower)
+    )(struct_list, own, came_x, came_y, lower)
 
     half, part = B // 2, B // 8
     total = diag[:half] + send(diag[half:], chip_swap)

time: 75 us -> 73.5 us (0.980)
  blocking collectives: 33.8 us -> 31.8 us
  Pallas kernels: 8.48 us -> 9.75 us
    all_gather x1, blocking collectives: 33.8 us -> 31.8 us  [line_body(): gathered = lax.all_gather(code, 'pcol', axis=0, tiled=True)]
    pallas_call x4, Pallas kernels: 1.99 us -> 2.92 us  [the longest x1 2.24 us: line_body(): call(own_kernel, shape((rows, B), f32), [SM, VM, VM, VM], [pltpu.VMEM((de...]
  transfers between devices with their start and end apart: 14 -> 14, of which waited for: 9 -> 7; matrix products, arithmetic and copies ran while one was open for 0% -> 0% of each run, Pallas kernels for 9% -> 10%
where the time goes in v4:
time: 73.5 us; the launch traced here: 73.3 us
  blocking collectives  31.8 us (43%)
  starting transfers between devices  17.2 us (23%)
  waiting for transfers between devices  12 us (16%)
  Pallas kernels  9.75 us (13%)
  local copies, waits for them, and re-layouts  1.17 us (2%)
  between operations  0.78 us (1%)
    all_gather x1, blocking collectives, line_body(): gathered = lax.all_gather(code, 'pcol', axis=0, tiled=True)  31.8 us
    ppermute x14, starting transfers between devices, send(): return lax.ppermute(value, AXES, found)  17.2 us
    ppermute x14, waiting for transfers between devices, send(): return lax.ppermute(value, AXES, found)  12 us
    pallas_call x2, Pallas kernels, sums(): call(functools.partial(sums_kernel, slots), (coded,) * outs, [SM, VM, VM]...  4.92 us
    pallas_call x1, Pallas kernels, line_body(): call(own_kernel, shape((rows, B), f32), [SM, VM, VM, VM], [pltpu.VMEM((de...  2.24 us
    pallas_call x1, Pallas kernels, line_body(): call(last_kernel, (shape((rows, B), bf16), shape((B, B), f32)), [SM] + [V...  1.71 us
  transfers between devices with their start and end apart: 14, of which 7 were waited for; matrix products, arithmetic and copies ran while one was open for 0% of the time, Pallas kernels for 10%

profile of v4, /device:TPU:0, one launch (start us, length us, event | category | flops | bytes accessed | tf_op | source)
XLA Modules:
  0.0 73.3 jit_solution(9067893490023689449)
XLA Ops:
  0.6 0.0 copy-start
  0.6 0.0 copy-start.1
  0.6 1.1 %copy-done.1 = bf16[192,1024]{1,0:T(8,128)(2,1)S(1)} copy-done((bf16[192,1024]{1,0:T(8,128)(2,1)S(1)}, bf16[192,1024]{1,0:T(8,128)(2,1)}, u32[]{:S(2)}) %copy-start.1) | copy-done | bytes 393240
  1.8 0.0 copy-start.2
  1.8 0.5 code.1
  2.3 3.0 %collective-permute-start.3 = (bf16[192,256]{1,0:T(8,128)(2,1)S(1)}, bf16[192,256]{1,0:T(8,128)(2,1)S(1)}, u32[]{:S(2)}, u32[]{:S(2)}) collective-permute-start(bf16[192,256]{1,0:T(8,128)(2,1)S(1)} %get-tuple-element.24), channel_id=1, source_target_pairs={{0,8},{1,9},{2,10},{3,11},{4,12},{5,13},{6,14},{7,15},{8,0},{9,1},... | collective-permute-start | bytes 294920 | tf_op jit(solution)/shard_map/ppermute | solution.py:267
  5.3 1.5 %collective-permute-start.4 = (bf16[192,256]{1,0:T(8,128)(2,1)S(1)}, bf16[192,256]{1,0:T(8,128)(2,1)S(1)}, u32[]{:S(2)}, u32[]{:S(2)}) collective-permute-start(bf16[192,256]{1,0:T(8,128)(2,1)S(1)} %get-tuple-element.25), channel_id=1, source_target_pairs={{0,16},{1,17},{2,18},{3,19},{4,20},{5,21},{6,22},{7,23},{8,24},{9,... | collective-permute-start | bytes 294920 | tf_op jit(solution)/shard_map/ppermute | solution.py:267
  6.9 0.0 collective-permute-start.5
  6.9 31.8 %all-gather.1.code_ref = s16[1536,1024]{1,0:T(8,128)(2,1)S(1)} all-gather(s16[192,1024]{1,0:T(8,128)(2,1)S(1)} %get-tuple-element.19), channel_id=1, replica_groups=mesh['prow'=4,'pcol'=8] {'pcol'}, dimensions={0}, use_global_device_ids=true | all-gather | bytes 3538944 | tf_op jit(solution)/shard_map/all_gather | solution.py:304
  38.6 0.0 copy-done
  38.6 0.0 copy-done.2
  38.6 2.0 %sums_d.1 = s16[784,256]{1,0:T(8,128)(2,1)S(1)} custom-call(s32[4,12]{1,0:T(4,128)S(1)} %copy-done.2, bf16[768,1536]{1,0:T(8,128)(2,1)S(1)} %copy-done, s16[1536,1024]{1,0:T(8,128)(2,1)S(1)} %all-gather.1.code_ref), custom_call_target="tpu_custom_call" | custom-call | flops 1 | bytes 1 | tf_op jit(solution)/shard_map/sums_d/pallas_call | solution.py:309
  40.6 2.5 %collective-permute-start = (s16[784,256]{1,0:T(8,128)(2,1)S(1)}, s16[784,256]{1,0:T(8,128)(2,1)S(1)}, u32[]{:S(2)}, u32[]{:S(2)}) collective-permute-start(s16[784,256]{1,0:T(8,128)(2,1)S(1)} %sums_d.1), channel_id=1, source_target_pairs={{0,24},{1,25},{2,26},{3,27},{4,28},{5,29},{6,30},{7,31},{8,16},{9,... | collective-permute-start | bytes 1204232 | tf_op jit(solution)/shard_map/ppermute | solution.py:267
  43.2 2.9 %sums_xy.1 = (s16[784,256]{1,0:T(8,128)(2,1)S(1)}, s16[784,256]{1,0:T(8,128)(2,1)S(1)}) custom-call(s32[4,12]{1,0:T(4,128)S(1)} %copy-done.2, bf16[768,1536]{1,0:T(8,128)(2,1)S(1)} %copy-done, s16[1536,1024]{1,0:T(8,128)(2,1)S(1)} %all-gather.1.code_ref), custom_call_target="tpu_custom_call" | custom-call | flops 1 | bytes 1 | tf_op jit(solution)/shard_map/sums_xy/pallas_call | solution.py:309
  46.1 0.2 collective-permute-start.1
  46.4 0.0 collective-permute-done.3.x
  46.4 0.4 collective-permute-start.2
  46.8 0.0 collective-permute-done.4.y
  46.8 0.0 collective-permute-done.5.both
  46.8 0.1 route.1
  46.9 0.3 collective-permute-start.6
  47.2 2.9 %collective-permute-start.7 = (bf16[192,256]{1,0:T(8,128)(2,1)S(1)}, bf16[192,256]{1,0:T(8,128)(2,1)S(1)}, u32[]{:S(2)}, u32[]{:S(2)}) collective-permute-start(bf16[192,256]{1,0:T(8,128)(2,1)S(1)} %get-tuple-element.29), channel_id=1, source_target_pairs={{0,4},{1,5},{2,6},{3,7},{4,0},{5,1},{6,2},{7,3},{8,12},{9,13},{10,... | collective-permute-start | bytes 294920 | tf_op jit(solution)/shard_map/ppermute | solution.py:267
  50.1 3.2 %collective-permute-done.6.one = bf16[192,256]{1,0:T(8,128)(2,1)S(1)} collective-permute-done((bf16[192,256]{1,0:T(8,128)(2,1)S(1)}, bf16[192,256]{1,0:T(8,128)(2,1)S(1)}, u32[]{:S(2)}, u32[]{:S(2)}) %collective-permute-start.6) | collective-permute-done | bytes 98336 | tf_op jit(solution)/shard_map/ppermute | solution.py:267
  53.3 2.1 %collective-permute-start.8 = (bf16[192,256]{1,0:T(8,128)(2,1)S(1)}, bf16[192,256]{1,0:T(8,128)(2,1)S(1)}, u32[]{:S(2)}, u32[]{:S(2)}) collective-permute-start(bf16[192,256]{1,0:T(8,128)(2,1)S(1)} %get-tuple-element.31), channel_id=1, source_target_pairs={{0,6},{1,7},{2,4},{3,5},{4,2},{5,3},{6,0},{7,1},{8,14},{9,15},{10,... | collective-permute-start | bytes 294920 | tf_op jit(solution)/shard_map/ppermute | solution.py:267
  55.3 0.8 %collective-permute-done.7.two = bf16[192,256]{1,0:T(8,128)(2,1)S(1)} collective-permute-done((bf16[192,256]{1,0:T(8,128)(2,1)S(1)}, bf16[192,256]{1,0:T(8,128)(2,1)S(1)}, u32[]{:S(2)}, u32[]{:S(2)}) %collective-permute-start.7) | collective-permute-done | bytes 98336 | tf_op jit(solution)/shard_map/ppermute | solution.py:267
  56.1 3.6 %collective-permute-done.8.three = bf16[192,256]{1,0:T(8,128)(2,1)S(1)} collective-permute-done((bf16[192,256]{1,0:T(8,128)(2,1)S(1)}, bf16[192,256]{1,0:T(8,128)(2,1)S(1)}, u32[]{:S(2)}, u32[]{:S(2)}) %collective-permute-start.8) | collective-permute-done | bytes 98336 | tf_op jit(solution)/shard_map/ppermute | solution.py:267
  59.7 0.1 share.1
  59.8 0.1 collective-permute-start.9
  59.8 0.0 collective-permute-done.came_d
  59.9 2.2 %own.1.own_ref = f32[768,256]{1,0:T(8,128)S(1)} custom-call(s32[4,12]{1,0:T(4,128)S(1)} %copy-done.2, bf16[768,1536]{1,0:T(8,128)(2,1)S(1)} %copy-done, s16[1536,1024]{1,0:T(8,128)(2,1)S(1)} %all-gather.1.code_ref, s16[784,256]{1,0:T(8,128)(2,1)S(1)} %collective-permute-done.came_d), custom_call_target="tpu_custom_call" | custom-call | flops 1 | bytes 1 | tf_op jit(solution)/shard_map/own/pallas_call | solution.py:335
  62.1 0.0 copy-start.3
  62.1 0.0 collective-permute-done.9.came
  62.1 0.2 turn.1.lower
  62.3 0.0 collective-permute-done.1.came_x
  62.3 0.0 collective-permute-done.2.came_y
  62.3 1.7 %last.1 = (bf16[768,256]{1,0:T(8,128)(2,1)}, f32[256,256]{1,0:T(8,128)S(1)}) custom-call(s32[4,12]{1,0:T(4,128)S(1)} %copy-done.2, f32[768,256]{1,0:T(8,128)S(1)} %own.1.own_ref, s16[784,256]{1,0:T(8,128)(2,1)S(1)} %collective-permute-done.1.came_x, s16[784,256]{1,0:T(8,128)(2,1)S(1)} %collective-permute-done.2.came_y, bf16[256,768]{1,0:T(8,128)(2,1)S(1)} %turn.1.lower), custom_call_target="tpu_custom_call" | custom-call | flops 201326592 | bytes 1572864 | tf_op jit(solution)/shard_map/last/pallas_call | solution.py:357
  64.1 0.6 collective-permute-start.10
  64.6 1.0 %collective-permute-done.10 = f32[128,256]{1,0:T(8,128)S(1)} collective-permute-done((f32[128,256]{1,0:T(8,128)S(1)}, f32[128,256]{1,0:T(8,128)S(1)}, u32[]{:S(2)}, u32[]{:S(2)}) %collective-permute-start.10) | collective-permute-done | bytes 131104 | tf_op jit(solution)/shard_map/ppermute | solution.py:267
  65.6 0.1 collective-permute-start.11
  65.7 2.1 %collective-permute-start.13 = (f32[32,256]{1,0:T(8,128)S(1)}, f32[32,256]{1,0:T(8,128)S(1)}, u32[]{:S(2)}, u32[]{:S(2)}) collective-permute-start(f32[32,256]{1,0:T(8,128)S(1)} %get-tuple-element.37), channel_id=1, source_target_pairs={{0,6},{1,7},{2,4},{3,5},{4,2},{5,3},{6,0},{7,1},{8,14},{9,15},{10,... | collective-permute-start | bytes 98312 | tf_op jit(solution)/shard_map/ppermute | solution.py:267
  67.9 1.3 %collective-permute-start.12 = (f32[32,256]{1,0:T(8,128)S(1)}, f32[32,256]{1,0:T(8,128)S(1)}, u32[]{:S(2)}, u32[]{:S(2)}) collective-permute-start(f32[32,256]{1,0:T(8,128)S(1)} %get-tuple-element.38), channel_id=1, source_target_pairs={{0,4},{1,5},{2,6},{3,7},{4,0},{5,1},{6,2},{7,3},{8,12},{9,13},{10,... | collective-permute-start | bytes 98312 | tf_op jit(solution)/shard_map/ppermute | solution.py:267
  69.2 0.4 collective-permute-done.11
  69.6 1.9 %collective-permute-done.13 = f32[32,256]{1,0:T(8,128)S(1)} collective-permute-done((f32[32,256]{1,0:T(8,128)S(1)}, f32[32,256]{1,0:T(8,128)S(1)}, u32[]{:S(2)}, u32[]{:S(2)}) %collective-permute-start.13) | collective-permute-done | bytes 32800 | tf_op jit(solution)/shard_map/ppermute | solution.py:267
  71.5 1.1 %collective-permute-done.12 = f32[32,256]{1,0:T(8,128)S(1)} collective-permute-done((f32[32,256]{1,0:T(8,128)S(1)}, f32[32,256]{1,0:T(8,128)S(1)}, u32[]{:S(2)}, u32[]{:S(2)}) %collective-permute-start.12) | collective-permute-done | bytes 32800 | tf_op jit(solution)/shard_map/ppermute | solution.py:267
  72.7 0.0 copy-done.3
  72.7 0.6 fusion.2
  (3 shorter events, 0.0 us)
Async XLA Ops:
  0.6 38.0 %copy-start = (bf16[768,1536]{1,0:T(8,128)(2,1)S(1)}, bf16[768,1536]{1,0:T(8,128)(2,1)}, u32[]{:S(2)}) copy-start(bf16[768,1536]{1,0:T(8,128)(2,1)} %a_ref.5) | copy-start | bytes 7077892
  0.6 1.1 %copy-start.1 = (bf16[192,1024]{1,0:T(8,128)(2,1)S(1)}, bf16[192,1024]{1,0:T(8,128)(2,1)}, u32[]{:S(2)}) copy-start(bf16[192,1024]{1,0:T(8,128)(2,1)} %lower_ref.1) | copy-start | bytes 1179652
  1.8 36.9 %copy-start.2 = (s32[4,12]{1,0:T(4,128)S(1)}, s32[4,12]{1,0:T(4,128)}, u32[]{:S(2)}) copy-start(s32[4,12]{1,0:T(4,128)} %struct_ref.6) | copy-start | bytes 580
  2.3 44.0 %collective-permute-start.3 = (bf16[192,256]{1,0:T(8,128)(2,1)S(1)}, bf16[192,256]{1,0:T(8,128)(2,1)S(1)}, u32[]{:S(2)}, u32[]{:S(2)}) collective-permute-start(bf16[192,256]{1,0:T(8,128)(2,1)S(1)} %get-tuple-element.24), channel_id=1, source_target_pairs={{0,8},{1,9},{2,10},{3,11},{4,12},{5,13},{6,14},{7,15},{8,0},{9,1},... | collective-permute-start | bytes 294920 | tf_op jit(solution)/shard_map/ppermute | solution.py:267
  5.3 41.4 %collective-permute-start.4 = (bf16[192,256]{1,0:T(8,128)(2,1)S(1)}, bf16[192,256]{1,0:T(8,128)(2,1)S(1)}, u32[]{:S(2)}, u32[]{:S(2)}) collective-permute-start(bf16[192,256]{1,0:T(8,128)(2,1)S(1)} %get-tuple-element.25), channel_id=1, source_target_pairs={{0,16},{1,17},{2,18},{3,19},{4,20},{5,21},{6,22},{7,23},{8,24},{9,... | collective-permute-start | bytes 294920 | tf_op jit(solution)/shard_map/ppermute | solution.py:267
  6.9 39.9 %collective-permute-start.5 = (bf16[192,256]{1,0:T(8,128)(2,1)S(1)}, bf16[192,256]{1,0:T(8,128)(2,1)S(1)}, u32[]{:S(2)}, u32[]{:S(2)}) collective-permute-start(bf16[192,256]{1,0:T(8,128)(2,1)S(1)} %get-tuple-element.26), channel_id=1, source_target_pairs={{0,24},{1,25},{2,26},{3,27},{4,28},{5,29},{6,30},{7,31},{8,16},{9,... | collective-permute-start | bytes 294920 | tf_op jit(solution)/shard_map/ppermute | solution.py:267
  40.6 19.2 %collective-permute-start = (s16[784,256]{1,0:T(8,128)(2,1)S(1)}, s16[784,256]{1,0:T(8,128)(2,1)S(1)}, u32[]{:S(2)}, u32[]{:S(2)}) collective-permute-start(s16[784,256]{1,0:T(8,128)(2,1)S(1)} %sums_d.1), channel_id=1, source_target_pairs={{0,24},{1,25},{2,26},{3,27},{4,28},{5,29},{6,30},{7,31},{8,16},{9,... | collective-permute-start | bytes 1204232 | tf_op jit(solution)/shard_map/ppermute | solution.py:267
  46.1 16.2 %collective-permute-start.1 = (s16[784,256]{1,0:T(8,128)(2,1)S(1)}, s16[784,256]{1,0:T(8,128)(2,1)S(1)}, u32[]{:S(2)}, u32[]{:S(2)}) collective-permute-start(s16[784,256]{1,0:T(8,128)(2,1)S(1)} %get-tuple-element.21), channel_id=1, source_target_pairs={{0,8},{1,9},{2,10},{3,11},{4,12},{5,13},{6,14},{7,15},{8,0},{9,1},... | collective-permute-start | bytes 1204232 | tf_op jit(solution)/shard_map/ppermute | solution.py:267
  46.4 16.0 %collective-permute-start.2 = (s16[784,256]{1,0:T(8,128)(2,1)S(1)}, s16[784,256]{1,0:T(8,128)(2,1)S(1)}, u32[]{:S(2)}, u32[]{:S(2)}) collective-permute-start(s16[784,256]{1,0:T(8,128)(2,1)S(1)} %get-tuple-element.22), channel_id=1, source_target_pairs={{0,16},{1,17},{2,18},{3,19},{4,20},{5,21},{6,22},{7,23},{8,24},{9,... | collective-permute-start | bytes 1204232 | tf_op jit(solution)/shard_map/ppermute | solution.py:267
  46.9 6.4 %collective-permute-start.6 = (bf16[192,256]{1,0:T(8,128)(2,1)S(1)}, bf16[192,256]{1,0:T(8,128)(2,1)S(1)}, u32[]{:S(2)}, u32[]{:S(2)}) collective-permute-start(bf16[192,256]{1,0:T(8,128)(2,1)S(1)} %get-tuple-element.28), channel_id=1, source_target_pairs={{0,2},{1,3},{2,0},{3,1},{4,6},{5,7},{6,4},{7,5},{8,10},{9,11},{10,... | collective-permute-start | bytes 294920 | tf_op jit(solution)/shard_map/ppermute | solution.py:267
  47.2 8.9 %collective-permute-start.7 = (bf16[192,256]{1,0:T(8,128)(2,1)S(1)}, bf16[192,256]{1,0:T(8,128)(2,1)S(1)}, u32[]{:S(2)}, u32[]{:S(2)}) collective-permute-start(bf16[192,256]{1,0:T(8,128)(2,1)S(1)} %get-tuple-element.29), channel_id=1, source_target_pairs={{0,4},{1,5},{2,6},{3,7},{4,0},{5,1},{6,2},{7,3},{8,12},{9,13},{10,... | collective-permute-start | bytes 294920 | tf_op jit(solution)/shard_map/ppermute | solution.py:267
  53.3 6.4 %collective-permute-start.8 = (bf16[192,256]{1,0:T(8,128)(2,1)S(1)}, bf16[192,256]{1,0:T(8,128)(2,1)S(1)}, u32[]{:S(2)}, u32[]{:S(2)}) collective-permute-start(bf16[192,256]{1,0:T(8,128)(2,1)S(1)} %get-tuple-element.31), channel_id=1, source_target_pairs={{0,6},{1,7},{2,4},{3,5},{4,2},{5,3},{6,0},{7,1},{8,14},{9,15},{10,... | collective-permute-start | bytes 294920 | tf_op jit(solution)/shard_map/ppermute | solution.py:267
  59.8 2.3 %collective-permute-start.9 = (bf16[384,256]{1,0:T(8,128)(2,1)S(1)}, bf16[384,256]{1,0:T(8,128)(2,1)S(1)}, u32[]{:S(2)}, u32[]{:S(2)}) collective-permute-start(bf16[384,256]{1,0:T(8,128)(2,1)S(1)} %get-tuple-element.33), channel_id=1, source_target_pairs={{0,1},{1,0},{2,3},{3,2},{4,5},{5,4},{6,7},{7,6},{8,9},{9,8},{10,11... | collective-permute-start | bytes 589832 | tf_op jit(solution)/shard_map/ppermute | solution.py:267
  62.1 10.6 %copy-start.3 = (f32[32,256]{1,0:T(8,128)S(1)}, f32[32,256]{1,0:T(8,128)}, u32[]{:S(2)}) copy-start(f32[32,256]{1,0:T(8,128)} %param.6) | copy-start | bytes 98308
  64.1 1.5 %collective-permute-start.10 = (f32[128,256]{1,0:T(8,128)S(1)}, f32[128,256]{1,0:T(8,128)S(1)}, u32[]{:S(2)}, u32[]{:S(2)}) collective-permute-start(f32[128,256]{1,0:T(8,128)S(1)} %slice.19), channel_id=1, source_target_pairs={{0,1},{1,0},{2,3},{3,2},{4,5},{5,4},{6,7},{7,6},{8,9},{9,8},{10,11... | collective-permute-start | bytes 393224 | tf_op jit(solution)/shard_map/ppermute | solution.py:267
  65.6 4.0 %collective-permute-start.11 = (f32[32,256]{1,0:T(8,128)S(1)}, f32[32,256]{1,0:T(8,128)S(1)}, u32[]{:S(2)}, u32[]{:S(2)}) collective-permute-start(f32[32,256]{1,0:T(8,128)S(1)} %get-tuple-element.36), channel_id=1, source_target_pairs={{0,2},{1,3},{2,0},{3,1},{4,6},{5,7},{6,4},{7,5},{8,10},{9,11},{10,... | collective-permute-start | bytes 98312 | tf_op jit(solution)/shard_map/ppermute | solution.py:267
  65.7 5.8 %collective-permute-start.13 = (f32[32,256]{1,0:T(8,128)S(1)}, f32[32,256]{1,0:T(8,128)S(1)}, u32[]{:S(2)}, u32[]{:S(2)}) collective-permute-start(f32[32,256]{1,0:T(8,128)S(1)} %get-tuple-element.37), channel_id=1, source_target_pairs={{0,6},{1,7},{2,4},{3,5},{4,2},{5,3},{6,0},{7,1},{8,14},{9,15},{10,... | collective-permute-start | bytes 98312 | tf_op jit(solution)/shard_map/ppermute | solution.py:267
  67.9 4.8 %collective-permute-start.12 = (f32[32,256]{1,0:T(8,128)S(1)}, f32[32,256]{1,0:T(8,128)S(1)}, u32[]{:S(2)}, u32[]{:S(2)}) collective-permute-start(f32[32,256]{1,0:T(8,128)S(1)} %get-tuple-element.38), channel_id=1, source_target_pairs={{0,4},{1,5},{2,6},{3,7},{4,0},{5,1},{6,2},{7,3},{8,12},{9,13},{10,... | collective-permute-start | bytes 98312 | tf_op jit(solution)/shard_map/ppermute | solution.py:267

commit v5 on v4

--- a/solution.py
+++ b/solution.py
@@ -130,7 +130,7 @@
 
     for flip, out in enumerate((own, to_x, to_y, to_both)):
         out[...] = level(p ^ flip)
-    for slot, flip in enumerate((3, 1, 2, 0)):
+    for slot, flip in enumerate((3, 1, 2)):
         value = level(p ^ flip).astype(jnp.float32)
         size = jnp.abs(value)
         power = jnp.floor(jnp.log2(jnp.maximum(size, TINY)))
@@ -183,15 +183,40 @@
     return jnp.exp2(from_code(ref[blocks * B : blocks * B + TAIL]) - 15.0) * (1.0 / FILL)
 
 
-def own_kernel(struct_ref, a_ref, code_ref, came_d, own_ref, panel):
-    load_panel(code_ref, panel, struct_ref, ((3, 0),))
-    blocks = own_ref.shape[0] // B
-    step = came_step(came_d, blocks)
+def pair_kernel(to_two, own_ref, one_ref, out_ref):
+    shard = own_ref.shape[0]
+    for at, ref in enumerate((to_two, own_ref, one_ref)):
+        out_ref[at * shard : (at + 1) * shard] = ref[...]
+
+
+def base_kernel(came_ref, base_ref):
+    blocks = base_ref.shape[0] // B
+    step = came_step(came_ref, blocks)
     for b in range(blocks):
         rows = slice(b * B, (b + 1) * B)
-        own_ref[rows] = from_code(came_d[rows]) * step[b : b + 1] - jnp.dot(
-            a_ref[rows], panel[...], preferred_element_type=jnp.float32
-        )
+        base_ref[rows] = from_code(came_ref[rows]) * step[b : b + 1]
+
+
+def own_kernel(
+    struct_ref, a_ref, pair, two, their_pair, their_two, base_ref, own_ref, panel
+):
+    p, z, c = place()
+    shard = panel.shape[0] // 8
+    for flip in range(4):
+        for refs, core in (((pair, two), c), ((their_pair, their_two), 1 - c)):
+            at = pl.multiple_of((2 * (z ^ flip) + core) * shard, FINE)
+            part = slice((flip % 2) * shard, (flip % 2 + 1) * shard)
+            panel[pl.ds(at, shard)] = refs[flip // 2][part]
+    blocks = panel.shape[0] // B
+    for block in range(blocks):
+
+        @pl.when(jnp.logical_not(is_member(struct_ref, p, p * blocks + block)))
+        def _(block=block):
+            panel[block * B : (block + 1) * B] = jnp.zeros((B, B), jnp.bfloat16)
+
+    own_ref[...] = base_ref[...] - jnp.dot(
+        a_ref[...], panel[...], preferred_element_type=jnp.float32
+    )
 
 
 def route_kernel(own, x, y, both, *outs):
@@ -213,11 +238,11 @@
 
         @pl.when(chip // 2 == c)
         def _(ref=ref, at=at):
-            keep_ref[pl.ds(at, shard)] = ref[...]
+            keep_ref[pl.ds(at, shard)] = ref[:shard]
 
         @pl.when(chip // 2 != c)
         def _(ref=ref, at=at):
-            give_ref[pl.ds(at, shard)] = ref[...]
+            give_ref[pl.ds(at, shard)] = ref[:shard]
 
 
 def turn_kernel(keep, came, out_ref, lower):
@@ -291,13 +316,18 @@
     piece = shape((shard, B), bf16)
     code, keep, to_x, to_y, to_both = call(
         code_kernel,
-        (shape((shard, NK * B), i16),) + (piece,) * 4,
+        (shape((shard, 3 * B), i16),) + (piece,) * 4,
         [VM],
         [],
         8 * shard * NK * B,
         4 * shard * NK * B,
         "code",
     )(lower_panel)
+    def small(kernel, outs, name, *args, flops=1):
+        return call(kernel, outs, [VM] * len(args), [], flops, 1, name, room=2**21)(*args)
+
+    own_piece = keep
+    far_one = send(keep, along(1))
     rows_x = send(to_x, across(1))
     rows_y = send(to_y, across(2))
     rows_both = send(to_both, across(3))
@@ -323,27 +353,31 @@
     )
     came_x = send(part_x, across(1))
     came_y = send(part_y, across(2))
-    def small(kernel, outs, name, *args, flops=1):
-        return call(kernel, outs, [VM] * len(args), [], flops, 1, name, room=2**21)(*args)
-
     stay, to_one, to_two, to_three = small(
-        route_kernel, (piece,) * 4, "route", keep, rows_x, rows_y, rows_both, flops=1
-    )
+        route_kernel, (piece,) * 4, "route", keep, rows_x, rows_y, rows_both, flops=8 * 10**9
+    )
+    to_one, to_two, to_three, _ = lax.optimization_barrier((to_one, to_two, to_three, part_d))
     from_one = send(to_one, along(1))
-    from_two = send(to_two, along(2))
-    from_three = send(after(to_three, from_one), along(3))
+    trio = small(
+        pair_kernel, shape((3 * shard, B), bf16), "pair", to_two, own_piece, far_one, flops=3 * 10**9
+    )
+    from_two = send(trio, along(2))
+    pair, two = trio[shard:], from_two[shard:]
+    their_pair = send(pair, chip_swap)
+    from_three = send(to_three, along(3))
+    base = small(base_kernel, shape((rows, B), f32), "base", came_d, flops=4 * 10**9)
     own = call(
         own_kernel,
         shape((rows, B), f32),
-        [SM, VM, VM, VM],
+        [SM] + [VM] * 6,
         [pltpu.VMEM((depth, B), bf16)],
         1,
         1,
         "own",
-    )(struct_list, ancestor_inverse, gathered, came_d)
+    )(struct_list, ancestor_inverse, pair, two, their_pair, send(two, chip_swap), base)
     half_rows = shape((2 * shard, B), bf16)
     keep, give = small(
-        share_kernel, (half_rows, half_rows), "share", stay, from_one, from_two, from_three
+        share_kernel, (half_rows, half_rows), "share", stay, from_one, from_two, from_three, flops=2 * 10**9
     )
     lower = call(
         turn_kernel,

time: 73.5 us -> 71 us (0.966)
  blocking collectives: 31.8 us -> 24.5 us
  starting transfers between devices: 17.2 us -> 22 us
  Pallas kernels: 9.75 us -> 8.18 us
  waiting for transfers between devices: 12 us -> 13.4 us
    all_gather x1, blocking collectives: 31.8 us -> 24.5 us  [line_body(): gathered = lax.all_gather(code, 'pcol', axis=0, tiled=True)]
    ppermute x14 -> x17, starting transfers between devices: 17.2 us -> 22 us  [send(): return lax.ppermute(value, AXES, found)]
    ppermute x14 -> x17, waiting for transfers between devices: 12 us -> 13.4 us  [send(): return lax.ppermute(value, AXES, found)]
    pallas_call x2, Pallas kernels: 4.92 us -> 4.08 us  [sums(): call(functools.partial(sums_kernel, slots), (coded,) * outs, [SM, VM, VM]...]
    pallas_call x2, Pallas kernels: 2.78 us -> 1.95 us  [the longest x1 1.53 us: line_body(): call(own_kernel, shape((rows, B), f32), [SM] + [VM] * 6, [pltpu.VMEM((dep...]
  transfers between devices with their start and end apart: 14 -> 17, of which waited for: 7 -> 8; matrix products, arithmetic and copies ran while one was open for 0% -> 0% of each run, Pallas kernels for 10% -> 9%
where the time goes in v5:
time: 71 us; the launch traced here: 70.8 us
  blocking collectives  24.5 us (35%)
  starting transfers between devices  22 us (31%)
  waiting for transfers between devices  13.4 us (19%)
  Pallas kernels  8.18 us (12%)
  local copies, waits for them, and re-layouts  1.2 us (2%)
  between operations  0.83 us (1%)
    all_gather x1, blocking collectives, line_body(): gathered = lax.all_gather(code, 'pcol', axis=0, tiled=True)  24.5 us
    ppermute x17, starting transfers between devices, send(): return lax.ppermute(value, AXES, found)  22 us
    ppermute x17, waiting for transfers between devices, send(): return lax.ppermute(value, AXES, found)  13.4 us
    pallas_call x2, Pallas kernels, sums(): call(functools.partial(sums_kernel, slots), (coded,) * outs, [SM, VM, VM]...  4.08 us
    pallas_call x1, Pallas kernels, line_body(): call(last_kernel, (shape((rows, B), bf16), shape((B, B), f32)), [SM] + [V...  1.7 us
    pallas_call x1, Pallas kernels, line_body(): call(own_kernel, shape((rows, B), f32), [SM] + [VM] * 6, [pltpu.VMEM((dep...  1.53 us
  transfers between devices with their start and end apart: 17, of which 8 were waited for; matrix products, arithmetic and copies ran while one was open for 0% of the time, Pallas kernels for 9%

profile of v5, /device:TPU:0, one launch (start us, length us, event | category | flops | bytes accessed | tf_op | source)
XLA Modules:
  0.0 70.8 jit_solution(2027955685022671700)
XLA Ops:
  0.6 0.0 copy-start
  0.6 0.0 copy-start.1
  0.6 1.1 %copy-done.1 = bf16[192,1024]{1,0:T(8,128)(2,1)S(1)} copy-done((bf16[192,1024]{1,0:T(8,128)(2,1)S(1)}, bf16[192,1024]{1,0:T(8,128)(2,1)}, u32[]{:S(2)}) %copy-start.1) | copy-done | bytes 393240
  1.8 0.0 copy-start.2
  1.8 0.4 code.1
  2.2 3.0 %collective-permute-start = (bf16[192,256]{1,0:T(8,128)(2,1)S(1)}, bf16[192,256]{1,0:T(8,128)(2,1)S(1)}, u32[]{:S(2)}, u32[]{:S(2)}) collective-permute-start(bf16[192,256]{1,0:T(8,128)(2,1)S(1)} %get-tuple-element.22), channel_id=1, source_target_pairs={{0,8},{1,9},{2,10},{3,11},{4,12},{5,13},{6,14},{7,15},{8,0},{9,1},... | collective-permute-start | bytes 294920 | tf_op jit(solution)/shard_map/ppermute | solution.py:292
  5.2 1.5 %collective-permute-start.1 = (bf16[192,256]{1,0:T(8,128)(2,1)S(1)}, bf16[192,256]{1,0:T(8,128)(2,1)S(1)}, u32[]{:S(2)}, u32[]{:S(2)}) collective-permute-start(bf16[192,256]{1,0:T(8,128)(2,1)S(1)} %get-tuple-element.23), channel_id=1, source_target_pairs={{0,16},{1,17},{2,18},{3,19},{4,20},{5,21},{6,22},{7,23},{8,24},{9,... | collective-permute-start | bytes 294920 | tf_op jit(solution)/shard_map/ppermute | solution.py:292
  6.7 0.0 collective-permute-start.2
  6.8 2.0 %collective-permute-start.3 = (bf16[192,256]{1,0:T(8,128)(2,1)S(1)}, bf16[192,256]{1,0:T(8,128)(2,1)S(1)}, u32[]{:S(2)}, u32[]{:S(2)}) collective-permute-start(bf16[192,256]{1,0:T(8,128)(2,1)S(1)} %get-tuple-element.21.own.own_ref), channel_id=1, source_target_pairs={{0,2},{1,3},{2,0},{3,1},{4,6},{5,7},{6,4},{7,5},{8,10},{9,11},{10,... | collective-permute-start | bytes 294920 | tf_op jit(solution)/shard_map/ppermute | solution.py:292
  8.8 24.5 %all-gather.1.code_ref = s16[1536,768]{1,0:T(8,128)(2,1)S(1)} all-gather(s16[192,768]{1,0:T(8,128)(2,1)S(1)} %get-tuple-element.28), channel_id=1, replica_groups=mesh['prow'=4,'pcol'=8] {'pcol'}, dimensions={0}, use_global_device_ids=true | all-gather | bytes 2654208 | tf_op jit(solution)/shard_map/all_gather | solution.py:334
  33.3 0.0 copy-done
  33.3 0.0 copy-done.2
  33.3 1.6 %sums_d.1 = s16[784,256]{1,0:T(8,128)(2,1)S(1)} custom-call(s32[4,12]{1,0:T(4,128)S(1)} %copy-done.2, bf16[768,1536]{1,0:T(8,128)(2,1)S(1)} %copy-done, s16[1536,768]{1,0:T(8,128)(2,1)S(1)} %all-gather.1.code_ref), custom_call_target="tpu_custom_call" | custom-call | flops 1 | bytes 1 | tf_op jit(solution)/shard_map/sums_d/pallas_call | solution.py:339
  35.0 0.0 collective-permute-done.x
  35.0 0.0 collective-permute-done.1.y
  35.0 0.0 collective-permute-done.2.both
  35.0 0.1 route.1
  35.1 0.0 collective-permute-done.3.one_ref
  35.1 1.0 %collective-permute-start.4 = (bf16[576,256]{1,0:T(8,128)(2,1)S(1)}, bf16[576,256]{1,0:T(8,128)(2,1)S(1)}, u32[]{:S(2)}, u32[]{:S(2)}) collective-permute-start(bf16[576,256]{1,0:T(8,128)(2,1)S(1)} %pair.1), channel_id=1, source_target_pairs={{0,4},{1,5},{2,6},{3,7},{4,0},{5,1},{6,2},{7,3},{8,12},{9,13},{10,... | collective-permute-start | bytes 884744 | tf_op jit(solution)/shard_map/ppermute | solution.py:292
  36.2 2.8 %collective-permute-start.7 = (s16[784,256]{1,0:T(8,128)(2,1)S(1)}, s16[784,256]{1,0:T(8,128)(2,1)S(1)}, u32[]{:S(2)}, u32[]{:S(2)}) collective-permute-start(s16[784,256]{1,0:T(8,128)(2,1)S(1)} %sums_d.1), channel_id=1, source_target_pairs={{0,24},{1,25},{2,26},{3,27},{4,28},{5,29},{6,30},{7,31},{8,16},{9,... | collective-permute-start | bytes 1204232 | tf_op jit(solution)/shard_map/ppermute | solution.py:292
  39.0 1.6 %collective-permute-start.10 = (bf16[192,256]{1,0:T(8,128)(2,1)S(1)}, bf16[192,256]{1,0:T(8,128)(2,1)S(1)}, u32[]{:S(2)}, u32[]{:S(2)}) collective-permute-start(bf16[192,256]{1,0:T(8,128)(2,1)S(1)} %get-tuple-element.34), channel_id=1, source_target_pairs={{0,2},{1,3},{2,0},{3,1},{4,6},{5,7},{6,4},{7,5},{8,10},{9,11},{10,... | collective-permute-start | bytes 294920 | tf_op jit(solution)/shard_map/ppermute | solution.py:292
  40.5 1.9 %collective-permute-start.11 = (bf16[192,256]{1,0:T(8,128)(2,1)S(1)}, bf16[192,256]{1,0:T(8,128)(2,1)S(1)}, u32[]{:S(2)}, u32[]{:S(2)}) collective-permute-start(bf16[192,256]{1,0:T(8,128)(2,1)S(1)} %get-tuple-element.35), channel_id=1, source_target_pairs={{0,6},{1,7},{2,4},{3,5},{4,2},{5,3},{6,0},{7,1},{8,14},{9,15},{10,... | collective-permute-start | bytes 294920 | tf_op jit(solution)/shard_map/ppermute | solution.py:292
  42.4 2.5 %sums_xy.1 = (s16[784,256]{1,0:T(8,128)(2,1)S(1)}, s16[784,256]{1,0:T(8,128)(2,1)S(1)}) custom-call(s32[4,12]{1,0:T(4,128)S(1)} %copy-done.2, bf16[768,1536]{1,0:T(8,128)(2,1)S(1)} %copy-done, s16[1536,768]{1,0:T(8,128)(2,1)S(1)} %all-gather.1.code_ref), custom_call_target="tpu_custom_call" | custom-call | flops 1 | bytes 1 | tf_op jit(solution)/shard_map/sums_xy/pallas_call | solution.py:339
  44.9 1.3 %collective-permute-start.8 = (s16[784,256]{1,0:T(8,128)(2,1)S(1)}, s16[784,256]{1,0:T(8,128)(2,1)S(1)}, u32[]{:S(2)}, u32[]{:S(2)}) collective-permute-start(s16[784,256]{1,0:T(8,128)(2,1)S(1)} %get-tuple-element.31), channel_id=1, source_target_pairs={{0,8},{1,9},{2,10},{3,11},{4,12},{5,13},{6,14},{7,15},{8,0},{9,1},... | collective-permute-start | bytes 1204232 | tf_op jit(solution)/shard_map/ppermute | solution.py:292
  46.2 0.0 collective-permute-done.10.one
  46.2 1.4 %collective-permute-start.9 = (s16[784,256]{1,0:T(8,128)(2,1)S(1)}, s16[784,256]{1,0:T(8,128)(2,1)S(1)}, u32[]{:S(2)}, u32[]{:S(2)}) collective-permute-start(s16[784,256]{1,0:T(8,128)(2,1)S(1)} %get-tuple-element.32), channel_id=1, source_target_pairs={{0,16},{1,17},{2,18},{3,19},{4,20},{5,21},{6,22},{7,23},{8,24},{9,... | collective-permute-start | bytes 1204232 | tf_op jit(solution)/shard_map/ppermute | solution.py:292
  47.7 1.5 %collective-permute-done.11.three = bf16[192,256]{1,0:T(8,128)(2,1)S(1)} collective-permute-done((bf16[192,256]{1,0:T(8,128)(2,1)S(1)}, bf16[192,256]{1,0:T(8,128)(2,1)S(1)}, u32[]{:S(2)}, u32[]{:S(2)}) %collective-permute-start.11) | collective-permute-done | bytes 98336 | tf_op jit(solution)/shard_map/ppermute | solution.py:292
  49.1 0.0 collective-permute-start.5
  49.1 4.1 %collective-permute-done.4.two = bf16[576,256]{1,0:T(8,128)(2,1)S(1)} collective-permute-done((bf16[576,256]{1,0:T(8,128)(2,1)S(1)}, bf16[576,256]{1,0:T(8,128)(2,1)S(1)}, u32[]{:S(2)}, u32[]{:S(2)}) %collective-permute-start.4) | collective-permute-done | bytes 294944 | tf_op jit(solution)/shard_map/ppermute | solution.py:292
  53.3 0.1 share.1
  53.4 0.1 collective-permute-start.12
  53.5 0.0 collective-permute-done.7.came_ref
  53.5 0.6 collective-permute-start.6
  54.0 0.1 base.1.base_ref
  54.1 0.8 %collective-permute-done.12.came = bf16[384,256]{1,0:T(8,128)(2,1)S(1)} collective-permute-done((bf16[384,256]{1,0:T(8,128)(2,1)S(1)}, bf16[384,256]{1,0:T(8,128)(2,1)S(1)}, u32[]{:S(2)}, u32[]{:S(2)}) %collective-permute-start.12) | collective-permute-done | bytes 196640 | tf_op jit(solution)/shard_map/ppermute | solution.py:292
  54.9 0.2 turn.1.lower
  55.1 0.0 collective-permute-done.5.their_pair
  55.1 0.1 collective-permute-done.6.their_two
  55.1 1.5 %own.1.own_ref = f32[768,256]{1,0:T(8,128)S(1)} custom-call(s32[4,12]{1,0:T(4,128)S(1)} %copy-done.2, bf16[768,1536]{1,0:T(8,128)(2,1)S(1)} %copy-done, bf16[384,256]{1,0:T(8,128)(2,1)S(1)} %slice.32.pair, bf16[384,256]{1,0:T(8,128)(2,1)S(1)} %slice.33.two, bf16[384,256]{1,0:T(8,128)(2,1)S(1)} %collective-permute-done.5.their_pair, ...), custom_call_target="tpu_custom_call" | custom-call | flops 1 | bytes 1 | tf_op jit(solution)/shard_map/own/pallas_call | solution.py:369
  56.7 0.0 copy-start.3
  56.7 0.8 %collective-permute-done.8.came_x = s16[784,256]{1,0:T(8,128)(2,1)S(1)} collective-permute-done((s16[784,256]{1,0:T(8,128)(2,1)S(1)}, s16[784,256]{1,0:T(8,128)(2,1)S(1)}, u32[]{:S(2)}, u32[]{:S(2)}) %collective-permute-start.8) | collective-permute-done | bytes 401440 | tf_op jit(solution)/shard_map/ppermute | solution.py:292
  57.5 0.0 collective-permute-done.9.came_y
  57.5 1.7 %last.1 = (bf16[768,256]{1,0:T(8,128)(2,1)}, f32[256,256]{1,0:T(8,128)S(1)}) custom-call(s32[4,12]{1,0:T(4,128)S(1)} %copy-done.2, f32[768,256]{1,0:T(8,128)S(1)} %own.1.own_ref, s16[784,256]{1,0:T(8,128)(2,1)S(1)} %collective-permute-done.8.came_x, s16[784,256]{1,0:T(8,128)(2,1)S(1)} %collective-permute-done.9.came_y, bf16[256,768]{1,0:T(8,128)(2,1)S(1)} %turn.1.lower), custom_call_target="tpu_custom_call" | custom-call | flops 201326592 | bytes 1572864 | tf_op jit(solution)/shard_map/last/pallas_call | solution.py:391
  59.2 0.1 collective-permute-start.13
  59.3 1.3 %collective-permute-done.13 = f32[128,256]{1,0:T(8,128)S(1)} collective-permute-done((f32[128,256]{1,0:T(8,128)S(1)}, f32[128,256]{1,0:T(8,128)S(1)}, u32[]{:S(2)}, u32[]{:S(2)}) %collective-permute-start.13) | collective-permute-done | bytes 131104 | tf_op jit(solution)/shard_map/ppermute | solution.py:292
  60.6 2.2 %collective-permute-start.14 = (f32[32,256]{1,0:T(8,128)S(1)}, f32[32,256]{1,0:T(8,128)S(1)}, u32[]{:S(2)}, u32[]{:S(2)}) collective-permute-start(f32[32,256]{1,0:T(8,128)S(1)} %get-tuple-element.40), channel_id=1, source_target_pairs={{0,2},{1,3},{2,0},{3,1},{4,6},{5,7},{6,4},{7,5},{8,10},{9,11},{10,... | collective-permute-start | bytes 98312 | tf_op jit(solution)/shard_map/ppermute | solution.py:292
  62.9 2.4 %collective-permute-start.16 = (f32[32,256]{1,0:T(8,128)S(1)}, f32[32,256]{1,0:T(8,128)S(1)}, u32[]{:S(2)}, u32[]{:S(2)}) collective-permute-start(f32[32,256]{1,0:T(8,128)S(1)} %get-tuple-element.41), channel_id=1, source_target_pairs={{0,6},{1,7},{2,4},{3,5},{4,2},{5,3},{6,0},{7,1},{8,14},{9,15},{10,... | collective-permute-start | bytes 98312 | tf_op jit(solution)/shard_map/ppermute | solution.py:292
  65.3 0.0 collective-permute-start.15
  65.3 0.0 collective-permute-done.14
  65.3 3.3 %collective-permute-done.16 = f32[32,256]{1,0:T(8,128)S(1)} collective-permute-done((f32[32,256]{1,0:T(8,128)S(1)}, f32[32,256]{1,0:T(8,128)S(1)}, u32[]{:S(2)}, u32[]{:S(2)}) %collective-permute-start.16) | collective-permute-done | bytes 32800 | tf_op jit(solution)/shard_map/ppermute | solution.py:292
  68.6 1.5 %collective-permute-done.15 = f32[32,256]{1,0:T(8,128)S(1)} collective-permute-done((f32[32,256]{1,0:T(8,128)S(1)}, f32[32,256]{1,0:T(8,128)S(1)}, u32[]{:S(2)}, u32[]{:S(2)}) %collective-permute-start.15) | collective-permute-done | bytes 32800 | tf_op jit(solution)/shard_map/ppermute | solution.py:292
  70.1 0.0 copy-done.3
  70.1 0.6 fusion.2
  (6 shorter events, 0.1 us)
Async XLA Ops:
  0.6 32.7 %copy-start = (bf16[768,1536]{1,0:T(8,128)(2,1)S(1)}, bf16[768,1536]{1,0:T(8,128)(2,1)}, u32[]{:S(2)}) copy-start(bf16[768,1536]{1,0:T(8,128)(2,1)} %a_ref.5) | copy-start | bytes 7077892
  0.6 1.1 %copy-start.1 = (bf16[192,1024]{1,0:T(8,128)(2,1)S(1)}, bf16[192,1024]{1,0:T(8,128)(2,1)}, u32[]{:S(2)}) copy-start(bf16[192,1024]{1,0:T(8,128)(2,1)} %lower_ref.1) | copy-start | bytes 1179652
  1.8 31.6 %copy-start.2 = (s32[4,12]{1,0:T(4,128)S(1)}, s32[4,12]{1,0:T(4,128)}, u32[]{:S(2)}) copy-start(s32[4,12]{1,0:T(4,128)} %struct_ref.6) | copy-start | bytes 580
  2.2 32.8 %collective-permute-start = (bf16[192,256]{1,0:T(8,128)(2,1)S(1)}, bf16[192,256]{1,0:T(8,128)(2,1)S(1)}, u32[]{:S(2)}, u32[]{:S(2)}) collective-permute-start(bf16[192,256]{1,0:T(8,128)(2,1)S(1)} %get-tuple-element.22), channel_id=1, source_target_pairs={{0,8},{1,9},{2,10},{3,11},{4,12},{5,13},{6,14},{7,15},{8,0},{9,1},... | collective-permute-start | bytes 294920 | tf_op jit(solution)/shard_map/ppermute | solution.py:292
  5.2 29.8 %collective-permute-start.1 = (bf16[192,256]{1,0:T(8,128)(2,1)S(1)}, bf16[192,256]{1,0:T(8,128)(2,1)S(1)}, u32[]{:S(2)}, u32[]{:S(2)}) collective-permute-start(bf16[192,256]{1,0:T(8,128)(2,1)S(1)} %get-tuple-element.23), channel_id=1, source_target_pairs={{0,16},{1,17},{2,18},{3,19},{4,20},{5,21},{6,22},{7,23},{8,24},{9,... | collective-permute-start | bytes 294920 | tf_op jit(solution)/shard_map/ppermute | solution.py:292
  6.7 28.3 %collective-permute-start.2 = (bf16[192,256]{1,0:T(8,128)(2,1)S(1)}, bf16[192,256]{1,0:T(8,128)(2,1)S(1)}, u32[]{:S(2)}, u32[]{:S(2)}) collective-permute-start(bf16[192,256]{1,0:T(8,128)(2,1)S(1)} %get-tuple-element.24), channel_id=1, source_target_pairs={{0,24},{1,25},{2,26},{3,27},{4,28},{5,29},{6,30},{7,31},{8,16},{9,... | collective-permute-start | bytes 294920 | tf_op jit(solution)/shard_map/ppermute | solution.py:292
  6.8 28.3 %collective-permute-start.3 = (bf16[192,256]{1,0:T(8,128)(2,1)S(1)}, bf16[192,256]{1,0:T(8,128)(2,1)S(1)}, u32[]{:S(2)}, u32[]{:S(2)}) collective-permute-start(bf16[192,256]{1,0:T(8,128)(2,1)S(1)} %get-tuple-element.21.own.own_ref), channel_id=1, source_target_pairs={{0,2},{1,3},{2,0},{3,1},{4,6},{5,7},{6,4},{7,5},{8,10},{9,11},{10,... | collective-permute-start | bytes 294920 | tf_op jit(solution)/shard_map/ppermute | solution.py:292
  35.1 18.1 %collective-permute-start.4 = (bf16[576,256]{1,0:T(8,128)(2,1)S(1)}, bf16[576,256]{1,0:T(8,128)(2,1)S(1)}, u32[]{:S(2)}, u32[]{:S(2)}) collective-permute-start(bf16[576,256]{1,0:T(8,128)(2,1)S(1)} %pair.1), channel_id=1, source_target_pairs={{0,4},{1,5},{2,6},{3,7},{4,0},{5,1},{6,2},{7,3},{8,12},{9,13},{10,... | collective-permute-start | bytes 884744 | tf_op jit(solution)/shard_map/ppermute | solution.py:292
  36.2 17.3 %collective-permute-start.7 = (s16[784,256]{1,0:T(8,128)(2,1)S(1)}, s16[784,256]{1,0:T(8,128)(2,1)S(1)}, u32[]{:S(2)}, u32[]{:S(2)}) collective-permute-start(s16[784,256]{1,0:T(8,128)(2,1)S(1)} %sums_d.1), channel_id=1, source_target_pairs={{0,24},{1,25},{2,26},{3,27},{4,28},{5,29},{6,30},{7,31},{8,16},{9,... | collective-permute-start | bytes 1204232 | tf_op jit(solution)/shard_map/ppermute | solution.py:292
  39.0 7.2 %collective-permute-start.10 = (bf16[192,256]{1,0:T(8,128)(2,1)S(1)}, bf16[192,256]{1,0:T(8,128)(2,1)S(1)}, u32[]{:S(2)}, u32[]{:S(2)}) collective-permute-start(bf16[192,256]{1,0:T(8,128)(2,1)S(1)} %get-tuple-element.34), channel_id=1, source_target_pairs={{0,2},{1,3},{2,0},{3,1},{4,6},{5,7},{6,4},{7,5},{8,10},{9,11},{10,... | collective-permute-start | bytes 294920 | tf_op jit(solution)/shard_map/ppermute | solution.py:292
  40.5 8.6 %collective-permute-start.11 = (bf16[192,256]{1,0:T(8,128)(2,1)S(1)}, bf16[192,256]{1,0:T(8,128)(2,1)S(1)}, u32[]{:S(2)}, u32[]{:S(2)}) collective-permute-start(bf16[192,256]{1,0:T(8,128)(2,1)S(1)} %get-tuple-element.35), channel_id=1, source_target_pairs={{0,6},{1,7},{2,4},{3,5},{4,2},{5,3},{6,0},{7,1},{8,14},{9,15},{10,... | collective-permute-start | bytes 294920 | tf_op jit(solution)/shard_map/ppermute | solution.py:292
  44.9 12.6 %collective-permute-start.8 = (s16[784,256]{1,0:T(8,128)(2,1)S(1)}, s16[784,256]{1,0:T(8,128)(2,1)S(1)}, u32[]{:S(2)}, u32[]{:S(2)}) collective-permute-start(s16[784,256]{1,0:T(8,128)(2,1)S(1)} %get-tuple-element.31), channel_id=1, source_target_pairs={{0,8},{1,9},{2,10},{3,11},{4,12},{5,13},{6,14},{7,15},{8,0},{9,1},... | collective-permute-start | bytes 1204232 | tf_op jit(solution)/shard_map/ppermute | solution.py:292
  46.2 11.2 %collective-permute-start.9 = (s16[784,256]{1,0:T(8,128)(2,1)S(1)}, s16[784,256]{1,0:T(8,128)(2,1)S(1)}, u32[]{:S(2)}, u32[]{:S(2)}) collective-permute-start(s16[784,256]{1,0:T(8,128)(2,1)S(1)} %get-tuple-element.32), channel_id=1, source_target_pairs={{0,16},{1,17},{2,18},{3,19},{4,20},{5,21},{6,22},{7,23},{8,24},{9,... | collective-permute-start | bytes 1204232 | tf_op jit(solution)/shard_map/ppermute | solution.py:292
  49.1 5.9 %collective-permute-start.5 = (bf16[384,256]{1,0:T(8,128)(2,1)S(1)}, bf16[384,256]{1,0:T(8,128)(2,1)S(1)}, u32[]{:S(2)}, u32[]{:S(2)}) collective-permute-start(bf16[384,256]{1,0:T(8,128)(2,1)S(1)} %slice.32.pair), channel_id=1, source_target_pairs={{0,1},{1,0},{2,3},{3,2},{4,5},{5,4},{6,7},{7,6},{8,9},{9,8},{10,11... | collective-permute-start | bytes 589832 | tf_op jit(solution)/shard_map/ppermute | solution.py:292
  53.4 1.5 %collective-permute-start.12 = (bf16[384,256]{1,0:T(8,128)(2,1)S(1)}, bf16[384,256]{1,0:T(8,128)(2,1)S(1)}, u32[]{:S(2)}, u32[]{:S(2)}) collective-permute-start(bf16[384,256]{1,0:T(8,128)(2,1)S(1)} %get-tuple-element.37), channel_id=1, source_target_pairs={{0,1},{1,0},{2,3},{3,2},{4,5},{5,4},{6,7},{7,6},{8,9},{9,8},{10,11... | collective-permute-start | bytes 589832 | tf_op jit(solution)/shard_map/ppermute | solution.py:292
  53.5 1.7 %collective-permute-start.6 = (bf16[384,256]{1,0:T(8,128)(2,1)S(1)}, bf16[384,256]{1,0:T(8,128)(2,1)S(1)}, u32[]{:S(2)}, u32[]{:S(2)}) collective-permute-start(bf16[384,256]{1,0:T(8,128)(2,1)S(1)} %slice.33.two), channel_id=1, source_target_pairs={{0,1},{1,0},{2,3},{3,2},{4,5},{5,4},{6,7},{7,6},{8,9},{9,8},{10,11... | collective-permute-start | bytes 589832 | tf_op jit(solution)/shard_map/ppermute | solution.py:292
  56.7 13.5 %copy-start.3 = (f32[32,256]{1,0:T(8,128)S(1)}, f32[32,256]{1,0:T(8,128)}, u32[]{:S(2)}) copy-start(f32[32,256]{1,0:T(8,128)} %param.6) | copy-start | bytes 98308
  59.2 1.4 %collective-permute-start.13 = (f32[128,256]{1,0:T(8,128)S(1)}, f32[128,256]{1,0:T(8,128)S(1)}, u32[]{:S(2)}, u32[]{:S(2)}) collective-permute-start(f32[128,256]{1,0:T(8,128)S(1)} %slice.27), channel_id=1, source_target_pairs={{0,1},{1,0},{2,3},{3,2},{4,5},{5,4},{6,7},{7,6},{8,9},{9,8},{10,11... | collective-permute-start | bytes 393224 | tf_op jit(solution)/shard_map/ppermute | solution.py:292
  60.6 4.7 %collective-permute-start.14 = (f32[32,256]{1,0:T(8,128)S(1)}, f32[32,256]{1,0:T(8,128)S(1)}, u32[]{:S(2)}, u32[]{:S(2)}) collective-permute-start(f32[32,256]{1,0:T(8,128)S(1)} %get-tuple-element.40), channel_id=1, source_target_pairs={{0,2},{1,3},{2,0},{3,1},{4,6},{5,7},{6,4},{7,5},{8,10},{9,11},{10,... | collective-permute-start | bytes 98312 | tf_op jit(solution)/shard_map/ppermute | solution.py:292
  62.9 5.7 %collective-permute-start.16 = (f32[32,256]{1,0:T(8,128)S(1)}, f32[32,256]{1,0:T(8,128)S(1)}, u32[]{:S(2)}, u32[]{:S(2)}) collective-permute-start(f32[32,256]{1,0:T(8,128)S(1)} %get-tuple-element.41), channel_id=1, source_target_pairs={{0,6},{1,7},{2,4},{3,5},{4,2},{5,3},{6,0},{7,1},{8,14},{9,15},{10,... | collective-permute-start | bytes 98312 | tf_op jit(solution)/shard_map/ppermute | solution.py:292
  65.3 4.8 %collective-permute-start.15 = (f32[32,256]{1,0:T(8,128)S(1)}, f32[32,256]{1,0:T(8,128)S(1)}, u32[]{:S(2)}, u32[]{:S(2)}) collective-permute-start(f32[32,256]{1,0:T(8,128)S(1)} %get-tuple-element.42), channel_id=1, source_target_pairs={{0,4},{1,5},{2,6},{3,7},{4,0},{5,1},{6,2},{7,3},{8,12},{9,13},{10,... | collective-permute-start | bytes 98312 | tf_op jit(solution)/shard_map/ppermute | solution.py:292

commit v6 on v5

--- a/solution.py
+++ b/solution.py
@@ -277,7 +277,9 @@
     piece = B // 8
     for zz in range(4):
         for cc in range(2):
-            slot = (cc ^ c) * 4 + (zz ^ z)
+            flip = zz ^ z
+            core = jnp.where(flip == 1, 0, jnp.where(flip == 2, 1, cc))
+            slot = jnp.where(flip == 0, 3, jnp.where(flip == 3, 2, cc)) + 4 * (core ^ c)
             at = (2 * zz + cc) * piece
             diag_ref[pl.ds(pl.multiple_of(slot * piece, piece), piece)] = diag[at : at + piece]
 
@@ -400,8 +402,12 @@
 
     half, part = B // 2, B // 8
     total = diag[:half] + send(diag[half:], chip_swap)
-    near = [send(total[i * part : (i + 1) * part], along(i)) for i in (1, 2, 3)]
-    return off_inverse, pivot_inverse - (total[:part] + near[0] + near[1] + near[2])
+    pair = send(total[: 2 * part], lambda p, z, c: (p, z ^ (1 + c), c))
+    total = total[3 * part :] + send(total[2 * part : 3 * part], along(3))
+    even = lax.axis_index("pcol") % 2 == 0
+    kept = jnp.where(even, pair[:part], pair[part:])
+    other = send(jnp.where(even, pair[part:], pair[:part]), chip_swap)
+    return off_inverse, pivot_inverse - (total + kept + other)
 
 
 def body(ancestor_inverse, lower_panel, pivot_inverse, struct_list):

time: 71 us -> 69.6 us (0.980)
  waiting for transfers between devices: 13.4 us -> 12.1 us
    ppermute x17, waiting for transfers between devices: 13.4 us -> 12.1 us  [send(): return lax.ppermute(value, AXES, found)]
where the time goes in v6:
time: 69.6 us; the launch traced here: 69.5 us
  blocking collectives  24.5 us (35%)
  starting transfers between devices  21.5 us (31%)
  waiting for transfers between devices  12.1 us (17%)
  Pallas kernels  8.67 us (12%)
  local copies, waits for them, and re-layouts  1.2 us (2%)
  between operations  0.83 us (1%)
    all_gather x1, blocking collectives, line_body(): gathered = lax.all_gather(code, 'pcol', axis=0, tiled=True)  24.5 us
    ppermute x17, starting transfers between devices, send(): return lax.ppermute(value, AXES, found)  21.5 us
    ppermute x17, waiting for transfers between devices, send(): return lax.ppermute(value, AXES, found)  12.1 us
    pallas_call x2, Pallas kernels, sums(): call(functools.partial(sums_kernel, slots), (coded,) * outs, [SM, VM, VM]...  4.56 us
    pallas_call x1, Pallas kernels, line_body(): call(last_kernel, (shape((rows, B), bf16), shape((B, B), f32)), [SM] + [V...  1.7 us
    pallas_call x1, Pallas kernels, line_body(): call(own_kernel, shape((rows, B), f32), [SM] + [VM] * 6, [pltpu.VMEM((dep...  1.53 us
  transfers between devices with their start and end apart: 17, of which 8 were waited for; matrix products, arithmetic and copies ran while one was open for 0% of the time, Pallas kernels for 9%

profile of v6, /device:TPU:0, one launch (start us, length us, event | category | flops | bytes accessed | tf_op | source)
XLA Modules:
  0.0 69.5 jit_solution(2676485184140196775)
XLA Ops:
  0.6 0.0 copy-start
  0.6 0.0 copy-start.1
  0.6 1.1 %copy-done.1 = bf16[192,1024]{1,0:T(8,128)(2,1)S(1)} copy-done((bf16[192,1024]{1,0:T(8,128)(2,1)S(1)}, bf16[192,1024]{1,0:T(8,128)(2,1)}, u32[]{:S(2)}) %copy-start.1) | copy-done | bytes 393240
  1.8 0.0 copy-start.2
  1.8 0.4 code.1
  2.2 3.0 %collective-permute-start = (bf16[192,256]{1,0:T(8,128)(2,1)S(1)}, bf16[192,256]{1,0:T(8,128)(2,1)S(1)}, u32[]{:S(2)}, u32[]{:S(2)}) collective-permute-start(bf16[192,256]{1,0:T(8,128)(2,1)S(1)} %get-tuple-element.22), channel_id=1, source_target_pairs={{0,8},{1,9},{2,10},{3,11},{4,12},{5,13},{6,14},{7,15},{8,0},{9,1},... | collective-permute-start | bytes 294920 | tf_op jit(solution)/shard_map/ppermute | solution.py:294
  5.2 1.5 %collective-permute-start.1 = (bf16[192,256]{1,0:T(8,128)(2,1)S(1)}, bf16[192,256]{1,0:T(8,128)(2,1)S(1)}, u32[]{:S(2)}, u32[]{:S(2)}) collective-permute-start(bf16[192,256]{1,0:T(8,128)(2,1)S(1)} %get-tuple-element.23), channel_id=1, source_target_pairs={{0,16},{1,17},{2,18},{3,19},{4,20},{5,21},{6,22},{7,23},{8,24},{9,... | collective-permute-start | bytes 294920 | tf_op jit(solution)/shard_map/ppermute | solution.py:294
  6.7 0.0 collective-permute-start.2
  6.8 2.0 %collective-permute-start.3 = (bf16[192,256]{1,0:T(8,128)(2,1)S(1)}, bf16[192,256]{1,0:T(8,128)(2,1)S(1)}, u32[]{:S(2)}, u32[]{:S(2)}) collective-permute-start(bf16[192,256]{1,0:T(8,128)(2,1)S(1)} %get-tuple-element.21.own.own_ref), channel_id=1, source_target_pairs={{0,2},{1,3},{2,0},{3,1},{4,6},{5,7},{6,4},{7,5},{8,10},{9,11},{10,... | collective-permute-start | bytes 294920 | tf_op jit(solution)/shard_map/ppermute | solution.py:294
  8.8 24.5 %all-gather.1.code_ref = s16[1536,768]{1,0:T(8,128)(2,1)S(1)} all-gather(s16[192,768]{1,0:T(8,128)(2,1)S(1)} %get-tuple-element.28), channel_id=1, replica_groups=mesh['prow'=4,'pcol'=8] {'pcol'}, dimensions={0}, use_global_device_ids=true | all-gather | bytes 2654208 | tf_op jit(solution)/shard_map/all_gather | solution.py:336
  33.3 0.0 copy-done
  33.3 0.0 copy-done.2
  33.3 1.6 %sums_d.1 = s16[784,256]{1,0:T(8,128)(2,1)S(1)} custom-call(s32[4,12]{1,0:T(4,128)S(1)} %copy-done.2, bf16[768,1536]{1,0:T(8,128)(2,1)S(1)} %copy-done, s16[1536,768]{1,0:T(8,128)(2,1)S(1)} %all-gather.1.code_ref), custom_call_target="tpu_custom_call" | custom-call | flops 1 | bytes 1 | tf_op jit(solution)/shard_map/sums_d/pallas_call | solution.py:341
  35.0 0.0 collective-permute-done.x
  35.0 0.0 collective-permute-done.1.y
  35.0 0.0 collective-permute-done.2.both
  35.0 0.1 route.1
  35.1 0.0 collective-permute-done.3.one_ref
  35.1 1.0 %collective-permute-start.4 = (bf16[576,256]{1,0:T(8,128)(2,1)S(1)}, bf16[576,256]{1,0:T(8,128)(2,1)S(1)}, u32[]{:S(2)}, u32[]{:S(2)}) collective-permute-start(bf16[576,256]{1,0:T(8,128)(2,1)S(1)} %pair.1), channel_id=1, source_target_pairs={{0,4},{1,5},{2,6},{3,7},{4,0},{5,1},{6,2},{7,3},{8,12},{9,13},{10,... | collective-permute-start | bytes 884744 | tf_op jit(solution)/shard_map/ppermute | solution.py:294
  36.2 2.7 %collective-permute-start.7 = (s16[784,256]{1,0:T(8,128)(2,1)S(1)}, s16[784,256]{1,0:T(8,128)(2,1)S(1)}, u32[]{:S(2)}, u32[]{:S(2)}) collective-permute-start(s16[784,256]{1,0:T(8,128)(2,1)S(1)} %sums_d.1), channel_id=1, source_target_pairs={{0,24},{1,25},{2,26},{3,27},{4,28},{5,29},{6,30},{7,31},{8,16},{9,... | collective-permute-start | bytes 1204232 | tf_op jit(solution)/shard_map/ppermute | solution.py:294
  38.8 1.6 %collective-permute-start.10 = (bf16[192,256]{1,0:T(8,128)(2,1)S(1)}, bf16[192,256]{1,0:T(8,128)(2,1)S(1)}, u32[]{:S(2)}, u32[]{:S(2)}) collective-permute-start(bf16[192,256]{1,0:T(8,128)(2,1)S(1)} %get-tuple-element.34), channel_id=1, source_target_pairs={{0,2},{1,3},{2,0},{3,1},{4,6},{5,7},{6,4},{7,5},{8,10},{9,11},{10,... | collective-permute-start | bytes 294920 | tf_op jit(solution)/shard_map/ppermute | solution.py:294
  40.4 1.9 %collective-permute-start.11 = (bf16[192,256]{1,0:T(8,128)(2,1)S(1)}, bf16[192,256]{1,0:T(8,128)(2,1)S(1)}, u32[]{:S(2)}, u32[]{:S(2)}) collective-permute-start(bf16[192,256]{1,0:T(8,128)(2,1)S(1)} %get-tuple-element.35), channel_id=1, source_target_pairs={{0,6},{1,7},{2,4},{3,5},{4,2},{5,3},{6,0},{7,1},{8,14},{9,15},{10,... | collective-permute-start | bytes 294920 | tf_op jit(solution)/shard_map/ppermute | solution.py:294
  42.3 2.9 %sums_xy.1 = (s16[784,256]{1,0:T(8,128)(2,1)S(1)}, s16[784,256]{1,0:T(8,128)(2,1)S(1)}) custom-call(s32[4,12]{1,0:T(4,128)S(1)} %copy-done.2, bf16[768,1536]{1,0:T(8,128)(2,1)S(1)} %copy-done, s16[1536,768]{1,0:T(8,128)(2,1)S(1)} %all-gather.1.code_ref), custom_call_target="tpu_custom_call" | custom-call | flops 1 | bytes 1 | tf_op jit(solution)/shard_map/sums_xy/pallas_call | solution.py:341
  45.2 1.1 %collective-permute-start.8 = (s16[784,256]{1,0:T(8,128)(2,1)S(1)}, s16[784,256]{1,0:T(8,128)(2,1)S(1)}, u32[]{:S(2)}, u32[]{:S(2)}) collective-permute-start(s16[784,256]{1,0:T(8,128)(2,1)S(1)} %get-tuple-element.31), channel_id=1, source_target_pairs={{0,8},{1,9},{2,10},{3,11},{4,12},{5,13},{6,14},{7,15},{8,0},{9,1},... | collective-permute-start | bytes 1204232 | tf_op jit(solution)/shard_map/ppermute | solution.py:294
  46.3 0.0 collective-permute-done.10.one
  46.3 1.2 %collective-permute-start.9 = (s16[784,256]{1,0:T(8,128)(2,1)S(1)}, s16[784,256]{1,0:T(8,128)(2,1)S(1)}, u32[]{:S(2)}, u32[]{:S(2)}) collective-permute-start(s16[784,256]{1,0:T(8,128)(2,1)S(1)} %get-tuple-element.32), channel_id=1, source_target_pairs={{0,16},{1,17},{2,18},{3,19},{4,20},{5,21},{6,22},{7,23},{8,24},{9,... | collective-permute-start | bytes 1204232 | tf_op jit(solution)/shard_map/ppermute | solution.py:294
  47.5 1.6 %collective-permute-done.11.three = bf16[192,256]{1,0:T(8,128)(2,1)S(1)} collective-permute-done((bf16[192,256]{1,0:T(8,128)(2,1)S(1)}, bf16[192,256]{1,0:T(8,128)(2,1)S(1)}, u32[]{:S(2)}, u32[]{:S(2)}) %collective-permute-start.11) | collective-permute-done | bytes 98336 | tf_op jit(solution)/shard_map/ppermute | solution.py:294
  49.1 0.0 collective-permute-start.5
  49.1 4.1 %collective-permute-done.4.two = bf16[576,256]{1,0:T(8,128)(2,1)S(1)} collective-permute-done((bf16[576,256]{1,0:T(8,128)(2,1)S(1)}, bf16[576,256]{1,0:T(8,128)(2,1)S(1)}, u32[]{:S(2)}, u32[]{:S(2)}) %collective-permute-start.4) | collective-permute-done | bytes 294944 | tf_op jit(solution)/shard_map/ppermute | solution.py:294
  53.3 0.1 share.1
  53.4 0.1 collective-permute-start.12
  53.5 0.0 collective-permute-done.7.came_ref
  53.5 0.6 collective-permute-start.6
  54.0 0.1 base.1.base_ref
  54.1 0.8 %collective-permute-done.12.came = bf16[384,256]{1,0:T(8,128)(2,1)S(1)} collective-permute-done((bf16[384,256]{1,0:T(8,128)(2,1)S(1)}, bf16[384,256]{1,0:T(8,128)(2,1)S(1)}, u32[]{:S(2)}, u32[]{:S(2)}) %collective-permute-start.12) | collective-permute-done | bytes 196640 | tf_op jit(solution)/shard_map/ppermute | solution.py:294
  54.9 0.2 turn.1.lower
  55.1 0.0 collective-permute-done.5.their_pair
  55.1 0.1 collective-permute-done.6.their_two
  55.1 1.5 %own.1.own_ref = f32[768,256]{1,0:T(8,128)S(1)} custom-call(s32[4,12]{1,0:T(4,128)S(1)} %copy-done.2, bf16[768,1536]{1,0:T(8,128)(2,1)S(1)} %copy-done, bf16[384,256]{1,0:T(8,128)(2,1)S(1)} %slice.38.pair, bf16[384,256]{1,0:T(8,128)(2,1)S(1)} %slice.39.two, bf16[384,256]{1,0:T(8,128)(2,1)S(1)} %collective-permute-done.5.their_pair, ...), custom_call_target="tpu_custom_call" | custom-call | flops 1 | bytes 1 | tf_op jit(solution)/shard_map/own/pallas_call | solution.py:371
  56.7 0.0 copy-start.3
  56.7 0.7 collective-permute-done.8.came_x
  57.3 0.0 collective-permute-done.9.came_y
  57.3 1.7 %last.1 = (bf16[768,256]{1,0:T(8,128)(2,1)}, f32[256,256]{1,0:T(8,128)S(1)}) custom-call(s32[4,12]{1,0:T(4,128)S(1)} %copy-done.2, f32[768,256]{1,0:T(8,128)S(1)} %own.1.own_ref, s16[784,256]{1,0:T(8,128)(2,1)S(1)} %collective-permute-done.8.came_x, s16[784,256]{1,0:T(8,128)(2,1)S(1)} %collective-permute-done.9.came_y, bf16[256,768]{1,0:T(8,128)(2,1)S(1)} %turn.1.lower), custom_call_target="tpu_custom_call" | custom-call | flops 201326592 | bytes 1572864 | tf_op jit(solution)/shard_map/last/pallas_call | solution.py:393
  59.1 0.1 collective-permute-start.13
  59.1 1.3 %collective-permute-done.13 = f32[128,256]{1,0:T(8,128)S(1)} collective-permute-done((f32[128,256]{1,0:T(8,128)S(1)}, f32[128,256]{1,0:T(8,128)S(1)}, u32[]{:S(2)}, u32[]{:S(2)}) %collective-permute-start.13) | collective-permute-done | bytes 131104 | tf_op jit(solution)/shard_map/ppermute | solution.py:294
  60.5 2.4 %collective-permute-start.15 = (f32[64,256]{1,0:T(8,128)S(1)}, f32[64,256]{1,0:T(8,128)S(1)}, u32[]{:S(2)}, u32[]{:S(2)}) collective-permute-start(f32[64,256]{1,0:T(8,128)S(1)} %slice.42), channel_id=1, source_target_pairs={{0,2},{1,5},{2,0},{3,7},{4,6},{5,1},{6,4},{7,3},{8,10},{9,13},{10,... | collective-permute-start | bytes 196616 | tf_op jit(solution)/shard_map/ppermute | solution.py:294
  62.9 2.4 %collective-permute-start.14 = (f32[32,256]{1,0:T(8,128)S(1)}, f32[32,256]{1,0:T(8,128)S(1)}, u32[]{:S(2)}, u32[]{:S(2)}) collective-permute-start(f32[32,256]{1,0:T(8,128)S(1)} %slice.41), channel_id=1, source_target_pairs={{0,6},{1,7},{2,4},{3,5},{4,2},{5,3},{6,0},{7,1},{8,14},{9,15},{10,... | collective-permute-start | bytes 98312 | tf_op jit(solution)/shard_map/ppermute | solution.py:294
  65.3 0.5 collective-permute-done.15
  65.8 0.0 collective-permute-start.16
  65.8 3.0 %collective-permute-done.14 = f32[32,256]{1,0:T(8,128)S(1)} collective-permute-done((f32[32,256]{1,0:T(8,128)S(1)}, f32[32,256]{1,0:T(8,128)S(1)}, u32[]{:S(2)}, u32[]{:S(2)}) %collective-permute-start.14) | collective-permute-done | bytes 32800 | tf_op jit(solution)/shard_map/ppermute | solution.py:294
  68.9 0.0 collective-permute-done.16
  68.9 0.0 copy-done.3
  68.9 0.6 fusion.2
  (8 shorter events, 0.1 us)
Async XLA Ops:
  0.6 32.7 %copy-start = (bf16[768,1536]{1,0:T(8,128)(2,1)S(1)}, bf16[768,1536]{1,0:T(8,128)(2,1)}, u32[]{:S(2)}) copy-start(bf16[768,1536]{1,0:T(8,128)(2,1)} %a_ref.5) | copy-start | bytes 7077892
  0.6 1.1 %copy-start.1 = (bf16[192,1024]{1,0:T(8,128)(2,1)S(1)}, bf16[192,1024]{1,0:T(8,128)(2,1)}, u32[]{:S(2)}) copy-start(bf16[192,1024]{1,0:T(8,128)(2,1)} %lower_ref.1) | copy-start | bytes 1179652
  1.8 31.6 %copy-start.2 = (s32[4,12]{1,0:T(4,128)S(1)}, s32[4,12]{1,0:T(4,128)}, u32[]{:S(2)}) copy-start(s32[4,12]{1,0:T(4,128)} %struct_ref.6) | copy-start | bytes 580
  2.2 32.8 %collective-permute-start = (bf16[192,256]{1,0:T(8,128)(2,1)S(1)}, bf16[192,256]{1,0:T(8,128)(2,1)S(1)}, u32[]{:S(2)}, u32[]{:S(2)}) collective-permute-start(bf16[192,256]{1,0:T(8,128)(2,1)S(1)} %get-tuple-element.22), channel_id=1, source_target_pairs={{0,8},{1,9},{2,10},{3,11},{4,12},{5,13},{6,14},{7,15},{8,0},{9,1},... | collective-permute-start | bytes 294920 | tf_op jit(solution)/shard_map/ppermute | solution.py:294
  5.2 29.8 %collective-permute-start.1 = (bf16[192,256]{1,0:T(8,128)(2,1)S(1)}, bf16[192,256]{1,0:T(8,128)(2,1)S(1)}, u32[]{:S(2)}, u32[]{:S(2)}) collective-permute-start(bf16[192,256]{1,0:T(8,128)(2,1)S(1)} %get-tuple-element.23), channel_id=1, source_target_pairs={{0,16},{1,17},{2,18},{3,19},{4,20},{5,21},{6,22},{7,23},{8,24},{9,... | collective-permute-start | bytes 294920 | tf_op jit(solution)/shard_map/ppermute | solution.py:294
  6.7 28.3 %collective-permute-start.2 = (bf16[192,256]{1,0:T(8,128)(2,1)S(1)}, bf16[192,256]{1,0:T(8,128)(2,1)S(1)}, u32[]{:S(2)}, u32[]{:S(2)}) collective-permute-start(bf16[192,256]{1,0:T(8,128)(2,1)S(1)} %get-tuple-element.24), channel_id=1, source_target_pairs={{0,24},{1,25},{2,26},{3,27},{4,28},{5,29},{6,30},{7,31},{8,16},{9,... | collective-permute-start | bytes 294920 | tf_op jit(solution)/shard_map/ppermute | solution.py:294
  6.8 28.3 %collective-permute-start.3 = (bf16[192,256]{1,0:T(8,128)(2,1)S(1)}, bf16[192,256]{1,0:T(8,128)(2,1)S(1)}, u32[]{:S(2)}, u32[]{:S(2)}) collective-permute-start(bf16[192,256]{1,0:T(8,128)(2,1)S(1)} %get-tuple-element.21.own.own_ref), channel_id=1, source_target_pairs={{0,2},{1,3},{2,0},{3,1},{4,6},{5,7},{6,4},{7,5},{8,10},{9,11},{10,... | collective-permute-start | bytes 294920 | tf_op jit(solution)/shard_map/ppermute | solution.py:294
  35.1 18.1 %collective-permute-start.4 = (bf16[576,256]{1,0:T(8,128)(2,1)S(1)}, bf16[576,256]{1,0:T(8,128)(2,1)S(1)}, u32[]{:S(2)}, u32[]{:S(2)}) collective-permute-start(bf16[576,256]{1,0:T(8,128)(2,1)S(1)} %pair.1), channel_id=1, source_target_pairs={{0,4},{1,5},{2,6},{3,7},{4,0},{5,1},{6,2},{7,3},{8,12},{9,13},{10,... | collective-permute-start | bytes 884744 | tf_op jit(solution)/shard_map/ppermute | solution.py:294
  36.2 17.3 %collective-permute-start.7 = (s16[784,256]{1,0:T(8,128)(2,1)S(1)}, s16[784,256]{1,0:T(8,128)(2,1)S(1)}, u32[]{:S(2)}, u32[]{:S(2)}) collective-permute-start(s16[784,256]{1,0:T(8,128)(2,1)S(1)} %sums_d.1), channel_id=1, source_target_pairs={{0,24},{1,25},{2,26},{3,27},{4,28},{5,29},{6,30},{7,31},{8,16},{9,... | collective-permute-start | bytes 1204232 | tf_op jit(solution)/shard_map/ppermute | solution.py:294
  38.8 7.5 %collective-permute-start.10 = (bf16[192,256]{1,0:T(8,128)(2,1)S(1)}, bf16[192,256]{1,0:T(8,128)(2,1)S(1)}, u32[]{:S(2)}, u32[]{:S(2)}) collective-permute-start(bf16[192,256]{1,0:T(8,128)(2,1)S(1)} %get-tuple-element.34), channel_id=1, source_target_pairs={{0,2},{1,3},{2,0},{3,1},{4,6},{5,7},{6,4},{7,5},{8,10},{9,11},{10,... | collective-permute-start | bytes 294920 | tf_op jit(solution)/shard_map/ppermute | solution.py:294
  40.4 8.7 %collective-permute-start.11 = (bf16[192,256]{1,0:T(8,128)(2,1)S(1)}, bf16[192,256]{1,0:T(8,128)(2,1)S(1)}, u32[]{:S(2)}, u32[]{:S(2)}) collective-permute-start(bf16[192,256]{1,0:T(8,128)(2,1)S(1)} %get-tuple-element.35), channel_id=1, source_target_pairs={{0,6},{1,7},{2,4},{3,5},{4,2},{5,3},{6,0},{7,1},{8,14},{9,15},{10,... | collective-permute-start | bytes 294920 | tf_op jit(solution)/shard_map/ppermute | solution.py:294
  45.2 12.1 %collective-permute-start.8 = (s16[784,256]{1,0:T(8,128)(2,1)S(1)}, s16[784,256]{1,0:T(8,128)(2,1)S(1)}, u32[]{:S(2)}, u32[]{:S(2)}) collective-permute-start(s16[784,256]{1,0:T(8,128)(2,1)S(1)} %get-tuple-element.31), channel_id=1, source_target_pairs={{0,8},{1,9},{2,10},{3,11},{4,12},{5,13},{6,14},{7,15},{8,0},{9,1},... | collective-permute-start | bytes 1204232 | tf_op jit(solution)/shard_map/ppermute | solution.py:294
  46.3 11.0 %collective-permute-start.9 = (s16[784,256]{1,0:T(8,128)(2,1)S(1)}, s16[784,256]{1,0:T(8,128)(2,1)S(1)}, u32[]{:S(2)}, u32[]{:S(2)}) collective-permute-start(s16[784,256]{1,0:T(8,128)(2,1)S(1)} %get-tuple-element.32), channel_id=1, source_target_pairs={{0,16},{1,17},{2,18},{3,19},{4,20},{5,21},{6,22},{7,23},{8,24},{9,... | collective-permute-start | bytes 1204232 | tf_op jit(solution)/shard_map/ppermute | solution.py:294
  49.1 5.9 %collective-permute-start.5 = (bf16[384,256]{1,0:T(8,128)(2,1)S(1)}, bf16[384,256]{1,0:T(8,128)(2,1)S(1)}, u32[]{:S(2)}, u32[]{:S(2)}) collective-permute-start(bf16[384,256]{1,0:T(8,128)(2,1)S(1)} %slice.38.pair), channel_id=1, source_target_pairs={{0,1},{1,0},{2,3},{3,2},{4,5},{5,4},{6,7},{7,6},{8,9},{9,8},{10,11... | collective-permute-start | bytes 589832 | tf_op jit(solution)/shard_map/ppermute | solution.py:294
  53.4 1.5 %collective-permute-start.12 = (bf16[384,256]{1,0:T(8,128)(2,1)S(1)}, bf16[384,256]{1,0:T(8,128)(2,1)S(1)}, u32[]{:S(2)}, u32[]{:S(2)}) collective-permute-start(bf16[384,256]{1,0:T(8,128)(2,1)S(1)} %get-tuple-element.37), channel_id=1, source_target_pairs={{0,1},{1,0},{2,3},{3,2},{4,5},{5,4},{6,7},{7,6},{8,9},{9,8},{10,11... | collective-permute-start | bytes 589832 | tf_op jit(solution)/shard_map/ppermute | solution.py:294
  53.5 1.7 %collective-permute-start.6 = (bf16[384,256]{1,0:T(8,128)(2,1)S(1)}, bf16[384,256]{1,0:T(8,128)(2,1)S(1)}, u32[]{:S(2)}, u32[]{:S(2)}) collective-permute-start(bf16[384,256]{1,0:T(8,128)(2,1)S(1)} %slice.39.two), channel_id=1, source_target_pairs={{0,1},{1,0},{2,3},{3,2},{4,5},{5,4},{6,7},{7,6},{8,9},{9,8},{10,11... | collective-permute-start | bytes 589832 | tf_op jit(solution)/shard_map/ppermute | solution.py:294
  56.7 12.2 %copy-start.3 = (f32[32,256]{1,0:T(8,128)S(1)}, f32[32,256]{1,0:T(8,128)}, u32[]{:S(2)}) copy-start(f32[32,256]{1,0:T(8,128)} %param.6) | copy-start | bytes 98308
  59.1 1.4 %collective-permute-start.13 = (f32[128,256]{1,0:T(8,128)S(1)}, f32[128,256]{1,0:T(8,128)S(1)}, u32[]{:S(2)}, u32[]{:S(2)}) collective-permute-start(f32[128,256]{1,0:T(8,128)S(1)} %slice.32), channel_id=1, source_target_pairs={{0,1},{1,0},{2,3},{3,2},{4,5},{5,4},{6,7},{7,6},{8,9},{9,8},{10,11... | collective-permute-start | bytes 393224 | tf_op jit(solution)/shard_map/ppermute | solution.py:294
  60.5 5.3 %collective-permute-start.15 = (f32[64,256]{1,0:T(8,128)S(1)}, f32[64,256]{1,0:T(8,128)S(1)}, u32[]{:S(2)}, u32[]{:S(2)}) collective-permute-start(f32[64,256]{1,0:T(8,128)S(1)} %slice.42), channel_id=1, source_target_pairs={{0,2},{1,5},{2,0},{3,7},{4,6},{5,1},{6,4},{7,3},{8,10},{9,13},{10,... | collective-permute-start | bytes 196616 | tf_op jit(solution)/shard_map/ppermute | solution.py:294
  62.9 6.0 %collective-permute-start.14 = (f32[32,256]{1,0:T(8,128)S(1)}, f32[32,256]{1,0:T(8,128)S(1)}, u32[]{:S(2)}, u32[]{:S(2)}) collective-permute-start(f32[32,256]{1,0:T(8,128)S(1)} %slice.41), channel_id=1, source_target_pairs={{0,6},{1,7},{2,4},{3,5},{4,2},{5,3},{6,0},{7,1},{8,14},{9,15},{10,... | collective-permute-start | bytes 98312 | tf_op jit(solution)/shard_map/ppermute | solution.py:294
  65.8 3.0 %collective-permute-start.16 = (f32[32,256]{1,0:T(8,128)S(1)}, f32[32,256]{1,0:T(8,128)S(1)}, u32[]{:S(2)}, u32[]{:S(2)}) collective-permute-start(f32[32,256]{1,0:T(8,128)S(1)} %slice_select_fusion), channel_id=1, source_target_pairs={{0,1},{1,0},{2,3},{3,2},{4,5},{5,4},{6,7},{7,6},{8,9},{9,8},{10,11... | collective-permute-start | bytes 98312 | tf_op jit(solution)/shard_map/ppermute | solution.py:294

commit v7 on v6

--- a/solution.py
+++ b/solution.py
@@ -189,34 +189,36 @@
         out_ref[at * shard : (at + 1) * shard] = ref[...]
 
 
-def base_kernel(came_ref, base_ref):
+def base_kernel(came_ref, near_ref, base_ref):
     blocks = base_ref.shape[0] // B
     step = came_step(came_ref, blocks)
     for b in range(blocks):
         rows = slice(b * B, (b + 1) * B)
-        base_ref[rows] = from_code(came_ref[rows]) * step[b : b + 1]
-
-
-def own_kernel(
-    struct_ref, a_ref, pair, two, their_pair, their_two, base_ref, own_ref, panel
-):
+        base_ref[rows] = near_ref[rows] + from_code(came_ref[rows]) * step[b : b + 1]
+
+
+def own_kernel(far, struct_ref, a_ref, mine, theirs, *refs):
+    own_ref, panel = refs[-2:]
     p, z, c = place()
-    shard = panel.shape[0] // 8
-    for flip in range(4):
-        for refs, core in (((pair, two), c), ((their_pair, their_two), 1 - c)):
-            at = pl.multiple_of((2 * (z ^ flip) + core) * shard, FINE)
-            part = slice((flip % 2) * shard, (flip % 2 + 1) * shard)
-            panel[pl.ds(at, shard)] = refs[flip // 2][part]
+    shard = mine.shape[0] // 2
+    half = (z // 2) ^ far
+    for i in range(2):
+        chip = ((z ^ i) % 2) * 2
+        for ref, core in ((mine, c), (theirs, 1 - c)):
+            at = pl.multiple_of((chip + core) * shard, FINE)
+            panel[pl.ds(at, shard)] = ref[i * shard : (i + 1) * shard]
     blocks = panel.shape[0] // B
     for block in range(blocks):
-
-        @pl.when(jnp.logical_not(is_member(struct_ref, p, p * blocks + block)))
+        listed = is_member(struct_ref, p, (2 * p + half) * blocks + block)
+
+        @pl.when(jnp.logical_not(listed))
         def _(block=block):
             panel[block * B : (block + 1) * B] = jnp.zeros((B, B), jnp.bfloat16)
 
-    own_ref[...] = base_ref[...] - jnp.dot(
-        a_ref[...], panel[...], preferred_element_type=jnp.float32
-    )
+    depth = panel.shape[0]
+    columns = a_ref[:, pl.ds(pl.multiple_of(half * depth, depth), depth)]
+    total = -jnp.dot(columns, panel[...], preferred_element_type=jnp.float32)
+    own_ref[...] = total + refs[0][...] if far else total
 
 
 def route_kernel(own, x, y, both, *outs):
@@ -354,7 +356,6 @@
         ((1, 1), (2, 2)), 2, "sums_xy", after(struct_list, part_d), ancestor_inverse, gathered
     )
     came_x = send(part_x, across(1))
-    came_y = send(part_y, across(2))
     stay, to_one, to_two, to_three = small(
         route_kernel, (piece,) * 4, "route", keep, rows_x, rows_y, rows_both, flops=8 * 10**9
     )
@@ -366,17 +367,22 @@
     from_two = send(trio, along(2))
     pair, two = trio[shard:], from_two[shard:]
     their_pair = send(pair, chip_swap)
+    def own_half(far, *args, flops=1):
+        return call(
+            functools.partial(own_kernel, far),
+            shape((rows, B), f32),
+            [SM] + [VM] * (1 + len(args)),
+            [pltpu.VMEM((depth // 2, B), bf16)],
+            flops,
+            1,
+            "own",
+        )(struct_list, ancestor_inverse, *args)
+
+    near_own = own_half(0, pair, their_pair)
+    came_y = send(after(part_y, near_own), across(2))
     from_three = send(to_three, along(3))
-    base = small(base_kernel, shape((rows, B), f32), "base", came_d, flops=4 * 10**9)
-    own = call(
-        own_kernel,
-        shape((rows, B), f32),
-        [SM] + [VM] * 6,
-        [pltpu.VMEM((depth, B), bf16)],
-        1,
-        1,
-        "own",
-    )(struct_list, ancestor_inverse, pair, two, their_pair, send(two, chip_swap), base)
+    base = small(base_kernel, shape((rows, B), f32), "base", came_d, near_own, flops=4 * 10**9)
+    own = own_half(1, two, send(two, chip_swap), base)
     half_rows = shape((2 * shard, B), bf16)
     keep, give = small(
         share_kernel, (half_rows, half_rows), "share", stay, from_one, from_two, from_three, flops=2 * 10**9

time: 69.6 us -> 69 us (level)
  starting transfers between devices: 21.5 us -> 19.6 us
  Pallas kernels: 8.67 us -> 9.47 us
    ppermute x17, starting transfers between devices: 21.5 us -> 19.6 us  [send(): return lax.ppermute(value, AXES, found)]
    pallas_call x1 -> x2, Pallas kernels: 1.53 us -> 2.3 us  [own_half(): call(functools.partial(own_kernel, far), shape((rows, B), f32), [SM] + [V...]
  transfers between devices with their start and end apart: 17 -> 17, of which waited for: 8 -> 9; matrix products, arithmetic and copies ran while one was open for 0% -> 0% of each run, Pallas kernels for 9% -> 11%
where the time goes in v7:
time: 69 us; the launch traced here: 68.9 us
  blocking collectives  24.5 us (36%)
  starting transfers between devices  19.6 us (28%)
  waiting for transfers between devices  12.6 us (18%)
  Pallas kernels  9.47 us (14%)
  local copies, waits for them, and re-layouts  1.2 us (2%)
  between operations  0.84 us (1%)
    all_gather x1, blocking collectives, line_body(): gathered = lax.all_gather(code, 'pcol', axis=0, tiled=True)  24.5 us
    ppermute x17, starting transfers between devices, send(): return lax.ppermute(value, AXES, found)  19.6 us
    ppermute x17, waiting for transfers between devices, send(): return lax.ppermute(value, AXES, found)  12.6 us
    pallas_call x2, Pallas kernels, sums(): call(functools.partial(sums_kernel, slots), (coded,) * outs, [SM, VM, VM]...  4.56 us
    pallas_call x2, Pallas kernels, own_half(): call(functools.partial(own_kernel, far), shape((rows, B), f32), [SM] + [V...  2.3 us
    pallas_call x1, Pallas kernels, line_body(): call(last_kernel, (shape((rows, B), bf16), shape((B, B), f32)), [SM] + [V...  1.71 us
  transfers between devices with their start and end apart: 17, of which 9 were waited for; matrix products, arithmetic and copies ran while one was open for 0% of the time, Pallas kernels for 11%

profile of v7, /device:TPU:0, one launch (start us, length us, event | category | flops | bytes accessed | tf_op | source)
XLA Modules:
  0.0 68.9 jit_solution(3895727423667781654)
XLA Ops:
  0.6 0.0 copy-start
  0.6 0.0 copy-start.1
  0.6 1.1 %copy-done.1 = bf16[192,1024]{1,0:T(8,128)(2,1)S(1)} copy-done((bf16[192,1024]{1,0:T(8,128)(2,1)S(1)}, bf16[192,1024]{1,0:T(8,128)(2,1)}, u32[]{:S(2)}) %copy-start.1) | copy-done | bytes 393240
  1.8 0.0 copy-start.2
  1.8 0.4 code.1
  2.2 3.0 %collective-permute-start = (bf16[192,256]{1,0:T(8,128)(2,1)S(1)}, bf16[192,256]{1,0:T(8,128)(2,1)S(1)}, u32[]{:S(2)}, u32[]{:S(2)}) collective-permute-start(bf16[192,256]{1,0:T(8,128)(2,1)S(1)} %get-tuple-element.23), channel_id=1, source_target_pairs={{0,8},{1,9},{2,10},{3,11},{4,12},{5,13},{6,14},{7,15},{8,0},{9,1},... | collective-permute-start | bytes 294920 | tf_op jit(solution)/shard_map/ppermute | solution.py:296
  5.2 1.5 %collective-permute-start.1 = (bf16[192,256]{1,0:T(8,128)(2,1)S(1)}, bf16[192,256]{1,0:T(8,128)(2,1)S(1)}, u32[]{:S(2)}, u32[]{:S(2)}) collective-permute-start(bf16[192,256]{1,0:T(8,128)(2,1)S(1)} %get-tuple-element.24), channel_id=1, source_target_pairs={{0,16},{1,17},{2,18},{3,19},{4,20},{5,21},{6,22},{7,23},{8,24},{9,... | collective-permute-start | bytes 294920 | tf_op jit(solution)/shard_map/ppermute | solution.py:296
  6.7 0.0 collective-permute-start.2
  6.8 2.0 %collective-permute-start.3 = (bf16[192,256]{1,0:T(8,128)(2,1)S(1)}, bf16[192,256]{1,0:T(8,128)(2,1)S(1)}, u32[]{:S(2)}, u32[]{:S(2)}) collective-permute-start(bf16[192,256]{1,0:T(8,128)(2,1)S(1)} %get-tuple-element.22.own.own_ref), channel_id=1, source_target_pairs={{0,2},{1,3},{2,0},{3,1},{4,6},{5,7},{6,4},{7,5},{8,10},{9,11},{10,... | collective-permute-start | bytes 294920 | tf_op jit(solution)/shard_map/ppermute | solution.py:296
  8.8 24.5 %all-gather.1.code_ref = s16[1536,768]{1,0:T(8,128)(2,1)S(1)} all-gather(s16[192,768]{1,0:T(8,128)(2,1)S(1)} %get-tuple-element.29), channel_id=1, replica_groups=mesh['prow'=4,'pcol'=8] {'pcol'}, dimensions={0}, use_global_device_ids=true | all-gather | bytes 2654208 | tf_op jit(solution)/shard_map/all_gather | solution.py:338
  33.3 0.0 copy-done
  33.3 0.0 copy-done.2
  33.3 1.6 %sums_d.1 = s16[784,256]{1,0:T(8,128)(2,1)S(1)} custom-call(s32[4,12]{1,0:T(4,128)S(1)} %copy-done.2, bf16[768,1536]{1,0:T(8,128)(2,1)S(1)} %copy-done, s16[1536,768]{1,0:T(8,128)(2,1)S(1)} %all-gather.1.code_ref), custom_call_target="tpu_custom_call" | custom-call | flops 1 | bytes 1 | tf_op jit(solution)/shard_map/sums_d/pallas_call | solution.py:343
  35.0 0.0 collective-permute-done.x
  35.0 0.0 collective-permute-done.1.y
  35.0 0.0 collective-permute-done.2.both
  35.0 0.1 route.1
  35.1 0.0 collective-permute-done.3.one_ref
  35.1 1.0 %collective-permute-start.4 = (bf16[576,256]{1,0:T(8,128)(2,1)S(1)}, bf16[576,256]{1,0:T(8,128)(2,1)S(1)}, u32[]{:S(2)}, u32[]{:S(2)}) collective-permute-start(bf16[576,256]{1,0:T(8,128)(2,1)S(1)} %pair.1), channel_id=1, source_target_pairs={{0,4},{1,5},{2,6},{3,7},{4,0},{5,1},{6,2},{7,3},{8,12},{9,13},{10,... | collective-permute-start | bytes 884744 | tf_op jit(solution)/shard_map/ppermute | solution.py:296
  36.2 3.0 %collective-permute-start.6 = (s16[784,256]{1,0:T(8,128)(2,1)S(1)}, s16[784,256]{1,0:T(8,128)(2,1)S(1)}, u32[]{:S(2)}, u32[]{:S(2)}) collective-permute-start(s16[784,256]{1,0:T(8,128)(2,1)S(1)} %sums_d.1), channel_id=1, source_target_pairs={{0,24},{1,25},{2,26},{3,27},{4,28},{5,29},{6,30},{7,31},{8,16},{9,... | collective-permute-start | bytes 1204232 | tf_op jit(solution)/shard_map/ppermute | solution.py:296
  39.2 0.1 collective-permute-start.7
  39.3 1.6 %collective-permute-start.10 = (bf16[192,256]{1,0:T(8,128)(2,1)S(1)}, bf16[192,256]{1,0:T(8,128)(2,1)S(1)}, u32[]{:S(2)}, u32[]{:S(2)}) collective-permute-start(bf16[192,256]{1,0:T(8,128)(2,1)S(1)} %get-tuple-element.36), channel_id=1, source_target_pairs={{0,2},{1,3},{2,0},{3,1},{4,6},{5,7},{6,4},{7,5},{8,10},{9,11},{10,... | collective-permute-start | bytes 294920 | tf_op jit(solution)/shard_map/ppermute | solution.py:296
  40.9 1.9 %collective-permute-start.11 = (bf16[192,256]{1,0:T(8,128)(2,1)S(1)}, bf16[192,256]{1,0:T(8,128)(2,1)S(1)}, u32[]{:S(2)}, u32[]{:S(2)}) collective-permute-start(bf16[192,256]{1,0:T(8,128)(2,1)S(1)} %get-tuple-element.37), channel_id=1, source_target_pairs={{0,6},{1,7},{2,4},{3,5},{4,2},{5,3},{6,0},{7,1},{8,14},{9,15},{10,... | collective-permute-start | bytes 294920 | tf_op jit(solution)/shard_map/ppermute | solution.py:296
  42.8 2.9 %sums_xy.1 = (s16[784,256]{1,0:T(8,128)(2,1)S(1)}, s16[784,256]{1,0:T(8,128)(2,1)S(1)}) custom-call(s32[4,12]{1,0:T(4,128)S(1)} %copy-done.2, bf16[768,1536]{1,0:T(8,128)(2,1)S(1)} %copy-done, s16[1536,768]{1,0:T(8,128)(2,1)S(1)} %all-gather.1.code_ref), custom_call_target="tpu_custom_call" | custom-call | flops 1 | bytes 1 | tf_op jit(solution)/shard_map/sums_xy/pallas_call | solution.py:343
  45.7 0.0 collective-permute-done.7.theirs
  45.8 0.1 collective-permute-start.8
  45.8 1.1 %own.2.near_ref = f32[768,256]{1,0:T(8,128)S(1)} custom-call(s32[4,12]{1,0:T(4,128)S(1)} %copy-done.2, bf16[768,1536]{1,0:T(8,128)(2,1)S(1)} %copy-done, bf16[384,256]{1,0:T(8,128)(2,1)S(1)} %slice.39.mine, bf16[384,256]{1,0:T(8,128)(2,1)S(1)} %collective-permute-done.7.theirs), custom_call_target="tpu_custom_call" | custom-call | flops 1 | bytes 1 | tf_op jit(solution)/shard_map/own/pallas_call | solution.py:371
  47.0 0.0 collective-permute-done.10.one
  47.0 1.2 %collective-permute-start.9 = (s16[784,256]{1,0:T(8,128)(2,1)S(1)}, s16[784,256]{1,0:T(8,128)(2,1)S(1)}, u32[]{:S(2)}, u32[]{:S(2)}) collective-permute-start(s16[784,256]{1,0:T(8,128)(2,1)S(1)} %get-tuple-element.34), channel_id=1, source_target_pairs={{0,16},{1,17},{2,18},{3,19},{4,20},{5,21},{6,22},{7,23},{8,24},{9,... | collective-permute-start | bytes 1204232 | tf_op jit(solution)/shard_map/ppermute | solution.py:296
  48.2 0.9 %collective-permute-done.11.three = bf16[192,256]{1,0:T(8,128)(2,1)S(1)} collective-permute-done((bf16[192,256]{1,0:T(8,128)(2,1)S(1)}, bf16[192,256]{1,0:T(8,128)(2,1)S(1)}, u32[]{:S(2)}, u32[]{:S(2)}) %collective-permute-start.11) | collective-permute-done | bytes 98336 | tf_op jit(solution)/shard_map/ppermute | solution.py:296
  49.1 4.1 %collective-permute-done.4.two = bf16[576,256]{1,0:T(8,128)(2,1)S(1)} collective-permute-done((bf16[576,256]{1,0:T(8,128)(2,1)S(1)}, bf16[576,256]{1,0:T(8,128)(2,1)S(1)}, u32[]{:S(2)}, u32[]{:S(2)}) %collective-permute-start.4) | collective-permute-done | bytes 294944 | tf_op jit(solution)/shard_map/ppermute | solution.py:296
  53.3 0.1 share.1
  53.4 0.1 collective-permute-start.12
  53.5 0.6 collective-permute-start.5
  54.0 0.0 collective-permute-done.6.came_ref
  54.0 0.1 base.1.refs_0_
  54.1 0.7 %collective-permute-done.12.came = bf16[384,256]{1,0:T(8,128)(2,1)S(1)} collective-permute-done((bf16[384,256]{1,0:T(8,128)(2,1)S(1)}, bf16[384,256]{1,0:T(8,128)(2,1)S(1)}, u32[]{:S(2)}, u32[]{:S(2)}) %collective-permute-start.12) | collective-permute-done | bytes 196640 | tf_op jit(solution)/shard_map/ppermute | solution.py:296
  54.9 0.2 turn.1.lower
  55.1 0.1 collective-permute-done.5.theirs
  55.1 1.2 %own.3.own_ref = f32[768,256]{1,0:T(8,128)S(1)} custom-call(s32[4,12]{1,0:T(4,128)S(1)} %copy-done.2, bf16[768,1536]{1,0:T(8,128)(2,1)S(1)} %copy-done, bf16[384,256]{1,0:T(8,128)(2,1)S(1)} %slice.38.mine, bf16[384,256]{1,0:T(8,128)(2,1)S(1)} %collective-permute-done.5.theirs, f32[768,256]{1,0:T(8,128)S(1)} %base.1.refs_0_), custom_call_target="tpu_custom_call" | custom-call | flops 1 | bytes 1 | tf_op jit(solution)/shard_map/own/pallas_call | solution.py:371
  56.3 0.0 copy-start.3
  56.3 0.7 collective-permute-done.8.came_x
  57.0 1.2 %collective-permute-done.9.came_y = s16[784,256]{1,0:T(8,128)(2,1)S(1)} collective-permute-done((s16[784,256]{1,0:T(8,128)(2,1)S(1)}, s16[784,256]{1,0:T(8,128)(2,1)S(1)}, u32[]{:S(2)}, u32[]{:S(2)}) %collective-permute-start.9) | collective-permute-done | bytes 401440 | tf_op jit(solution)/shard_map/ppermute | solution.py:296
  58.2 1.7 %last.1 = (bf16[768,256]{1,0:T(8,128)(2,1)}, f32[256,256]{1,0:T(8,128)S(1)}) custom-call(s32[4,12]{1,0:T(4,128)S(1)} %copy-done.2, f32[768,256]{1,0:T(8,128)S(1)} %own.3.own_ref, s16[784,256]{1,0:T(8,128)(2,1)S(1)} %collective-permute-done.8.came_x, s16[784,256]{1,0:T(8,128)(2,1)S(1)} %collective-permute-done.9.came_y, bf16[256,768]{1,0:T(8,128)(2,1)S(1)} %turn.1.lower), custom_call_target="tpu_custom_call" | custom-call | flops 201326592 | bytes 1572864 | tf_op jit(solution)/shard_map/last/pallas_call | solution.py:399
  59.9 0.1 collective-permute-start.13
  60.0 1.3 %collective-permute-done.13 = f32[128,256]{1,0:T(8,128)S(1)} collective-permute-done((f32[128,256]{1,0:T(8,128)S(1)}, f32[128,256]{1,0:T(8,128)S(1)}, u32[]{:S(2)}, u32[]{:S(2)}) %collective-permute-start.13) | collective-permute-done | bytes 131104 | tf_op jit(solution)/shard_map/ppermute | solution.py:296
  61.3 0.9 %collective-permute-start.15 = (f32[64,256]{1,0:T(8,128)S(1)}, f32[64,256]{1,0:T(8,128)S(1)}, u32[]{:S(2)}, u32[]{:S(2)}) collective-permute-start(f32[64,256]{1,0:T(8,128)S(1)} %slice.42), channel_id=1, source_target_pairs={{0,2},{1,5},{2,0},{3,7},{4,6},{5,1},{6,4},{7,3},{8,10},{9,13},{10,... | collective-permute-start | bytes 196616 | tf_op jit(solution)/shard_map/ppermute | solution.py:296
  62.2 2.4 %collective-permute-start.14 = (f32[32,256]{1,0:T(8,128)S(1)}, f32[32,256]{1,0:T(8,128)S(1)}, u32[]{:S(2)}, u32[]{:S(2)}) collective-permute-start(f32[32,256]{1,0:T(8,128)S(1)} %slice.41), channel_id=1, source_target_pairs={{0,6},{1,7},{2,4},{3,5},{4,2},{5,3},{6,0},{7,1},{8,14},{9,15},{10,... | collective-permute-start | bytes 98312 | tf_op jit(solution)/shard_map/ppermute | solution.py:296
  64.6 1.5 %collective-permute-done.15 = f32[64,256]{1,0:T(8,128)S(1)} collective-permute-done((f32[64,256]{1,0:T(8,128)S(1)}, f32[64,256]{1,0:T(8,128)S(1)}, u32[]{:S(2)}, u32[]{:S(2)}) %collective-permute-start.15) | collective-permute-done | bytes 65568 | tf_op jit(solution)/shard_map/ppermute | solution.py:296
  66.2 0.1 collective-permute-start.16
  66.3 2.0 %collective-permute-done.14 = f32[32,256]{1,0:T(8,128)S(1)} collective-permute-done((f32[32,256]{1,0:T(8,128)S(1)}, f32[32,256]{1,0:T(8,128)S(1)}, u32[]{:S(2)}, u32[]{:S(2)}) %collective-permute-start.14) | collective-permute-done | bytes 32800 | tf_op jit(solution)/shard_map/ppermute | solution.py:296
  68.2 0.0 collective-permute-done.16
  68.2 0.0 copy-done.3
  68.2 0.6 fusion.2
  (8 shorter events, 0.1 us)
Async XLA Ops:
  0.6 32.7 %copy-start = (bf16[768,1536]{1,0:T(8,128)(2,1)S(1)}, bf16[768,1536]{1,0:T(8,128)(2,1)}, u32[]{:S(2)}) copy-start(bf16[768,1536]{1,0:T(8,128)(2,1)} %a_ref.7) | copy-start | bytes 7077892
  0.6 1.1 %copy-start.1 = (bf16[192,1024]{1,0:T(8,128)(2,1)S(1)}, bf16[192,1024]{1,0:T(8,128)(2,1)}, u32[]{:S(2)}) copy-start(bf16[192,1024]{1,0:T(8,128)(2,1)} %lower_ref.1) | copy-start | bytes 1179652
  1.8 31.6 %copy-start.2 = (s32[4,12]{1,0:T(4,128)S(1)}, s32[4,12]{1,0:T(4,128)}, u32[]{:S(2)}) copy-start(s32[4,12]{1,0:T(4,128)} %struct_ref.8) | copy-start | bytes 580
  2.2 32.8 %collective-permute-start = (bf16[192,256]{1,0:T(8,128)(2,1)S(1)}, bf16[192,256]{1,0:T(8,128)(2,1)S(1)}, u32[]{:S(2)}, u32[]{:S(2)}) collective-permute-start(bf16[192,256]{1,0:T(8,128)(2,1)S(1)} %get-tuple-element.23), channel_id=1, source_target_pairs={{0,8},{1,9},{2,10},{3,11},{4,12},{5,13},{6,14},{7,15},{8,0},{9,1},... | collective-permute-start | bytes 294920 | tf_op jit(solution)/shard_map/ppermute | solution.py:296
  5.2 29.8 %collective-permute-start.1 = (bf16[192,256]{1,0:T(8,128)(2,1)S(1)}, bf16[192,256]{1,0:T(8,128)(2,1)S(1)}, u32[]{:S(2)}, u32[]{:S(2)}) collective-permute-start(bf16[192,256]{1,0:T(8,128)(2,1)S(1)} %get-tuple-element.24), channel_id=1, source_target_pairs={{0,16},{1,17},{2,18},{3,19},{4,20},{5,21},{6,22},{7,23},{8,24},{9,... | collective-permute-start | bytes 294920 | tf_op jit(solution)/shard_map/ppermute | solution.py:296
  6.7 28.3 %collective-permute-start.2 = (bf16[192,256]{1,0:T(8,128)(2,1)S(1)}, bf16[192,256]{1,0:T(8,128)(2,1)S(1)}, u32[]{:S(2)}, u32[]{:S(2)}) collective-permute-start(bf16[192,256]{1,0:T(8,128)(2,1)S(1)} %get-tuple-element.25), channel_id=1, source_target_pairs={{0,24},{1,25},{2,26},{3,27},{4,28},{5,29},{6,30},{7,31},{8,16},{9,... | collective-permute-start | bytes 294920 | tf_op jit(solution)/shard_map/ppermute | solution.py:296
  6.8 28.3 %collective-permute-start.3 = (bf16[192,256]{1,0:T(8,128)(2,1)S(1)}, bf16[192,256]{1,0:T(8,128)(2,1)S(1)}, u32[]{:S(2)}, u32[]{:S(2)}) collective-permute-start(bf16[192,256]{1,0:T(8,128)(2,1)S(1)} %get-tuple-element.22.own.own_ref), channel_id=1, source_target_pairs={{0,2},{1,3},{2,0},{3,1},{4,6},{5,7},{6,4},{7,5},{8,10},{9,11},{10,... | collective-permute-start | bytes 294920 | tf_op jit(solution)/shard_map/ppermute | solution.py:296
  35.1 18.1 %collective-permute-start.4 = (bf16[576,256]{1,0:T(8,128)(2,1)S(1)}, bf16[576,256]{1,0:T(8,128)(2,1)S(1)}, u32[]{:S(2)}, u32[]{:S(2)}) collective-permute-start(bf16[576,256]{1,0:T(8,128)(2,1)S(1)} %pair.1), channel_id=1, source_target_pairs={{0,4},{1,5},{2,6},{3,7},{4,0},{5,1},{6,2},{7,3},{8,12},{9,13},{10,... | collective-permute-start | bytes 884744 | tf_op jit(solution)/shard_map/ppermute | solution.py:296
  36.2 17.9 %collective-permute-start.6 = (s16[784,256]{1,0:T(8,128)(2,1)S(1)}, s16[784,256]{1,0:T(8,128)(2,1)S(1)}, u32[]{:S(2)}, u32[]{:S(2)}) collective-permute-start(s16[784,256]{1,0:T(8,128)(2,1)S(1)} %sums_d.1), channel_id=1, source_target_pairs={{0,24},{1,25},{2,26},{3,27},{4,28},{5,29},{6,30},{7,31},{8,16},{9,... | collective-permute-start | bytes 1204232 | tf_op jit(solution)/shard_map/ppermute | solution.py:296
  39.2 6.5 %collective-permute-start.7 = (bf16[384,256]{1,0:T(8,128)(2,1)S(1)}, bf16[384,256]{1,0:T(8,128)(2,1)S(1)}, u32[]{:S(2)}, u32[]{:S(2)}) collective-permute-start(bf16[384,256]{1,0:T(8,128)(2,1)S(1)} %slice.39.mine), channel_id=1, source_target_pairs={{0,1},{1,0},{2,3},{3,2},{4,5},{5,4},{6,7},{7,6},{8,9},{9,8},{10,11... | collective-permute-start | bytes 589832 | tf_op jit(solution)/shard_map/ppermute | solution.py:296
  39.3 7.7 %collective-permute-start.10 = (bf16[192,256]{1,0:T(8,128)(2,1)S(1)}, bf16[192,256]{1,0:T(8,128)(2,1)S(1)}, u32[]{:S(2)}, u32[]{:S(2)}) collective-permute-start(bf16[192,256]{1,0:T(8,128)(2,1)S(1)} %get-tuple-element.36), channel_id=1, source_target_pairs={{0,2},{1,3},{2,0},{3,1},{4,6},{5,7},{6,4},{7,5},{8,10},{9,11},{10,... | collective-permute-start | bytes 294920 | tf_op jit(solution)/shard_map/ppermute | solution.py:296
  40.9 8.2 %collective-permute-start.11 = (bf16[192,256]{1,0:T(8,128)(2,1)S(1)}, bf16[192,256]{1,0:T(8,128)(2,1)S(1)}, u32[]{:S(2)}, u32[]{:S(2)}) collective-permute-start(bf16[192,256]{1,0:T(8,128)(2,1)S(1)} %get-tuple-element.37), channel_id=1, source_target_pairs={{0,6},{1,7},{2,4},{3,5},{4,2},{5,3},{6,0},{7,1},{8,14},{9,15},{10,... | collective-permute-start | bytes 294920 | tf_op jit(solution)/shard_map/ppermute | solution.py:296
  45.8 11.2 %collective-permute-start.8 = (s16[784,256]{1,0:T(8,128)(2,1)S(1)}, s16[784,256]{1,0:T(8,128)(2,1)S(1)}, u32[]{:S(2)}, u32[]{:S(2)}) collective-permute-start(s16[784,256]{1,0:T(8,128)(2,1)S(1)} %get-tuple-element.32), channel_id=1, source_target_pairs={{0,8},{1,9},{2,10},{3,11},{4,12},{5,13},{6,14},{7,15},{8,0},{9,1},... | collective-permute-start | bytes 1204232 | tf_op jit(solution)/shard_map/ppermute | solution.py:296
  47.0 11.2 %collective-permute-start.9 = (s16[784,256]{1,0:T(8,128)(2,1)S(1)}, s16[784,256]{1,0:T(8,128)(2,1)S(1)}, u32[]{:S(2)}, u32[]{:S(2)}) collective-permute-start(s16[784,256]{1,0:T(8,128)(2,1)S(1)} %get-tuple-element.34), channel_id=1, source_target_pairs={{0,16},{1,17},{2,18},{3,19},{4,20},{5,21},{6,22},{7,23},{8,24},{9,... | collective-permute-start | bytes 1204232 | tf_op jit(solution)/shard_map/ppermute | solution.py:296
  53.4 1.5 %collective-permute-start.12 = (bf16[384,256]{1,0:T(8,128)(2,1)S(1)}, bf16[384,256]{1,0:T(8,128)(2,1)S(1)}, u32[]{:S(2)}, u32[]{:S(2)}) collective-permute-start(bf16[384,256]{1,0:T(8,128)(2,1)S(1)} %get-tuple-element.39), channel_id=1, source_target_pairs={{0,1},{1,0},{2,3},{3,2},{4,5},{5,4},{6,7},{7,6},{8,9},{9,8},{10,11... | collective-permute-start | bytes 589832 | tf_op jit(solution)/shard_map/ppermute | solution.py:296
  53.5 1.7 %collective-permute-start.5 = (bf16[384,256]{1,0:T(8,128)(2,1)S(1)}, bf16[384,256]{1,0:T(8,128)(2,1)S(1)}, u32[]{:S(2)}, u32[]{:S(2)}) collective-permute-start(bf16[384,256]{1,0:T(8,128)(2,1)S(1)} %slice.38.mine), channel_id=1, source_target_pairs={{0,1},{1,0},{2,3},{3,2},{4,5},{5,4},{6,7},{7,6},{8,9},{9,8},{10,11... | collective-permute-start | bytes 589832 | tf_op jit(solution)/shard_map/ppermute | solution.py:296
  56.3 11.9 %copy-start.3 = (f32[32,256]{1,0:T(8,128)S(1)}, f32[32,256]{1,0:T(8,128)}, u32[]{:S(2)}) copy-start(f32[32,256]{1,0:T(8,128)} %param.6) | copy-start | bytes 98308
  59.9 1.4 %collective-permute-start.13 = (f32[128,256]{1,0:T(8,128)S(1)}, f32[128,256]{1,0:T(8,128)S(1)}, u32[]{:S(2)}, u32[]{:S(2)}) collective-permute-start(f32[128,256]{1,0:T(8,128)S(1)} %slice.32), channel_id=1, source_target_pairs={{0,1},{1,0},{2,3},{3,2},{4,5},{5,4},{6,7},{7,6},{8,9},{9,8},{10,11... | collective-permute-start | bytes 393224 | tf_op jit(solution)/shard_map/ppermute | solution.py:296
  61.3 4.8 %collective-permute-start.15 = (f32[64,256]{1,0:T(8,128)S(1)}, f32[64,256]{1,0:T(8,128)S(1)}, u32[]{:S(2)}, u32[]{:S(2)}) collective-permute-start(f32[64,256]{1,0:T(8,128)S(1)} %slice.42), channel_id=1, source_target_pairs={{0,2},{1,5},{2,0},{3,7},{4,6},{5,1},{6,4},{7,3},{8,10},{9,13},{10,... | collective-permute-start | bytes 196616 | tf_op jit(solution)/shard_map/ppermute | solution.py:296
  62.2 6.0 %collective-permute-start.14 = (f32[32,256]{1,0:T(8,128)S(1)}, f32[32,256]{1,0:T(8,128)S(1)}, u32[]{:S(2)}, u32[]{:S(2)}) collective-permute-start(f32[32,256]{1,0:T(8,128)S(1)} %slice.41), channel_id=1, source_target_pairs={{0,6},{1,7},{2,4},{3,5},{4,2},{5,3},{6,0},{7,1},{8,14},{9,15},{10,... | collective-permute-start | bytes 98312 | tf_op jit(solution)/shard_map/ppermute | solution.py:296
  66.2 2.1 %collective-permute-start.16 = (f32[32,256]{1,0:T(8,128)S(1)}, f32[32,256]{1,0:T(8,128)S(1)}, u32[]{:S(2)}, u32[]{:S(2)}) collective-permute-start(f32[32,256]{1,0:T(8,128)S(1)} %slice_select_fusion), channel_id=1, source_target_pairs={{0,1},{1,0},{2,3},{3,2},{4,5},{5,4},{6,7},{7,6},{8,9},{9,8},{10,11... | collective-permute-start | bytes 98312 | tf_op jit(solution)/shard_map/ppermute | solution.py:296

commit v8 on v7

--- a/solution.py
+++ b/solution.py
@@ -100,12 +100,6 @@
     return found
 
 
-def column_power(value):
-    top = jnp.maximum(jnp.max(jnp.abs(value), axis=0, keepdims=True), 2e-34)
-    power = jnp.floor(jnp.log2(top)) + 1.0
-    return jnp.where(top >= jnp.exp2(power), power + 1.0, power)
-
-
 def put_tail(ref, powers, rows):
     row = lax.broadcasted_iota(jnp.int32, (TAIL, ref.shape[1]), 0)
     tail = jnp.zeros((TAIL, ref.shape[1]), jnp.float32)
@@ -172,7 +166,8 @@
         total = -jnp.dot(a_ref[rows], panel[...], preferred_element_type=jnp.float32)
         for i, ref in enumerate(outs):
             part = total[:, i * B : (i + 1) * B]
-            power = column_power(part)
+            top = jnp.maximum(jnp.max(jnp.abs(part), axis=0, keepdims=True), 2e-34)
+            power = jnp.floor(jnp.log2(top)) + 1.0
             ref[rows] = to_code(part * (jnp.exp2(15.0 - power) * FILL))
             powers[i].append(power)
     for ref, power in zip(outs, powers):

time: 69 us -> 69.2 us (level)
  transfers between devices with their start and end apart: 17 -> 17, of which waited for: 9 -> 9; matrix products, arithmetic and copies ran while one was open for 0% -> 0% of each run, Pallas kernels for 11% -> 10%
where the time goes in v8:
time: 69.2 us; the launch traced here: 68.9 us
  blocking collectives  24.5 us (35%)
  starting transfers between devices  19.5 us (28%)
  waiting for transfers between devices  13.1 us (19%)
  Pallas kernels  9.07 us (13%)
  local copies, waits for them, and re-layouts  1.2 us (2%)
  between operations  0.84 us (1%)
    all_gather x1, blocking collectives, line_body(): gathered = lax.all_gather(code, 'pcol', axis=0, tiled=True)  24.5 us
    ppermute x17, starting transfers between devices, send(): return lax.ppermute(value, AXES, found)  19.5 us
    ppermute x17, waiting for transfers between devices, send(): return lax.ppermute(value, AXES, found)  13.1 us
    pallas_call x2, Pallas kernels, sums(): call(functools.partial(sums_kernel, slots), (coded,) * outs, [SM, VM, VM]...  4.19 us
    pallas_call x2, Pallas kernels, own_half(): call(functools.partial(own_kernel, far), shape((rows, B), f32), [SM] + [V...  2.26 us
    pallas_call x1, Pallas kernels, line_body(): call(last_kernel, (shape((rows, B), bf16), shape((B, B), f32)), [SM] + [V...  1.71 us
  transfers between devices with their start and end apart: 17, of which 9 were waited for; matrix products, arithmetic and copies ran while one was open for 0% of the time, Pallas kernels for 10%

profile of v8, /device:TPU:0, one launch (start us, length us, event | category | flops | bytes accessed | tf_op | source)
XLA Modules:
  0.0 68.9 jit_solution(5280382221694205612)
XLA Ops:
  0.6 0.0 copy-start
  0.6 0.0 copy-start.1
  0.6 1.1 %copy-done.1 = bf16[192,1024]{1,0:T(8,128)(2,1)S(1)} copy-done((bf16[192,1024]{1,0:T(8,128)(2,1)S(1)}, bf16[192,1024]{1,0:T(8,128)(2,1)}, u32[]{:S(2)}) %copy-start.1) | copy-done | bytes 393240
  1.8 0.0 copy-start.2
  1.8 0.4 code.1
  2.2 3.0 %collective-permute-start = (bf16[192,256]{1,0:T(8,128)(2,1)S(1)}, bf16[192,256]{1,0:T(8,128)(2,1)S(1)}, u32[]{:S(2)}, u32[]{:S(2)}) collective-permute-start(bf16[192,256]{1,0:T(8,128)(2,1)S(1)} %get-tuple-element.23), channel_id=1, source_target_pairs={{0,8},{1,9},{2,10},{3,11},{4,12},{5,13},{6,14},{7,15},{8,0},{9,1},... | collective-permute-start | bytes 294920 | tf_op jit(solution)/shard_map/ppermute | solution.py:291
  5.2 1.5 %collective-permute-start.1 = (bf16[192,256]{1,0:T(8,128)(2,1)S(1)}, bf16[192,256]{1,0:T(8,128)(2,1)S(1)}, u32[]{:S(2)}, u32[]{:S(2)}) collective-permute-start(bf16[192,256]{1,0:T(8,128)(2,1)S(1)} %get-tuple-element.24), channel_id=1, source_target_pairs={{0,16},{1,17},{2,18},{3,19},{4,20},{5,21},{6,22},{7,23},{8,24},{9,... | collective-permute-start | bytes 294920 | tf_op jit(solution)/shard_map/ppermute | solution.py:291
  6.7 0.0 collective-permute-start.2
  6.8 2.0 %collective-permute-start.3 = (bf16[192,256]{1,0:T(8,128)(2,1)S(1)}, bf16[192,256]{1,0:T(8,128)(2,1)S(1)}, u32[]{:S(2)}, u32[]{:S(2)}) collective-permute-start(bf16[192,256]{1,0:T(8,128)(2,1)S(1)} %get-tuple-element.22.own.own_ref), channel_id=1, source_target_pairs={{0,2},{1,3},{2,0},{3,1},{4,6},{5,7},{6,4},{7,5},{8,10},{9,11},{10,... | collective-permute-start | bytes 294920 | tf_op jit(solution)/shard_map/ppermute | solution.py:291
  8.8 24.5 %all-gather.1.code_ref = s16[1536,768]{1,0:T(8,128)(2,1)S(1)} all-gather(s16[192,768]{1,0:T(8,128)(2,1)S(1)} %get-tuple-element.29), channel_id=1, replica_groups=mesh['prow'=4,'pcol'=8] {'pcol'}, dimensions={0}, use_global_device_ids=true | all-gather | bytes 2654208 | tf_op jit(solution)/shard_map/all_gather | solution.py:333
  33.3 0.0 copy-done
  33.3 0.0 copy-done.2
  33.3 1.6 %sums_d.1 = s16[784,256]{1,0:T(8,128)(2,1)S(1)} custom-call(s32[4,12]{1,0:T(4,128)S(1)} %copy-done.2, bf16[768,1536]{1,0:T(8,128)(2,1)S(1)} %copy-done, s16[1536,768]{1,0:T(8,128)(2,1)S(1)} %all-gather.1.code_ref), custom_call_target="tpu_custom_call" | custom-call | flops 1 | bytes 1 | tf_op jit(solution)/shard_map/sums_d/pallas_call | solution.py:338
  35.0 0.0 collective-permute-done.x
  35.0 0.0 collective-permute-done.1.y
  35.0 0.0 collective-permute-done.2.both
  35.0 0.1 route.1
  35.1 0.0 collective-permute-done.3.one_ref
  35.1 1.0 %collective-permute-start.4 = (bf16[576,256]{1,0:T(8,128)(2,1)S(1)}, bf16[576,256]{1,0:T(8,128)(2,1)S(1)}, u32[]{:S(2)}, u32[]{:S(2)}) collective-permute-start(bf16[576,256]{1,0:T(8,128)(2,1)S(1)} %pair.1), channel_id=1, source_target_pairs={{0,4},{1,5},{2,6},{3,7},{4,0},{5,1},{6,2},{7,3},{8,12},{9,13},{10,... | collective-permute-start | bytes 884744 | tf_op jit(solution)/shard_map/ppermute | solution.py:291
  36.2 2.6 %collective-permute-start.6 = (s16[784,256]{1,0:T(8,128)(2,1)S(1)}, s16[784,256]{1,0:T(8,128)(2,1)S(1)}, u32[]{:S(2)}, u32[]{:S(2)}) collective-permute-start(s16[784,256]{1,0:T(8,128)(2,1)S(1)} %sums_d.1), channel_id=1, source_target_pairs={{0,24},{1,25},{2,26},{3,27},{4,28},{5,29},{6,30},{7,31},{8,16},{9,... | collective-permute-start | bytes 1204232 | tf_op jit(solution)/shard_map/ppermute | solution.py:291
  38.7 0.1 collective-permute-start.7
  38.8 1.6 %collective-permute-start.10 = (bf16[192,256]{1,0:T(8,128)(2,1)S(1)}, bf16[192,256]{1,0:T(8,128)(2,1)S(1)}, u32[]{:S(2)}, u32[]{:S(2)}) collective-permute-start(bf16[192,256]{1,0:T(8,128)(2,1)S(1)} %get-tuple-element.36), channel_id=1, source_target_pairs={{0,2},{1,3},{2,0},{3,1},{4,6},{5,7},{6,4},{7,5},{8,10},{9,11},{10,... | collective-permute-start | bytes 294920 | tf_op jit(solution)/shard_map/ppermute | solution.py:291
  40.5 1.9 %collective-permute-start.11 = (bf16[192,256]{1,0:T(8,128)(2,1)S(1)}, bf16[192,256]{1,0:T(8,128)(2,1)S(1)}, u32[]{:S(2)}, u32[]{:S(2)}) collective-permute-start(bf16[192,256]{1,0:T(8,128)(2,1)S(1)} %get-tuple-element.37), channel_id=1, source_target_pairs={{0,6},{1,7},{2,4},{3,5},{4,2},{5,3},{6,0},{7,1},{8,14},{9,15},{10,... | collective-permute-start | bytes 294920 | tf_op jit(solution)/shard_map/ppermute | solution.py:291
  42.3 2.6 %sums_xy.1 = (s16[784,256]{1,0:T(8,128)(2,1)S(1)}, s16[784,256]{1,0:T(8,128)(2,1)S(1)}) custom-call(s32[4,12]{1,0:T(4,128)S(1)} %copy-done.2, bf16[768,1536]{1,0:T(8,128)(2,1)S(1)} %copy-done, s16[1536,768]{1,0:T(8,128)(2,1)S(1)} %all-gather.1.code_ref), custom_call_target="tpu_custom_call" | custom-call | flops 1 | bytes 1 | tf_op jit(solution)/shard_map/sums_xy/pallas_call | solution.py:338
  44.9 0.0 collective-permute-done.7.theirs
  44.9 1.6 %collective-permute-start.8 = (s16[784,256]{1,0:T(8,128)(2,1)S(1)}, s16[784,256]{1,0:T(8,128)(2,1)S(1)}, u32[]{:S(2)}, u32[]{:S(2)}) collective-permute-start(s16[784,256]{1,0:T(8,128)(2,1)S(1)} %get-tuple-element.32), channel_id=1, source_target_pairs={{0,8},{1,9},{2,10},{3,11},{4,12},{5,13},{6,14},{7,15},{8,0},{9,1},... | collective-permute-start | bytes 1204232 | tf_op jit(solution)/shard_map/ppermute | solution.py:291
  46.5 1.1 %own.2.near_ref = f32[768,256]{1,0:T(8,128)S(1)} custom-call(s32[4,12]{1,0:T(4,128)S(1)} %copy-done.2, bf16[768,1536]{1,0:T(8,128)(2,1)S(1)} %copy-done, bf16[384,256]{1,0:T(8,128)(2,1)S(1)} %slice.39.mine, bf16[384,256]{1,0:T(8,128)(2,1)S(1)} %collective-permute-done.7.theirs), custom_call_target="tpu_custom_call" | custom-call | flops 1 | bytes 1 | tf_op jit(solution)/shard_map/own/pallas_call | solution.py:366
  47.6 0.0 collective-permute-done.10.one
  47.6 0.2 collective-permute-start.9
  47.8 1.4 %collective-permute-done.11.three = bf16[192,256]{1,0:T(8,128)(2,1)S(1)} collective-permute-done((bf16[192,256]{1,0:T(8,128)(2,1)S(1)}, bf16[192,256]{1,0:T(8,128)(2,1)S(1)}, u32[]{:S(2)}, u32[]{:S(2)}) %collective-permute-start.11) | collective-permute-done | bytes 98336 | tf_op jit(solution)/shard_map/ppermute | solution.py:291
  49.1 4.1 %collective-permute-done.4.two = bf16[576,256]{1,0:T(8,128)(2,1)S(1)} collective-permute-done((bf16[576,256]{1,0:T(8,128)(2,1)S(1)}, bf16[576,256]{1,0:T(8,128)(2,1)S(1)}, u32[]{:S(2)}, u32[]{:S(2)}) %collective-permute-start.4) | collective-permute-done | bytes 294944 | tf_op jit(solution)/shard_map/ppermute | solution.py:291
  53.3 0.1 share.1
  53.3 0.1 collective-permute-start.12
  53.4 0.6 collective-permute-start.5
  54.0 0.0 collective-permute-done.6.came_ref
  54.0 0.1 base.1.refs_0_
  54.1 0.7 %collective-permute-done.12.came = bf16[384,256]{1,0:T(8,128)(2,1)S(1)} collective-permute-done((bf16[384,256]{1,0:T(8,128)(2,1)S(1)}, bf16[384,256]{1,0:T(8,128)(2,1)S(1)}, u32[]{:S(2)}, u32[]{:S(2)}) %collective-permute-start.12) | collective-permute-done | bytes 196640 | tf_op jit(solution)/shard_map/ppermute | solution.py:291
  54.9 0.2 turn.1.lower
  55.0 0.1 collective-permute-done.5.theirs
  55.1 1.1 %own.3.own_ref = f32[768,256]{1,0:T(8,128)S(1)} custom-call(s32[4,12]{1,0:T(4,128)S(1)} %copy-done.2, bf16[768,1536]{1,0:T(8,128)(2,1)S(1)} %copy-done, bf16[384,256]{1,0:T(8,128)(2,1)S(1)} %slice.38.mine, bf16[384,256]{1,0:T(8,128)(2,1)S(1)} %collective-permute-done.5.theirs, f32[768,256]{1,0:T(8,128)S(1)} %base.1.refs_0_), custom_call_target="tpu_custom_call" | custom-call | flops 1 | bytes 1 | tf_op jit(solution)/shard_map/own/pallas_call | solution.py:366
  56.3 0.0 copy-start.3
  56.3 1.3 %collective-permute-done.8.came_x = s16[784,256]{1,0:T(8,128)(2,1)S(1)} collective-permute-done((s16[784,256]{1,0:T(8,128)(2,1)S(1)}, s16[784,256]{1,0:T(8,128)(2,1)S(1)}, u32[]{:S(2)}, u32[]{:S(2)}) %collective-permute-start.8) | collective-permute-done | bytes 401440 | tf_op jit(solution)/shard_map/ppermute | solution.py:291
  57.6 0.9 %collective-permute-done.9.came_y = s16[784,256]{1,0:T(8,128)(2,1)S(1)} collective-permute-done((s16[784,256]{1,0:T(8,128)(2,1)S(1)}, s16[784,256]{1,0:T(8,128)(2,1)S(1)}, u32[]{:S(2)}, u32[]{:S(2)}) %collective-permute-start.9) | collective-permute-done | bytes 401440 | tf_op jit(solution)/shard_map/ppermute | solution.py:291
  58.5 1.7 %last.1 = (bf16[768,256]{1,0:T(8,128)(2,1)}, f32[256,256]{1,0:T(8,128)S(1)}) custom-call(s32[4,12]{1,0:T(4,128)S(1)} %copy-done.2, f32[768,256]{1,0:T(8,128)S(1)} %own.3.own_ref, s16[784,256]{1,0:T(8,128)(2,1)S(1)} %collective-permute-done.8.came_x, s16[784,256]{1,0:T(8,128)(2,1)S(1)} %collective-permute-done.9.came_y, bf16[256,768]{1,0:T(8,128)(2,1)S(1)} %turn.1.lower), custom_call_target="tpu_custom_call" | custom-call | flops 201326592 | bytes 1572864 | tf_op jit(solution)/shard_map/last/pallas_call | solution.py:394
  60.2 0.1 collective-permute-start.13
  60.3 1.3 %collective-permute-done.13 = f32[128,256]{1,0:T(8,128)S(1)} collective-permute-done((f32[128,256]{1,0:T(8,128)S(1)}, f32[128,256]{1,0:T(8,128)S(1)}, u32[]{:S(2)}, u32[]{:S(2)}) %collective-permute-start.13) | collective-permute-done | bytes 131104 | tf_op jit(solution)/shard_map/ppermute | solution.py:291
  61.7 0.7 %collective-permute-start.15 = (f32[64,256]{1,0:T(8,128)S(1)}, f32[64,256]{1,0:T(8,128)S(1)}, u32[]{:S(2)}, u32[]{:S(2)}) collective-permute-start(f32[64,256]{1,0:T(8,128)S(1)} %slice.42), channel_id=1, source_target_pairs={{0,2},{1,5},{2,0},{3,7},{4,6},{5,1},{6,4},{7,3},{8,10},{9,13},{10,... | collective-permute-start | bytes 196616 | tf_op jit(solution)/shard_map/ppermute | solution.py:291
  62.4 2.2 %collective-permute-start.14 = (f32[32,256]{1,0:T(8,128)S(1)}, f32[32,256]{1,0:T(8,128)S(1)}, u32[]{:S(2)}, u32[]{:S(2)}) collective-permute-start(f32[32,256]{1,0:T(8,128)S(1)} %slice.41), channel_id=1, source_target_pairs={{0,6},{1,7},{2,4},{3,5},{4,2},{5,3},{6,0},{7,1},{8,14},{9,15},{10,... | collective-permute-start | bytes 98312 | tf_op jit(solution)/shard_map/ppermute | solution.py:291
  64.6 1.6 %collective-permute-done.15 = f32[64,256]{1,0:T(8,128)S(1)} collective-permute-done((f32[64,256]{1,0:T(8,128)S(1)}, f32[64,256]{1,0:T(8,128)S(1)}, u32[]{:S(2)}, u32[]{:S(2)}) %collective-permute-start.15) | collective-permute-done | bytes 65568 | tf_op jit(solution)/shard_map/ppermute | solution.py:291
  66.2 0.4 collective-permute-start.16
  66.6 1.7 %collective-permute-done.14 = f32[32,256]{1,0:T(8,128)S(1)} collective-permute-done((f32[32,256]{1,0:T(8,128)S(1)}, f32[32,256]{1,0:T(8,128)S(1)}, u32[]{:S(2)}, u32[]{:S(2)}) %collective-permute-start.14) | collective-permute-done | bytes 32800 | tf_op jit(solution)/shard_map/ppermute | solution.py:291
  68.3 0.0 collective-permute-done.16
  68.3 0.0 copy-done.3
  68.3 0.6 fusion.2
  (8 shorter events, 0.1 us)
Async XLA Ops:
  0.6 32.7 %copy-start = (bf16[768,1536]{1,0:T(8,128)(2,1)S(1)}, bf16[768,1536]{1,0:T(8,128)(2,1)}, u32[]{:S(2)}) copy-start(bf16[768,1536]{1,0:T(8,128)(2,1)} %a_ref.7) | copy-start | bytes 7077892
  0.6 1.1 %copy-start.1 = (bf16[192,1024]{1,0:T(8,128)(2,1)S(1)}, bf16[192,1024]{1,0:T(8,128)(2,1)}, u32[]{:S(2)}) copy-start(bf16[192,1024]{1,0:T(8,128)(2,1)} %lower_ref.1) | copy-start | bytes 1179652
  1.8 31.6 %copy-start.2 = (s32[4,12]{1,0:T(4,128)S(1)}, s32[4,12]{1,0:T(4,128)}, u32[]{:S(2)}) copy-start(s32[4,12]{1,0:T(4,128)} %struct_ref.8) | copy-start | bytes 580
  2.2 32.8 %collective-permute-start = (bf16[192,256]{1,0:T(8,128)(2,1)S(1)}, bf16[192,256]{1,0:T(8,128)(2,1)S(1)}, u32[]{:S(2)}, u32[]{:S(2)}) collective-permute-start(bf16[192,256]{1,0:T(8,128)(2,1)S(1)} %get-tuple-element.23), channel_id=1, source_target_pairs={{0,8},{1,9},{2,10},{3,11},{4,12},{5,13},{6,14},{7,15},{8,0},{9,1},... | collective-permute-start | bytes 294920 | tf_op jit(solution)/shard_map/ppermute | solution.py:291
  5.2 29.8 %collective-permute-start.1 = (bf16[192,256]{1,0:T(8,128)(2,1)S(1)}, bf16[192,256]{1,0:T(8,128)(2,1)S(1)}, u32[]{:S(2)}, u32[]{:S(2)}) collective-permute-start(bf16[192,256]{1,0:T(8,128)(2,1)S(1)} %get-tuple-element.24), channel_id=1, source_target_pairs={{0,16},{1,17},{2,18},{3,19},{4,20},{5,21},{6,22},{7,23},{8,24},{9,... | collective-permute-start | bytes 294920 | tf_op jit(solution)/shard_map/ppermute | solution.py:291
  6.7 28.2 %collective-permute-start.2 = (bf16[192,256]{1,0:T(8,128)(2,1)S(1)}, bf16[192,256]{1,0:T(8,128)(2,1)S(1)}, u32[]{:S(2)}, u32[]{:S(2)}) collective-permute-start(bf16[192,256]{1,0:T(8,128)(2,1)S(1)} %get-tuple-element.25), channel_id=1, source_target_pairs={{0,24},{1,25},{2,26},{3,27},{4,28},{5,29},{6,30},{7,31},{8,16},{9,... | collective-permute-start | bytes 294920 | tf_op jit(solution)/shard_map/ppermute | solution.py:291
  6.8 28.3 %collective-permute-start.3 = (bf16[192,256]{1,0:T(8,128)(2,1)S(1)}, bf16[192,256]{1,0:T(8,128)(2,1)S(1)}, u32[]{:S(2)}, u32[]{:S(2)}) collective-permute-start(bf16[192,256]{1,0:T(8,128)(2,1)S(1)} %get-tuple-element.22.own.own_ref), channel_id=1, source_target_pairs={{0,2},{1,3},{2,0},{3,1},{4,6},{5,7},{6,4},{7,5},{8,10},{9,11},{10,... | collective-permute-start | bytes 294920 | tf_op jit(solution)/shard_map/ppermute | solution.py:291
  35.1 18.1 %collective-permute-start.4 = (bf16[576,256]{1,0:T(8,128)(2,1)S(1)}, bf16[576,256]{1,0:T(8,128)(2,1)S(1)}, u32[]{:S(2)}, u32[]{:S(2)}) collective-permute-start(bf16[576,256]{1,0:T(8,128)(2,1)S(1)} %pair.1), channel_id=1, source_target_pairs={{0,4},{1,5},{2,6},{3,7},{4,0},{5,1},{6,2},{7,3},{8,12},{9,13},{10,... | collective-permute-start | bytes 884744 | tf_op jit(solution)/shard_map/ppermute | solution.py:291
  36.2 17.9 %collective-permute-start.6 = (s16[784,256]{1,0:T(8,128)(2,1)S(1)}, s16[784,256]{1,0:T(8,128)(2,1)S(1)}, u32[]{:S(2)}, u32[]{:S(2)}) collective-permute-start(s16[784,256]{1,0:T(8,128)(2,1)S(1)} %sums_d.1), channel_id=1, source_target_pairs={{0,24},{1,25},{2,26},{3,27},{4,28},{5,29},{6,30},{7,31},{8,16},{9,... | collective-permute-start | bytes 1204232 | tf_op jit(solution)/shard_map/ppermute | solution.py:291
  38.7 6.2 %collective-permute-start.7 = (bf16[384,256]{1,0:T(8,128)(2,1)S(1)}, bf16[384,256]{1,0:T(8,128)(2,1)S(1)}, u32[]{:S(2)}, u32[]{:S(2)}) collective-permute-start(bf16[384,256]{1,0:T(8,128)(2,1)S(1)} %slice.39.mine), channel_id=1, source_target_pairs={{0,1},{1,0},{2,3},{3,2},{4,5},{5,4},{6,7},{7,6},{8,9},{9,8},{10,11... | collective-permute-start | bytes 589832 | tf_op jit(solution)/shard_map/ppermute | solution.py:291
  38.8 8.8 %collective-permute-start.10 = (bf16[192,256]{1,0:T(8,128)(2,1)S(1)}, bf16[192,256]{1,0:T(8,128)(2,1)S(1)}, u32[]{:S(2)}, u32[]{:S(2)}) collective-permute-start(bf16[192,256]{1,0:T(8,128)(2,1)S(1)} %get-tuple-element.36), channel_id=1, source_target_pairs={{0,2},{1,3},{2,0},{3,1},{4,6},{5,7},{6,4},{7,5},{8,10},{9,11},{10,... | collective-permute-start | bytes 294920 | tf_op jit(solution)/shard_map/ppermute | solution.py:291
  40.5 8.7 %collective-permute-start.11 = (bf16[192,256]{1,0:T(8,128)(2,1)S(1)}, bf16[192,256]{1,0:T(8,128)(2,1)S(1)}, u32[]{:S(2)}, u32[]{:S(2)}) collective-permute-start(bf16[192,256]{1,0:T(8,128)(2,1)S(1)} %get-tuple-element.37), channel_id=1, source_target_pairs={{0,6},{1,7},{2,4},{3,5},{4,2},{5,3},{6,0},{7,1},{8,14},{9,15},{10,... | collective-permute-start | bytes 294920 | tf_op jit(solution)/shard_map/ppermute | solution.py:291
  44.9 12.7 %collective-permute-start.8 = (s16[784,256]{1,0:T(8,128)(2,1)S(1)}, s16[784,256]{1,0:T(8,128)(2,1)S(1)}, u32[]{:S(2)}, u32[]{:S(2)}) collective-permute-start(s16[784,256]{1,0:T(8,128)(2,1)S(1)} %get-tuple-element.32), channel_id=1, source_target_pairs={{0,8},{1,9},{2,10},{3,11},{4,12},{5,13},{6,14},{7,15},{8,0},{9,1},... | collective-permute-start | bytes 1204232 | tf_op jit(solution)/shard_map/ppermute | solution.py:291
  47.6 10.9 %collective-permute-start.9 = (s16[784,256]{1,0:T(8,128)(2,1)S(1)}, s16[784,256]{1,0:T(8,128)(2,1)S(1)}, u32[]{:S(2)}, u32[]{:S(2)}) collective-permute-start(s16[784,256]{1,0:T(8,128)(2,1)S(1)} %get-tuple-element.34), channel_id=1, source_target_pairs={{0,16},{1,17},{2,18},{3,19},{4,20},{5,21},{6,22},{7,23},{8,24},{9,... | collective-permute-start | bytes 1204232 | tf_op jit(solution)/shard_map/ppermute | solution.py:291
  53.3 1.5 %collective-permute-start.12 = (bf16[384,256]{1,0:T(8,128)(2,1)S(1)}, bf16[384,256]{1,0:T(8,128)(2,1)S(1)}, u32[]{:S(2)}, u32[]{:S(2)}) collective-permute-start(bf16[384,256]{1,0:T(8,128)(2,1)S(1)} %get-tuple-element.39), channel_id=1, source_target_pairs={{0,1},{1,0},{2,3},{3,2},{4,5},{5,4},{6,7},{7,6},{8,9},{9,8},{10,11... | collective-permute-start | bytes 589832 | tf_op jit(solution)/shard_map/ppermute | solution.py:291
  53.4 1.7 %collective-permute-start.5 = (bf16[384,256]{1,0:T(8,128)(2,1)S(1)}, bf16[384,256]{1,0:T(8,128)(2,1)S(1)}, u32[]{:S(2)}, u32[]{:S(2)}) collective-permute-start(bf16[384,256]{1,0:T(8,128)(2,1)S(1)} %slice.38.mine), channel_id=1, source_target_pairs={{0,1},{1,0},{2,3},{3,2},{4,5},{5,4},{6,7},{7,6},{8,9},{9,8},{10,11... | collective-permute-start | bytes 589832 | tf_op jit(solution)/shard_map/ppermute | solution.py:291
  56.3 12.0 %copy-start.3 = (f32[32,256]{1,0:T(8,128)S(1)}, f32[32,256]{1,0:T(8,128)}, u32[]{:S(2)}) copy-start(f32[32,256]{1,0:T(8,128)} %param.6) | copy-start | bytes 98308
  60.2 1.4 %collective-permute-start.13 = (f32[128,256]{1,0:T(8,128)S(1)}, f32[128,256]{1,0:T(8,128)S(1)}, u32[]{:S(2)}, u32[]{:S(2)}) collective-permute-start(f32[128,256]{1,0:T(8,128)S(1)} %slice.32), channel_id=1, source_target_pairs={{0,1},{1,0},{2,3},{3,2},{4,5},{5,4},{6,7},{7,6},{8,9},{9,8},{10,11... | collective-permute-start | bytes 393224 | tf_op jit(solution)/shard_map/ppermute | solution.py:291
  61.7 4.5 %collective-permute-start.15 = (f32[64,256]{1,0:T(8,128)S(1)}, f32[64,256]{1,0:T(8,128)S(1)}, u32[]{:S(2)}, u32[]{:S(2)}) collective-permute-start(f32[64,256]{1,0:T(8,128)S(1)} %slice.42), channel_id=1, source_target_pairs={{0,2},{1,5},{2,0},{3,7},{4,6},{5,1},{6,4},{7,3},{8,10},{9,13},{10,... | collective-permute-start | bytes 196616 | tf_op jit(solution)/shard_map/ppermute | solution.py:291
  62.4 5.9 %collective-permute-start.14 = (f32[32,256]{1,0:T(8,128)S(1)}, f32[32,256]{1,0:T(8,128)S(1)}, u32[]{:S(2)}, u32[]{:S(2)}) collective-permute-start(f32[32,256]{1,0:T(8,128)S(1)} %slice.41), channel_id=1, source_target_pairs={{0,6},{1,7},{2,4},{3,5},{4,2},{5,3},{6,0},{7,1},{8,14},{9,15},{10,... | collective-permute-start | bytes 98312 | tf_op jit(solution)/shard_map/ppermute | solution.py:291
  66.2 2.1 %collective-permute-start.16 = (f32[32,256]{1,0:T(8,128)S(1)}, f32[32,256]{1,0:T(8,128)S(1)}, u32[]{:S(2)}, u32[]{:S(2)}) collective-permute-start(f32[32,256]{1,0:T(8,128)S(1)} %slice_select_fusion), channel_id=1, source_target_pairs={{0,1},{1,0},{2,3},{3,2},{4,5},{5,4},{6,7},{7,6},{8,9},{9,8},{10,11... | collective-permute-start | bytes 98312 | tf_op jit(solution)/shard_map/ppermute | solution.py:291

commit v9 on v7

--- a/solution.py
+++ b/solution.py
@@ -379,7 +379,7 @@
         )(struct_list, ancestor_inverse, *args)
 
     near_own = own_half(0, pair, their_pair)
-    came_y = send(after(part_y, near_own), across(2))
+    came_y = send(part_y, across(2))
     from_three = send(to_three, along(3))
     base = small(base_kernel, shape((rows, B), f32), "base", came_d, near_own, flops=4 * 10**9)
     own = own_half(1, two, send(two, chip_swap), base)

time: 69 us -> 69.1 us (level)
  no operation moved by 1% of the time
where the time goes in v9:
time: 69.1 us; the launch traced here: 68.9 us
  blocking collectives  24.5 us (35%)
  starting transfers between devices  19.1 us (28%)
  waiting for transfers between devices  12.6 us (18%)
  Pallas kernels  9.95 us (14%)
  local copies, waits for them, and re-layouts  1.2 us (2%)
  between operations  0.84 us (1%)
    all_gather x1, blocking collectives, line_body(): gathered = lax.all_gather(code, 'pcol', axis=0, tiled=True)  24.5 us
    ppermute x17, starting transfers between devices, send(): return lax.ppermute(value, AXES, found)  19.1 us
    ppermute x17, waiting for transfers between devices, send(): return lax.ppermute(value, AXES, found)  12.6 us
    pallas_call x2, Pallas kernels, sums(): call(functools.partial(sums_kernel, slots), (coded,) * outs, [SM, VM, VM]...  5.04 us
    pallas_call x2, Pallas kernels, own_half(): call(functools.partial(own_kernel, far), shape((rows, B), f32), [SM] + [V...  2.3 us
    pallas_call x1, Pallas kernels, line_body(): call(last_kernel, (shape((rows, B), bf16), shape((B, B), f32)), [SM] + [V...  1.71 us
  transfers between devices with their start and end apart: 17, of which 9 were waited for; matrix products, arithmetic and copies ran while one was open for 0% of the time, Pallas kernels for 11%

profile of v9, /device:TPU:0, one launch (start us, length us, event | category | flops | bytes accessed | tf_op | source)
XLA Modules:
  0.0 68.9 jit_solution(773397342101753156)
XLA Ops:
  0.6 0.0 copy-start
  0.6 0.0 copy-start.1
  0.6 1.1 %copy-done.1 = bf16[192,1024]{1,0:T(8,128)(2,1)S(1)} copy-done((bf16[192,1024]{1,0:T(8,128)(2,1)S(1)}, bf16[192,1024]{1,0:T(8,128)(2,1)}, u32[]{:S(2)}) %copy-start.1) | copy-done | bytes 393240
  1.8 0.0 copy-start.2
  1.8 0.4 code.1
  2.2 3.0 %collective-permute-start = (bf16[192,256]{1,0:T(8,128)(2,1)S(1)}, bf16[192,256]{1,0:T(8,128)(2,1)S(1)}, u32[]{:S(2)}, u32[]{:S(2)}) collective-permute-start(bf16[192,256]{1,0:T(8,128)(2,1)S(1)} %get-tuple-element.22), channel_id=1, source_target_pairs={{0,8},{1,9},{2,10},{3,11},{4,12},{5,13},{6,14},{7,15},{8,0},{9,1},... | collective-permute-start | bytes 294920 | tf_op jit(solution)/shard_map/ppermute | solution.py:296
  5.2 1.5 %collective-permute-start.1 = (bf16[192,256]{1,0:T(8,128)(2,1)S(1)}, bf16[192,256]{1,0:T(8,128)(2,1)S(1)}, u32[]{:S(2)}, u32[]{:S(2)}) collective-permute-start(bf16[192,256]{1,0:T(8,128)(2,1)S(1)} %get-tuple-element.23), channel_id=1, source_target_pairs={{0,16},{1,17},{2,18},{3,19},{4,20},{5,21},{6,22},{7,23},{8,24},{9,... | collective-permute-start | bytes 294920 | tf_op jit(solution)/shard_map/ppermute | solution.py:296
  6.7 0.0 collective-permute-start.2
  6.8 2.0 %collective-permute-start.3 = (bf16[192,256]{1,0:T(8,128)(2,1)S(1)}, bf16[192,256]{1,0:T(8,128)(2,1)S(1)}, u32[]{:S(2)}, u32[]{:S(2)}) collective-permute-start(bf16[192,256]{1,0:T(8,128)(2,1)S(1)} %get-tuple-element.21.own.own_ref), channel_id=1, source_target_pairs={{0,2},{1,3},{2,0},{3,1},{4,6},{5,7},{6,4},{7,5},{8,10},{9,11},{10,... | collective-permute-start | bytes 294920 | tf_op jit(solution)/shard_map/ppermute | solution.py:296
  8.8 24.5 %all-gather.1.code_ref = s16[1536,768]{1,0:T(8,128)(2,1)S(1)} all-gather(s16[192,768]{1,0:T(8,128)(2,1)S(1)} %get-tuple-element.28), channel_id=1, replica_groups=mesh['prow'=4,'pcol'=8] {'pcol'}, dimensions={0}, use_global_device_ids=true | all-gather | bytes 2654208 | tf_op jit(solution)/shard_map/all_gather | solution.py:338
  33.3 0.0 copy-done
  33.3 0.0 copy-done.2
  33.3 1.6 %sums_d.1 = s16[784,256]{1,0:T(8,128)(2,1)S(1)} custom-call(s32[4,12]{1,0:T(4,128)S(1)} %copy-done.2, bf16[768,1536]{1,0:T(8,128)(2,1)S(1)} %copy-done, s16[1536,768]{1,0:T(8,128)(2,1)S(1)} %all-gather.1.code_ref), custom_call_target="tpu_custom_call" | custom-call | flops 1 | bytes 1 | tf_op jit(solution)/shard_map/sums_d/pallas_call | solution.py:343
  35.0 0.0 collective-permute-done.x
  35.0 0.0 collective-permute-done.1.y
  35.0 0.0 collective-permute-done.2.both
  35.0 0.1 route.1
  35.1 0.0 collective-permute-done.3.one_ref
  35.1 1.0 %collective-permute-start.4 = (bf16[576,256]{1,0:T(8,128)(2,1)S(1)}, bf16[576,256]{1,0:T(8,128)(2,1)S(1)}, u32[]{:S(2)}, u32[]{:S(2)}) collective-permute-start(bf16[576,256]{1,0:T(8,128)(2,1)S(1)} %pair.1), channel_id=1, source_target_pairs={{0,4},{1,5},{2,6},{3,7},{4,0},{5,1},{6,2},{7,3},{8,12},{9,13},{10,... | collective-permute-start | bytes 884744 | tf_op jit(solution)/shard_map/ppermute | solution.py:296
  36.2 2.6 %collective-permute-start.6 = (s16[784,256]{1,0:T(8,128)(2,1)S(1)}, s16[784,256]{1,0:T(8,128)(2,1)S(1)}, u32[]{:S(2)}, u32[]{:S(2)}) collective-permute-start(s16[784,256]{1,0:T(8,128)(2,1)S(1)} %sums_d.1), channel_id=1, source_target_pairs={{0,24},{1,25},{2,26},{3,27},{4,28},{5,29},{6,30},{7,31},{8,16},{9,... | collective-permute-start | bytes 1204232 | tf_op jit(solution)/shard_map/ppermute | solution.py:296
  38.7 0.1 collective-permute-start.7
  38.8 1.6 %collective-permute-start.10 = (bf16[192,256]{1,0:T(8,128)(2,1)S(1)}, bf16[192,256]{1,0:T(8,128)(2,1)S(1)}, u32[]{:S(2)}, u32[]{:S(2)}) collective-permute-start(bf16[192,256]{1,0:T(8,128)(2,1)S(1)} %get-tuple-element.34), channel_id=1, source_target_pairs={{0,2},{1,3},{2,0},{3,1},{4,6},{5,7},{6,4},{7,5},{8,10},{9,11},{10,... | collective-permute-start | bytes 294920 | tf_op jit(solution)/shard_map/ppermute | solution.py:296
  40.5 1.9 %collective-permute-start.11 = (bf16[192,256]{1,0:T(8,128)(2,1)S(1)}, bf16[192,256]{1,0:T(8,128)(2,1)S(1)}, u32[]{:S(2)}, u32[]{:S(2)}) collective-permute-start(bf16[192,256]{1,0:T(8,128)(2,1)S(1)} %get-tuple-element.35), channel_id=1, source_target_pairs={{0,6},{1,7},{2,4},{3,5},{4,2},{5,3},{6,0},{7,1},{8,14},{9,15},{10,... | collective-permute-start | bytes 294920 | tf_op jit(solution)/shard_map/ppermute | solution.py:296
  42.3 3.4 %sums_xy.1 = (s16[784,256]{1,0:T(8,128)(2,1)S(1)}, s16[784,256]{1,0:T(8,128)(2,1)S(1)}) custom-call(s32[4,12]{1,0:T(4,128)S(1)} %copy-done.2, bf16[768,1536]{1,0:T(8,128)(2,1)S(1)} %copy-done, s16[1536,768]{1,0:T(8,128)(2,1)S(1)} %all-gather.1.code_ref), custom_call_target="tpu_custom_call" | custom-call | flops 1 | bytes 1 | tf_op jit(solution)/shard_map/sums_xy/pallas_call | solution.py:343
  45.7 0.0 collective-permute-done.7.theirs
  45.8 0.1 collective-permute-start.8
  45.9 1.1 %own.2.near_ref = f32[768,256]{1,0:T(8,128)S(1)} custom-call(s32[4,12]{1,0:T(4,128)S(1)} %copy-done.2, bf16[768,1536]{1,0:T(8,128)(2,1)S(1)} %copy-done, bf16[384,256]{1,0:T(8,128)(2,1)S(1)} %slice.39.mine, bf16[384,256]{1,0:T(8,128)(2,1)S(1)} %collective-permute-done.7.theirs), custom_call_target="tpu_custom_call" | custom-call | flops 1 | bytes 1 | tf_op jit(solution)/shard_map/own/pallas_call | solution.py:371
  47.0 0.0 collective-permute-done.10.one
  47.0 1.2 %collective-permute-start.9 = (s16[784,256]{1,0:T(8,128)(2,1)S(1)}, s16[784,256]{1,0:T(8,128)(2,1)S(1)}, u32[]{:S(2)}, u32[]{:S(2)}) collective-permute-start(s16[784,256]{1,0:T(8,128)(2,1)S(1)} %get-tuple-element.32), channel_id=1, source_target_pairs={{0,16},{1,17},{2,18},{3,19},{4,20},{5,21},{6,22},{7,23},{8,24},{9,... | collective-permute-start | bytes 1204232 | tf_op jit(solution)/shard_map/ppermute | solution.py:296
  48.2 0.9 %collective-permute-done.11.three = bf16[192,256]{1,0:T(8,128)(2,1)S(1)} collective-permute-done((bf16[192,256]{1,0:T(8,128)(2,1)S(1)}, bf16[192,256]{1,0:T(8,128)(2,1)S(1)}, u32[]{:S(2)}, u32[]{:S(2)}) %collective-permute-start.11) | collective-permute-done | bytes 98336 | tf_op jit(solution)/shard_map/ppermute | solution.py:296
  49.1 4.1 %collective-permute-done.4.two = bf16[576,256]{1,0:T(8,128)(2,1)S(1)} collective-permute-done((bf16[576,256]{1,0:T(8,128)(2,1)S(1)}, bf16[576,256]{1,0:T(8,128)(2,1)S(1)}, u32[]{:S(2)}, u32[]{:S(2)}) %collective-permute-start.4) | collective-permute-done | bytes 294944 | tf_op jit(solution)/shard_map/ppermute | solution.py:296
  53.3 0.1 share.1
  53.4 0.1 collective-permute-start.12
  53.5 0.6 collective-permute-start.5
  54.0 0.0 collective-permute-done.6.came_ref
  54.0 0.1 base.1.refs_0_
  54.1 0.7 %collective-permute-done.12.came = bf16[384,256]{1,0:T(8,128)(2,1)S(1)} collective-permute-done((bf16[384,256]{1,0:T(8,128)(2,1)S(1)}, bf16[384,256]{1,0:T(8,128)(2,1)S(1)}, u32[]{:S(2)}, u32[]{:S(2)}) %collective-permute-start.12) | collective-permute-done | bytes 196640 | tf_op jit(solution)/shard_map/ppermute | solution.py:296
  54.9 0.2 turn.1.lower
  55.1 0.1 collective-permute-done.5.theirs
  55.1 1.2 %own.3.own_ref = f32[768,256]{1,0:T(8,128)S(1)} custom-call(s32[4,12]{1,0:T(4,128)S(1)} %copy-done.2, bf16[768,1536]{1,0:T(8,128)(2,1)S(1)} %copy-done, bf16[384,256]{1,0:T(8,128)(2,1)S(1)} %slice.38.mine, bf16[384,256]{1,0:T(8,128)(2,1)S(1)} %collective-permute-done.5.theirs, f32[768,256]{1,0:T(8,128)S(1)} %base.1.refs_0_), custom_call_target="tpu_custom_call" | custom-call | flops 1 | bytes 1 | tf_op jit(solution)/shard_map/own/pallas_call | solution.py:371
  56.3 0.0 copy-start.3
  56.3 0.7 collective-permute-done.8.came_x
  57.0 1.2 %collective-permute-done.9.came_y = s16[784,256]{1,0:T(8,128)(2,1)S(1)} collective-permute-done((s16[784,256]{1,0:T(8,128)(2,1)S(1)}, s16[784,256]{1,0:T(8,128)(2,1)S(1)}, u32[]{:S(2)}, u32[]{:S(2)}) %collective-permute-start.9) | collective-permute-done | bytes 401440 | tf_op jit(solution)/shard_map/ppermute | solution.py:296
  58.2 1.7 %last.1 = (bf16[768,256]{1,0:T(8,128)(2,1)}, f32[256,256]{1,0:T(8,128)S(1)}) custom-call(s32[4,12]{1,0:T(4,128)S(1)} %copy-done.2, f32[768,256]{1,0:T(8,128)S(1)} %own.3.own_ref, s16[784,256]{1,0:T(8,128)(2,1)S(1)} %collective-permute-done.8.came_x, s16[784,256]{1,0:T(8,128)(2,1)S(1)} %collective-permute-done.9.came_y, bf16[256,768]{1,0:T(8,128)(2,1)S(1)} %turn.1.lower), custom_call_target="tpu_custom_call" | custom-call | flops 201326592 | bytes 1572864 | tf_op jit(solution)/shard_map/last/pallas_call | solution.py:399
  59.9 0.1 collective-permute-start.13
  60.0 1.3 %collective-permute-done.13 = f32[128,256]{1,0:T(8,128)S(1)} collective-permute-done((f32[128,256]{1,0:T(8,128)S(1)}, f32[128,256]{1,0:T(8,128)S(1)}, u32[]{:S(2)}, u32[]{:S(2)}) %collective-permute-start.13) | collective-permute-done | bytes 131104 | tf_op jit(solution)/shard_map/ppermute | solution.py:296
  61.3 0.9 %collective-permute-start.15 = (f32[64,256]{1,0:T(8,128)S(1)}, f32[64,256]{1,0:T(8,128)S(1)}, u32[]{:S(2)}, u32[]{:S(2)}) collective-permute-start(f32[64,256]{1,0:T(8,128)S(1)} %slice.42), channel_id=1, source_target_pairs={{0,2},{1,5},{2,0},{3,7},{4,6},{5,1},{6,4},{7,3},{8,10},{9,13},{10,... | collective-permute-start | bytes 196616 | tf_op jit(solution)/shard_map/ppermute | solution.py:296
  62.2 2.4 %collective-permute-start.14 = (f32[32,256]{1,0:T(8,128)S(1)}, f32[32,256]{1,0:T(8,128)S(1)}, u32[]{:S(2)}, u32[]{:S(2)}) collective-permute-start(f32[32,256]{1,0:T(8,128)S(1)} %slice.41), channel_id=1, source_target_pairs={{0,6},{1,7},{2,4},{3,5},{4,2},{5,3},{6,0},{7,1},{8,14},{9,15},{10,... | collective-permute-start | bytes 98312 | tf_op jit(solution)/shard_map/ppermute | solution.py:296
  64.6 1.5 %collective-permute-done.15 = f32[64,256]{1,0:T(8,128)S(1)} collective-permute-done((f32[64,256]{1,0:T(8,128)S(1)}, f32[64,256]{1,0:T(8,128)S(1)}, u32[]{:S(2)}, u32[]{:S(2)}) %collective-permute-start.15) | collective-permute-done | bytes 65568 | tf_op jit(solution)/shard_map/ppermute | solution.py:296
  66.2 0.1 collective-permute-start.16
  66.3 2.0 %collective-permute-done.14 = f32[32,256]{1,0:T(8,128)S(1)} collective-permute-done((f32[32,256]{1,0:T(8,128)S(1)}, f32[32,256]{1,0:T(8,128)S(1)}, u32[]{:S(2)}, u32[]{:S(2)}) %collective-permute-start.14) | collective-permute-done | bytes 32800 | tf_op jit(solution)/shard_map/ppermute | solution.py:296
  68.2 0.0 collective-permute-done.16
  68.2 0.0 copy-done.3
  68.2 0.6 fusion.2
  (8 shorter events, 0.1 us)
Async XLA Ops:
  0.6 32.7 %copy-start = (bf16[768,1536]{1,0:T(8,128)(2,1)S(1)}, bf16[768,1536]{1,0:T(8,128)(2,1)}, u32[]{:S(2)}) copy-start(bf16[768,1536]{1,0:T(8,128)(2,1)} %a_ref.7) | copy-start | bytes 7077892
  0.6 1.1 %copy-start.1 = (bf16[192,1024]{1,0:T(8,128)(2,1)S(1)}, bf16[192,1024]{1,0:T(8,128)(2,1)}, u32[]{:S(2)}) copy-start(bf16[192,1024]{1,0:T(8,128)(2,1)} %lower_ref.1) | copy-start | bytes 1179652
  1.8 31.6 %copy-start.2 = (s32[4,12]{1,0:T(4,128)S(1)}, s32[4,12]{1,0:T(4,128)}, u32[]{:S(2)}) copy-start(s32[4,12]{1,0:T(4,128)} %struct_ref.8) | copy-start | bytes 580
  2.2 32.8 %collective-permute-start = (bf16[192,256]{1,0:T(8,128)(2,1)S(1)}, bf16[192,256]{1,0:T(8,128)(2,1)S(1)}, u32[]{:S(2)}, u32[]{:S(2)}) collective-permute-start(bf16[192,256]{1,0:T(8,128)(2,1)S(1)} %get-tuple-element.22), channel_id=1, source_target_pairs={{0,8},{1,9},{2,10},{3,11},{4,12},{5,13},{6,14},{7,15},{8,0},{9,1},... | collective-permute-start | bytes 294920 | tf_op jit(solution)/shard_map/ppermute | solution.py:296
  5.2 29.8 %collective-permute-start.1 = (bf16[192,256]{1,0:T(8,128)(2,1)S(1)}, bf16[192,256]{1,0:T(8,128)(2,1)S(1)}, u32[]{:S(2)}, u32[]{:S(2)}) collective-permute-start(bf16[192,256]{1,0:T(8,128)(2,1)S(1)} %get-tuple-element.23), channel_id=1, source_target_pairs={{0,16},{1,17},{2,18},{3,19},{4,20},{5,21},{6,22},{7,23},{8,24},{9,... | collective-permute-start | bytes 294920 | tf_op jit(solution)/shard_map/ppermute | solution.py:296
  6.7 28.3 %collective-permute-start.2 = (bf16[192,256]{1,0:T(8,128)(2,1)S(1)}, bf16[192,256]{1,0:T(8,128)(2,1)S(1)}, u32[]{:S(2)}, u32[]{:S(2)}) collective-permute-start(bf16[192,256]{1,0:T(8,128)(2,1)S(1)} %get-tuple-element.24), channel_id=1, source_target_pairs={{0,24},{1,25},{2,26},{3,27},{4,28},{5,29},{6,30},{7,31},{8,16},{9,... | collective-permute-start | bytes 294920 | tf_op jit(solution)/shard_map/ppermute | solution.py:296
  6.8 28.3 %collective-permute-start.3 = (bf16[192,256]{1,0:T(8,128)(2,1)S(1)}, bf16[192,256]{1,0:T(8,128)(2,1)S(1)}, u32[]{:S(2)}, u32[]{:S(2)}) collective-permute-start(bf16[192,256]{1,0:T(8,128)(2,1)S(1)} %get-tuple-element.21.own.own_ref), channel_id=1, source_target_pairs={{0,2},{1,3},{2,0},{3,1},{4,6},{5,7},{6,4},{7,5},{8,10},{9,11},{10,... | collective-permute-start | bytes 294920 | tf_op jit(solution)/shard_map/ppermute | solution.py:296
  35.1 18.1 %collective-permute-start.4 = (bf16[576,256]{1,0:T(8,128)(2,1)S(1)}, bf16[576,256]{1,0:T(8,128)(2,1)S(1)}, u32[]{:S(2)}, u32[]{:S(2)}) collective-permute-start(bf16[576,256]{1,0:T(8,128)(2,1)S(1)} %pair.1), channel_id=1, source_target_pairs={{0,4},{1,5},{2,6},{3,7},{4,0},{5,1},{6,2},{7,3},{8,12},{9,13},{10,... | collective-permute-start | bytes 884744 | tf_op jit(solution)/shard_map/ppermute | solution.py:296
  36.2 17.9 %collective-permute-start.6 = (s16[784,256]{1,0:T(8,128)(2,1)S(1)}, s16[784,256]{1,0:T(8,128)(2,1)S(1)}, u32[]{:S(2)}, u32[]{:S(2)}) collective-permute-start(s16[784,256]{1,0:T(8,128)(2,1)S(1)} %sums_d.1), channel_id=1, source_target_pairs={{0,24},{1,25},{2,26},{3,27},{4,28},{5,29},{6,30},{7,31},{8,16},{9,... | collective-permute-start | bytes 1204232 | tf_op jit(solution)/shard_map/ppermute | solution.py:296
  38.7 7.0 %collective-permute-start.7 = (bf16[384,256]{1,0:T(8,128)(2,1)S(1)}, bf16[384,256]{1,0:T(8,128)(2,1)S(1)}, u32[]{:S(2)}, u32[]{:S(2)}) collective-permute-start(bf16[384,256]{1,0:T(8,128)(2,1)S(1)} %slice.39.mine), channel_id=1, source_target_pairs={{0,1},{1,0},{2,3},{3,2},{4,5},{5,4},{6,7},{7,6},{8,9},{9,8},{10,11... | collective-permute-start | bytes 589832 | tf_op jit(solution)/shard_map/ppermute | solution.py:296
  38.8 8.2 %collective-permute-start.10 = (bf16[192,256]{1,0:T(8,128)(2,1)S(1)}, bf16[192,256]{1,0:T(8,128)(2,1)S(1)}, u32[]{:S(2)}, u32[]{:S(2)}) collective-permute-start(bf16[192,256]{1,0:T(8,128)(2,1)S(1)} %get-tuple-element.34), channel_id=1, source_target_pairs={{0,2},{1,3},{2,0},{3,1},{4,6},{5,7},{6,4},{7,5},{8,10},{9,11},{10,... | collective-permute-start | bytes 294920 | tf_op jit(solution)/shard_map/ppermute | solution.py:296
  40.5 8.7 %collective-permute-start.11 = (bf16[192,256]{1,0:T(8,128)(2,1)S(1)}, bf16[192,256]{1,0:T(8,128)(2,1)S(1)}, u32[]{:S(2)}, u32[]{:S(2)}) collective-permute-start(bf16[192,256]{1,0:T(8,128)(2,1)S(1)} %get-tuple-element.35), channel_id=1, source_target_pairs={{0,6},{1,7},{2,4},{3,5},{4,2},{5,3},{6,0},{7,1},{8,14},{9,15},{10,... | collective-permute-start | bytes 294920 | tf_op jit(solution)/shard_map/ppermute | solution.py:296
  45.8 11.2 %collective-permute-start.8 = (s16[784,256]{1,0:T(8,128)(2,1)S(1)}, s16[784,256]{1,0:T(8,128)(2,1)S(1)}, u32[]{:S(2)}, u32[]{:S(2)}) collective-permute-start(s16[784,256]{1,0:T(8,128)(2,1)S(1)} %get-tuple-element.31), channel_id=1, source_target_pairs={{0,8},{1,9},{2,10},{3,11},{4,12},{5,13},{6,14},{7,15},{8,0},{9,1},... | collective-permute-start | bytes 1204232 | tf_op jit(solution)/shard_map/ppermute | solution.py:296
  47.0 11.1 %collective-permute-start.9 = (s16[784,256]{1,0:T(8,128)(2,1)S(1)}, s16[784,256]{1,0:T(8,128)(2,1)S(1)}, u32[]{:S(2)}, u32[]{:S(2)}) collective-permute-start(s16[784,256]{1,0:T(8,128)(2,1)S(1)} %get-tuple-element.32), channel_id=1, source_target_pairs={{0,16},{1,17},{2,18},{3,19},{4,20},{5,21},{6,22},{7,23},{8,24},{9,... | collective-permute-start | bytes 1204232 | tf_op jit(solution)/shard_map/ppermute | solution.py:296
  53.4 1.5 %collective-permute-start.12 = (bf16[384,256]{1,0:T(8,128)(2,1)S(1)}, bf16[384,256]{1,0:T(8,128)(2,1)S(1)}, u32[]{:S(2)}, u32[]{:S(2)}) collective-permute-start(bf16[384,256]{1,0:T(8,128)(2,1)S(1)} %get-tuple-element.37), channel_id=1, source_target_pairs={{0,1},{1,0},{2,3},{3,2},{4,5},{5,4},{6,7},{7,6},{8,9},{9,8},{10,11... | collective-permute-start | bytes 589832 | tf_op jit(solution)/shard_map/ppermute | solution.py:296
  53.5 1.7 %collective-permute-start.5 = (bf16[384,256]{1,0:T(8,128)(2,1)S(1)}, bf16[384,256]{1,0:T(8,128)(2,1)S(1)}, u32[]{:S(2)}, u32[]{:S(2)}) collective-permute-start(bf16[384,256]{1,0:T(8,128)(2,1)S(1)} %slice.38.mine), channel_id=1, source_target_pairs={{0,1},{1,0},{2,3},{3,2},{4,5},{5,4},{6,7},{7,6},{8,9},{9,8},{10,11... | collective-permute-start | bytes 589832 | tf_op jit(solution)/shard_map/ppermute | solution.py:296
  56.3 11.9 %copy-start.3 = (f32[32,256]{1,0:T(8,128)S(1)}, f32[32,256]{1,0:T(8,128)}, u32[]{:S(2)}) copy-start(f32[32,256]{1,0:T(8,128)} %param.6) | copy-start | bytes 98308
  59.9 1.4 %collective-permute-start.13 = (f32[128,256]{1,0:T(8,128)S(1)}, f32[128,256]{1,0:T(8,128)S(1)}, u32[]{:S(2)}, u32[]{:S(2)}) collective-permute-start(f32[128,256]{1,0:T(8,128)S(1)} %slice.32), channel_id=1, source_target_pairs={{0,1},{1,0},{2,3},{3,2},{4,5},{5,4},{6,7},{7,6},{8,9},{9,8},{10,11... | collective-permute-start | bytes 393224 | tf_op jit(solution)/shard_map/ppermute | solution.py:296
  61.3 4.8 %collective-permute-start.15 = (f32[64,256]{1,0:T(8,128)S(1)}, f32[64,256]{1,0:T(8,128)S(1)}, u32[]{:S(2)}, u32[]{:S(2)}) collective-permute-start(f32[64,256]{1,0:T(8,128)S(1)} %slice.42), channel_id=1, source_target_pairs={{0,2},{1,5},{2,0},{3,7},{4,6},{5,1},{6,4},{7,3},{8,10},{9,13},{10,... | collective-permute-start | bytes 196616 | tf_op jit(solution)/shard_map/ppermute | solution.py:296
  62.2 6.0 %collective-permute-start.14 = (f32[32,256]{1,0:T(8,128)S(1)}, f32[32,256]{1,0:T(8,128)S(1)}, u32[]{:S(2)}, u32[]{:S(2)}) collective-permute-start(f32[32,256]{1,0:T(8,128)S(1)} %slice.41), channel_id=1, source_target_pairs={{0,6},{1,7},{2,4},{3,5},{4,2},{5,3},{6,0},{7,1},{8,14},{9,15},{10,... | collective-permute-start | bytes 98312 | tf_op jit(solution)/shard_map/ppermute | solution.py:296
  66.2 2.1 %collective-permute-start.16 = (f32[32,256]{1,0:T(8,128)S(1)}, f32[32,256]{1,0:T(8,128)S(1)}, u32[]{:S(2)}, u32[]{:S(2)}) collective-permute-start(f32[32,256]{1,0:T(8,128)S(1)} %slice_select_fusion), channel_id=1, source_target_pairs={{0,1},{1,0},{2,3},{3,2},{4,5},{5,4},{6,7},{7,6},{8,9},{9,8},{10,11... | collective-permute-start | bytes 98312 | tf_op jit(solution)/shard_map/ppermute | solution.py:296

commit v10 on v7

--- a/solution.py
+++ b/solution.py
@@ -357,7 +357,7 @@
     )
     came_x = send(part_x, across(1))
     stay, to_one, to_two, to_three = small(
-        route_kernel, (piece,) * 4, "route", keep, rows_x, rows_y, rows_both, flops=8 * 10**9
+        route_kernel, (piece,) * 4, "route", keep, rows_x, rows_y, rows_both, flops=10**10
     )
     to_one, to_two, to_three, _ = lax.optimization_barrier((to_one, to_two, to_three, part_d))
     from_one = send(to_one, along(1))
@@ -381,7 +381,7 @@
     near_own = own_half(0, pair, their_pair)
     came_y = send(after(part_y, near_own), across(2))
     from_three = send(to_three, along(3))
-    base = small(base_kernel, shape((rows, B), f32), "base", came_d, near_own, flops=4 * 10**9)
+    base = small(base_kernel, shape((rows, B), f32), "base", came_d, near_own, flops=6 * 10**9)
     own = own_half(1, two, send(two, chip_swap), base)
     half_rows = shape((2 * shard, B), bf16)
     keep, give = small(

time: 69 us -> 69.1 us (level)
  starting transfers between devices: 19.6 us -> 18.3 us
  waiting for transfers between devices: 12.6 us -> 13.5 us
    ppermute x17, starting transfers between devices: 19.6 us -> 18.3 us  [send(): return lax.ppermute(value, AXES, found)]
    ppermute x17, waiting for transfers between devices: 12.6 us -> 13.5 us  [send(): return lax.ppermute(value, AXES, found)]
where the time goes in v10:
time: 69.1 us; the launch traced here: 68.8 us
  blocking collectives  24.5 us (35%)
  starting transfers between devices  18.3 us (26%)
  waiting for transfers between devices  13.5 us (20%)
  Pallas kernels  9.81 us (14%)
  local copies, waits for them, and re-layouts  1.2 us (2%)
  between operations  0.85 us (1%)
    all_gather x1, blocking collectives, line_body(): gathered = lax.all_gather(code, 'pcol', axis=0, tiled=True)  24.5 us
    ppermute x17, starting transfers between devices, send(): return lax.ppermute(value, AXES, found)  18.3 us
    ppermute x17, waiting for transfers between devices, send(): return lax.ppermute(value, AXES, found)  13.5 us
    pallas_call x2, Pallas kernels, sums(): call(functools.partial(sums_kernel, slots), (coded,) * outs, [SM, VM, VM]...  4.92 us
    pallas_call x2, Pallas kernels, own_half(): call(functools.partial(own_kernel, far), shape((rows, B), f32), [SM] + [V...  2.28 us
    pallas_call x1, Pallas kernels, line_body(): call(last_kernel, (shape((rows, B), bf16), shape((B, B), f32)), [SM] + [V...  1.71 us
  transfers between devices with their start and end apart: 17, of which 9 were waited for; matrix products, arithmetic and copies ran while one was open for 0% of the time, Pallas kernels for 11%

profile of v10, /device:TPU:0, one launch (start us, length us, event | category | flops | bytes accessed | tf_op | source)
XLA Modules:
  0.0 68.8 jit_solution(3895727423667781654)
XLA Ops:
  0.6 0.0 copy-start
  0.6 0.0 copy-start.1
  0.6 1.1 %copy-done.1 = bf16[192,1024]{1,0:T(8,128)(2,1)S(1)} copy-done((bf16[192,1024]{1,0:T(8,128)(2,1)S(1)}, bf16[192,1024]{1,0:T(8,128)(2,1)}, u32[]{:S(2)}) %copy-start.1) | copy-done | bytes 393240
  1.8 0.0 copy-start.2
  1.8 0.4 code.1
  2.2 3.0 %collective-permute-start = (bf16[192,256]{1,0:T(8,128)(2,1)S(1)}, bf16[192,256]{1,0:T(8,128)(2,1)S(1)}, u32[]{:S(2)}, u32[]{:S(2)}) collective-permute-start(bf16[192,256]{1,0:T(8,128)(2,1)S(1)} %get-tuple-element.23), channel_id=1, source_target_pairs={{0,8},{1,9},{2,10},{3,11},{4,12},{5,13},{6,14},{7,15},{8,0},{9,1},... | collective-permute-start | bytes 294920 | tf_op jit(solution)/shard_map/ppermute | solution.py:296
  5.2 1.5 %collective-permute-start.1 = (bf16[192,256]{1,0:T(8,128)(2,1)S(1)}, bf16[192,256]{1,0:T(8,128)(2,1)S(1)}, u32[]{:S(2)}, u32[]{:S(2)}) collective-permute-start(bf16[192,256]{1,0:T(8,128)(2,1)S(1)} %get-tuple-element.24), channel_id=1, source_target_pairs={{0,16},{1,17},{2,18},{3,19},{4,20},{5,21},{6,22},{7,23},{8,24},{9,... | collective-permute-start | bytes 294920 | tf_op jit(solution)/shard_map/ppermute | solution.py:296
  6.7 0.0 collective-permute-start.2
  6.8 2.0 %collective-permute-start.3 = (bf16[192,256]{1,0:T(8,128)(2,1)S(1)}, bf16[192,256]{1,0:T(8,128)(2,1)S(1)}, u32[]{:S(2)}, u32[]{:S(2)}) collective-permute-start(bf16[192,256]{1,0:T(8,128)(2,1)S(1)} %get-tuple-element.22.own.own_ref), channel_id=1, source_target_pairs={{0,2},{1,3},{2,0},{3,1},{4,6},{5,7},{6,4},{7,5},{8,10},{9,11},{10,... | collective-permute-start | bytes 294920 | tf_op jit(solution)/shard_map/ppermute | solution.py:296
  8.8 24.5 %all-gather.1.code_ref = s16[1536,768]{1,0:T(8,128)(2,1)S(1)} all-gather(s16[192,768]{1,0:T(8,128)(2,1)S(1)} %get-tuple-element.29), channel_id=1, replica_groups=mesh['prow'=4,'pcol'=8] {'pcol'}, dimensions={0}, use_global_device_ids=true | all-gather | bytes 2654208 | tf_op jit(solution)/shard_map/all_gather | solution.py:338
  33.3 0.0 copy-done
  33.3 0.0 copy-done.2
  33.3 1.6 %sums_d.1 = s16[784,256]{1,0:T(8,128)(2,1)S(1)} custom-call(s32[4,12]{1,0:T(4,128)S(1)} %copy-done.2, bf16[768,1536]{1,0:T(8,128)(2,1)S(1)} %copy-done, s16[1536,768]{1,0:T(8,128)(2,1)S(1)} %all-gather.1.code_ref), custom_call_target="tpu_custom_call" | custom-call | flops 1 | bytes 1 | tf_op jit(solution)/shard_map/sums_d/pallas_call | solution.py:343
  35.0 0.0 collective-permute-done.x
  35.0 0.0 collective-permute-done.1.y
  35.0 0.0 collective-permute-done.2.both
  35.0 0.1 route.1
  35.1 0.0 collective-permute-done.3.one_ref
  35.1 1.0 %collective-permute-start.4 = (bf16[576,256]{1,0:T(8,128)(2,1)S(1)}, bf16[576,256]{1,0:T(8,128)(2,1)S(1)}, u32[]{:S(2)}, u32[]{:S(2)}) collective-permute-start(bf16[576,256]{1,0:T(8,128)(2,1)S(1)} %pair.1), channel_id=1, source_target_pairs={{0,4},{1,5},{2,6},{3,7},{4,0},{5,1},{6,2},{7,3},{8,12},{9,13},{10,... | collective-permute-start | bytes 884744 | tf_op jit(solution)/shard_map/ppermute | solution.py:296
  36.2 2.4 %collective-permute-start.6 = (s16[784,256]{1,0:T(8,128)(2,1)S(1)}, s16[784,256]{1,0:T(8,128)(2,1)S(1)}, u32[]{:S(2)}, u32[]{:S(2)}) collective-permute-start(s16[784,256]{1,0:T(8,128)(2,1)S(1)} %sums_d.1), channel_id=1, source_target_pairs={{0,24},{1,25},{2,26},{3,27},{4,28},{5,29},{6,30},{7,31},{8,16},{9,... | collective-permute-start | bytes 1204232 | tf_op jit(solution)/shard_map/ppermute | solution.py:296
  38.6 0.1 collective-permute-start.7
  38.7 1.6 %collective-permute-start.10 = (bf16[192,256]{1,0:T(8,128)(2,1)S(1)}, bf16[192,256]{1,0:T(8,128)(2,1)S(1)}, u32[]{:S(2)}, u32[]{:S(2)}) collective-permute-start(bf16[192,256]{1,0:T(8,128)(2,1)S(1)} %get-tuple-element.36), channel_id=1, source_target_pairs={{0,2},{1,3},{2,0},{3,1},{4,6},{5,7},{6,4},{7,5},{8,10},{9,11},{10,... | collective-permute-start | bytes 294920 | tf_op jit(solution)/shard_map/ppermute | solution.py:296
  40.3 1.9 %collective-permute-start.11 = (bf16[192,256]{1,0:T(8,128)(2,1)S(1)}, bf16[192,256]{1,0:T(8,128)(2,1)S(1)}, u32[]{:S(2)}, u32[]{:S(2)}) collective-permute-start(bf16[192,256]{1,0:T(8,128)(2,1)S(1)} %get-tuple-element.37), channel_id=1, source_target_pairs={{0,6},{1,7},{2,4},{3,5},{4,2},{5,3},{6,0},{7,1},{8,14},{9,15},{10,... | collective-permute-start | bytes 294920 | tf_op jit(solution)/shard_map/ppermute | solution.py:296
  42.2 3.3 %sums_xy.1 = (s16[784,256]{1,0:T(8,128)(2,1)S(1)}, s16[784,256]{1,0:T(8,128)(2,1)S(1)}) custom-call(s32[4,12]{1,0:T(4,128)S(1)} %copy-done.2, bf16[768,1536]{1,0:T(8,128)(2,1)S(1)} %copy-done, s16[1536,768]{1,0:T(8,128)(2,1)S(1)} %all-gather.1.code_ref), custom_call_target="tpu_custom_call" | custom-call | flops 1 | bytes 1 | tf_op jit(solution)/shard_map/sums_xy/pallas_call | solution.py:343
  45.5 0.0 collective-permute-done.7.theirs
  45.5 1.2 %collective-permute-start.8 = (s16[784,256]{1,0:T(8,128)(2,1)S(1)}, s16[784,256]{1,0:T(8,128)(2,1)S(1)}, u32[]{:S(2)}, u32[]{:S(2)}) collective-permute-start(s16[784,256]{1,0:T(8,128)(2,1)S(1)} %get-tuple-element.32), channel_id=1, source_target_pairs={{0,8},{1,9},{2,10},{3,11},{4,12},{5,13},{6,14},{7,15},{8,0},{9,1},... | collective-permute-start | bytes 1204232 | tf_op jit(solution)/shard_map/ppermute | solution.py:296
  46.7 1.1 %own.2.near_ref = f32[768,256]{1,0:T(8,128)S(1)} custom-call(s32[4,12]{1,0:T(4,128)S(1)} %copy-done.2, bf16[768,1536]{1,0:T(8,128)(2,1)S(1)} %copy-done, bf16[384,256]{1,0:T(8,128)(2,1)S(1)} %slice.39.mine, bf16[384,256]{1,0:T(8,128)(2,1)S(1)} %collective-permute-done.7.theirs), custom_call_target="tpu_custom_call" | custom-call | flops 1 | bytes 1 | tf_op jit(solution)/shard_map/own/pallas_call | solution.py:371
  47.9 0.0 collective-permute-done.10.one
  47.9 0.1 collective-permute-start.9
  48.0 1.2 %collective-permute-done.11.three = bf16[192,256]{1,0:T(8,128)(2,1)S(1)} collective-permute-done((bf16[192,256]{1,0:T(8,128)(2,1)S(1)}, bf16[192,256]{1,0:T(8,128)(2,1)S(1)}, u32[]{:S(2)}, u32[]{:S(2)}) %collective-permute-start.11) | collective-permute-done | bytes 98336 | tf_op jit(solution)/shard_map/ppermute | solution.py:296
  49.1 4.1 %collective-permute-done.4.two = bf16[576,256]{1,0:T(8,128)(2,1)S(1)} collective-permute-done((bf16[576,256]{1,0:T(8,128)(2,1)S(1)}, bf16[576,256]{1,0:T(8,128)(2,1)S(1)}, u32[]{:S(2)}, u32[]{:S(2)}) %collective-permute-start.4) | collective-permute-done | bytes 294944 | tf_op jit(solution)/shard_map/ppermute | solution.py:296
  53.3 0.1 share.1
  53.4 0.1 collective-permute-start.12
  53.5 0.6 collective-permute-start.5
  54.0 0.0 collective-permute-done.6.came_ref
  54.0 0.1 base.1.refs_0_
  54.1 0.7 %collective-permute-done.12.came = bf16[384,256]{1,0:T(8,128)(2,1)S(1)} collective-permute-done((bf16[384,256]{1,0:T(8,128)(2,1)S(1)}, bf16[384,256]{1,0:T(8,128)(2,1)S(1)}, u32[]{:S(2)}, u32[]{:S(2)}) %collective-permute-start.12) | collective-permute-done | bytes 196640 | tf_op jit(solution)/shard_map/ppermute | solution.py:296
  54.9 0.2 turn.1.lower
  55.1 0.1 collective-permute-done.5.theirs
  55.1 1.1 %own.3.own_ref = f32[768,256]{1,0:T(8,128)S(1)} custom-call(s32[4,12]{1,0:T(4,128)S(1)} %copy-done.2, bf16[768,1536]{1,0:T(8,128)(2,1)S(1)} %copy-done, bf16[384,256]{1,0:T(8,128)(2,1)S(1)} %slice.38.mine, bf16[384,256]{1,0:T(8,128)(2,1)S(1)} %collective-permute-done.5.theirs, f32[768,256]{1,0:T(8,128)S(1)} %base.1.refs_0_), custom_call_target="tpu_custom_call" | custom-call | flops 1 | bytes 1 | tf_op jit(solution)/shard_map/own/pallas_call | solution.py:371
  56.3 0.0 copy-start.3
  56.3 1.0 %collective-permute-done.8.came_x = s16[784,256]{1,0:T(8,128)(2,1)S(1)} collective-permute-done((s16[784,256]{1,0:T(8,128)(2,1)S(1)}, s16[784,256]{1,0:T(8,128)(2,1)S(1)}, u32[]{:S(2)}, u32[]{:S(2)}) %collective-permute-start.8) | collective-permute-done | bytes 401440 | tf_op jit(solution)/shard_map/ppermute | solution.py:296
  57.3 1.4 %collective-permute-done.9.came_y = s16[784,256]{1,0:T(8,128)(2,1)S(1)} collective-permute-done((s16[784,256]{1,0:T(8,128)(2,1)S(1)}, s16[784,256]{1,0:T(8,128)(2,1)S(1)}, u32[]{:S(2)}, u32[]{:S(2)}) %collective-permute-start.9) | collective-permute-done | bytes 401440 | tf_op jit(solution)/shard_map/ppermute | solution.py:296
  58.8 1.7 %last.1 = (bf16[768,256]{1,0:T(8,128)(2,1)}, f32[256,256]{1,0:T(8,128)S(1)}) custom-call(s32[4,12]{1,0:T(4,128)S(1)} %copy-done.2, f32[768,256]{1,0:T(8,128)S(1)} %own.3.own_ref, s16[784,256]{1,0:T(8,128)(2,1)S(1)} %collective-permute-done.8.came_x, s16[784,256]{1,0:T(8,128)(2,1)S(1)} %collective-permute-done.9.came_y, bf16[256,768]{1,0:T(8,128)(2,1)S(1)} %turn.1.lower), custom_call_target="tpu_custom_call" | custom-call | flops 201326592 | bytes 1572864 | tf_op jit(solution)/shard_map/last/pallas_call | solution.py:399
  60.5 0.1 collective-permute-start.13
  60.6 1.3 %collective-permute-done.13 = f32[128,256]{1,0:T(8,128)S(1)} collective-permute-done((f32[128,256]{1,0:T(8,128)S(1)}, f32[128,256]{1,0:T(8,128)S(1)}, u32[]{:S(2)}, u32[]{:S(2)}) %collective-permute-start.13) | collective-permute-done | bytes 131104 | tf_op jit(solution)/shard_map/ppermute | solution.py:296
  61.9 0.3 collective-permute-start.15
  62.2 2.4 %collective-permute-start.14 = (f32[32,256]{1,0:T(8,128)S(1)}, f32[32,256]{1,0:T(8,128)S(1)}, u32[]{:S(2)}, u32[]{:S(2)}) collective-permute-start(f32[32,256]{1,0:T(8,128)S(1)} %slice.41), channel_id=1, source_target_pairs={{0,6},{1,7},{2,4},{3,5},{4,2},{5,3},{6,0},{7,1},{8,14},{9,15},{10,... | collective-permute-start | bytes 98312 | tf_op jit(solution)/shard_map/ppermute | solution.py:296
  64.6 2.3 %collective-permute-done.15 = f32[64,256]{1,0:T(8,128)S(1)} collective-permute-done((f32[64,256]{1,0:T(8,128)S(1)}, f32[64,256]{1,0:T(8,128)S(1)}, u32[]{:S(2)}, u32[]{:S(2)}) %collective-permute-start.15) | collective-permute-done | bytes 65568 | tf_op jit(solution)/shard_map/ppermute | solution.py:296
  67.0 0.0 collective-permute-start.16
  67.0 1.2 %collective-permute-done.14 = f32[32,256]{1,0:T(8,128)S(1)} collective-permute-done((f32[32,256]{1,0:T(8,128)S(1)}, f32[32,256]{1,0:T(8,128)S(1)}, u32[]{:S(2)}, u32[]{:S(2)}) %collective-permute-start.14) | collective-permute-done | bytes 32800 | tf_op jit(solution)/shard_map/ppermute | solution.py:296
  68.2 0.0 collective-permute-done.16
  68.2 0.0 copy-done.3
  68.2 0.6 fusion.2
  (8 shorter events, 0.1 us)
Async XLA Ops:
  0.6 32.7 %copy-start = (bf16[768,1536]{1,0:T(8,128)(2,1)S(1)}, bf16[768,1536]{1,0:T(8,128)(2,1)}, u32[]{:S(2)}) copy-start(bf16[768,1536]{1,0:T(8,128)(2,1)} %a_ref.7) | copy-start | bytes 7077892
  0.6 1.1 %copy-start.1 = (bf16[192,1024]{1,0:T(8,128)(2,1)S(1)}, bf16[192,1024]{1,0:T(8,128)(2,1)}, u32[]{:S(2)}) copy-start(bf16[192,1024]{1,0:T(8,128)(2,1)} %lower_ref.1) | copy-start | bytes 1179652
  1.8 31.6 %copy-start.2 = (s32[4,12]{1,0:T(4,128)S(1)}, s32[4,12]{1,0:T(4,128)}, u32[]{:S(2)}) copy-start(s32[4,12]{1,0:T(4,128)} %struct_ref.8) | copy-start | bytes 580
  2.2 32.8 %collective-permute-start = (bf16[192,256]{1,0:T(8,128)(2,1)S(1)}, bf16[192,256]{1,0:T(8,128)(2,1)S(1)}, u32[]{:S(2)}, u32[]{:S(2)}) collective-permute-start(bf16[192,256]{1,0:T(8,128)(2,1)S(1)} %get-tuple-element.23), channel_id=1, source_target_pairs={{0,8},{1,9},{2,10},{3,11},{4,12},{5,13},{6,14},{7,15},{8,0},{9,1},... | collective-permute-start | bytes 294920 | tf_op jit(solution)/shard_map/ppermute | solution.py:296
  5.2 29.8 %collective-permute-start.1 = (bf16[192,256]{1,0:T(8,128)(2,1)S(1)}, bf16[192,256]{1,0:T(8,128)(2,1)S(1)}, u32[]{:S(2)}, u32[]{:S(2)}) collective-permute-start(bf16[192,256]{1,0:T(8,128)(2,1)S(1)} %get-tuple-element.24), channel_id=1, source_target_pairs={{0,16},{1,17},{2,18},{3,19},{4,20},{5,21},{6,22},{7,23},{8,24},{9,... | collective-permute-start | bytes 294920 | tf_op jit(solution)/shard_map/ppermute | solution.py:296
  6.7 28.3 %collective-permute-start.2 = (bf16[192,256]{1,0:T(8,128)(2,1)S(1)}, bf16[192,256]{1,0:T(8,128)(2,1)S(1)}, u32[]{:S(2)}, u32[]{:S(2)}) collective-permute-start(bf16[192,256]{1,0:T(8,128)(2,1)S(1)} %get-tuple-element.25), channel_id=1, source_target_pairs={{0,24},{1,25},{2,26},{3,27},{4,28},{5,29},{6,30},{7,31},{8,16},{9,... | collective-permute-start | bytes 294920 | tf_op jit(solution)/shard_map/ppermute | solution.py:296
  6.8 28.3 %collective-permute-start.3 = (bf16[192,256]{1,0:T(8,128)(2,1)S(1)}, bf16[192,256]{1,0:T(8,128)(2,1)S(1)}, u32[]{:S(2)}, u32[]{:S(2)}) collective-permute-start(bf16[192,256]{1,0:T(8,128)(2,1)S(1)} %get-tuple-element.22.own.own_ref), channel_id=1, source_target_pairs={{0,2},{1,3},{2,0},{3,1},{4,6},{5,7},{6,4},{7,5},{8,10},{9,11},{10,... | collective-permute-start | bytes 294920 | tf_op jit(solution)/shard_map/ppermute | solution.py:296
  35.1 18.1 %collective-permute-start.4 = (bf16[576,256]{1,0:T(8,128)(2,1)S(1)}, bf16[576,256]{1,0:T(8,128)(2,1)S(1)}, u32[]{:S(2)}, u32[]{:S(2)}) collective-permute-start(bf16[576,256]{1,0:T(8,128)(2,1)S(1)} %pair.1), channel_id=1, source_target_pairs={{0,4},{1,5},{2,6},{3,7},{4,0},{5,1},{6,2},{7,3},{8,12},{9,13},{10,... | collective-permute-start | bytes 884744 | tf_op jit(solution)/shard_map/ppermute | solution.py:296
  36.2 17.9 %collective-permute-start.6 = (s16[784,256]{1,0:T(8,128)(2,1)S(1)}, s16[784,256]{1,0:T(8,128)(2,1)S(1)}, u32[]{:S(2)}, u32[]{:S(2)}) collective-permute-start(s16[784,256]{1,0:T(8,128)(2,1)S(1)} %sums_d.1), channel_id=1, source_target_pairs={{0,24},{1,25},{2,26},{3,27},{4,28},{5,29},{6,30},{7,31},{8,16},{9,... | collective-permute-start | bytes 1204232 | tf_op jit(solution)/shard_map/ppermute | solution.py:296
  38.6 6.9 %collective-permute-start.7 = (bf16[384,256]{1,0:T(8,128)(2,1)S(1)}, bf16[384,256]{1,0:T(8,128)(2,1)S(1)}, u32[]{:S(2)}, u32[]{:S(2)}) collective-permute-start(bf16[384,256]{1,0:T(8,128)(2,1)S(1)} %slice.39.mine), channel_id=1, source_target_pairs={{0,1},{1,0},{2,3},{3,2},{4,5},{5,4},{6,7},{7,6},{8,9},{9,8},{10,11... | collective-permute-start | bytes 589832 | tf_op jit(solution)/shard_map/ppermute | solution.py:296
  38.7 9.2 %collective-permute-start.10 = (bf16[192,256]{1,0:T(8,128)(2,1)S(1)}, bf16[192,256]{1,0:T(8,128)(2,1)S(1)}, u32[]{:S(2)}, u32[]{:S(2)}) collective-permute-start(bf16[192,256]{1,0:T(8,128)(2,1)S(1)} %get-tuple-element.36), channel_id=1, source_target_pairs={{0,2},{1,3},{2,0},{3,1},{4,6},{5,7},{6,4},{7,5},{8,10},{9,11},{10,... | collective-permute-start | bytes 294920 | tf_op jit(solution)/shard_map/ppermute | solution.py:296
  40.3 8.8 %collective-permute-start.11 = (bf16[192,256]{1,0:T(8,128)(2,1)S(1)}, bf16[192,256]{1,0:T(8,128)(2,1)S(1)}, u32[]{:S(2)}, u32[]{:S(2)}) collective-permute-start(bf16[192,256]{1,0:T(8,128)(2,1)S(1)} %get-tuple-element.37), channel_id=1, source_target_pairs={{0,6},{1,7},{2,4},{3,5},{4,2},{5,3},{6,0},{7,1},{8,14},{9,15},{10,... | collective-permute-start | bytes 294920 | tf_op jit(solution)/shard_map/ppermute | solution.py:296
  45.5 11.8 %collective-permute-start.8 = (s16[784,256]{1,0:T(8,128)(2,1)S(1)}, s16[784,256]{1,0:T(8,128)(2,1)S(1)}, u32[]{:S(2)}, u32[]{:S(2)}) collective-permute-start(s16[784,256]{1,0:T(8,128)(2,1)S(1)} %get-tuple-element.32), channel_id=1, source_target_pairs={{0,8},{1,9},{2,10},{3,11},{4,12},{5,13},{6,14},{7,15},{8,0},{9,1},... | collective-permute-start | bytes 1204232 | tf_op jit(solution)/shard_map/ppermute | solution.py:296
  47.9 10.9 %collective-permute-start.9 = (s16[784,256]{1,0:T(8,128)(2,1)S(1)}, s16[784,256]{1,0:T(8,128)(2,1)S(1)}, u32[]{:S(2)}, u32[]{:S(2)}) collective-permute-start(s16[784,256]{1,0:T(8,128)(2,1)S(1)} %get-tuple-element.34), channel_id=1, source_target_pairs={{0,16},{1,17},{2,18},{3,19},{4,20},{5,21},{6,22},{7,23},{8,24},{9,... | collective-permute-start | bytes 1204232 | tf_op jit(solution)/shard_map/ppermute | solution.py:296
  53.4 1.5 %collective-permute-start.12 = (bf16[384,256]{1,0:T(8,128)(2,1)S(1)}, bf16[384,256]{1,0:T(8,128)(2,1)S(1)}, u32[]{:S(2)}, u32[]{:S(2)}) collective-permute-start(bf16[384,256]{1,0:T(8,128)(2,1)S(1)} %get-tuple-element.39), channel_id=1, source_target_pairs={{0,1},{1,0},{2,3},{3,2},{4,5},{5,4},{6,7},{7,6},{8,9},{9,8},{10,11... | collective-permute-start | bytes 589832 | tf_op jit(solution)/shard_map/ppermute | solution.py:296
  53.5 1.7 %collective-permute-start.5 = (bf16[384,256]{1,0:T(8,128)(2,1)S(1)}, bf16[384,256]{1,0:T(8,128)(2,1)S(1)}, u32[]{:S(2)}, u32[]{:S(2)}) collective-permute-start(bf16[384,256]{1,0:T(8,128)(2,1)S(1)} %slice.38.mine), channel_id=1, source_target_pairs={{0,1},{1,0},{2,3},{3,2},{4,5},{5,4},{6,7},{7,6},{8,9},{9,8},{10,11... | collective-permute-start | bytes 589832 | tf_op jit(solution)/shard_map/ppermute | solution.py:296
  56.3 11.9 %copy-start.3 = (f32[32,256]{1,0:T(8,128)S(1)}, f32[32,256]{1,0:T(8,128)}, u32[]{:S(2)}) copy-start(f32[32,256]{1,0:T(8,128)} %param.6) | copy-start | bytes 98308
  60.5 1.4 %collective-permute-start.13 = (f32[128,256]{1,0:T(8,128)S(1)}, f32[128,256]{1,0:T(8,128)S(1)}, u32[]{:S(2)}, u32[]{:S(2)}) collective-permute-start(f32[128,256]{1,0:T(8,128)S(1)} %slice.32), channel_id=1, source_target_pairs={{0,1},{1,0},{2,3},{3,2},{4,5},{5,4},{6,7},{7,6},{8,9},{9,8},{10,11... | collective-permute-start | bytes 393224 | tf_op jit(solution)/shard_map/ppermute | solution.py:296
  61.9 5.0 %collective-permute-start.15 = (f32[64,256]{1,0:T(8,128)S(1)}, f32[64,256]{1,0:T(8,128)S(1)}, u32[]{:S(2)}, u32[]{:S(2)}) collective-permute-start(f32[64,256]{1,0:T(8,128)S(1)} %slice.42), channel_id=1, source_target_pairs={{0,2},{1,5},{2,0},{3,7},{4,6},{5,1},{6,4},{7,3},{8,10},{9,13},{10,... | collective-permute-start | bytes 196616 | tf_op jit(solution)/shard_map/ppermute | solution.py:296
  62.2 6.0 %collective-permute-start.14 = (f32[32,256]{1,0:T(8,128)S(1)}, f32[32,256]{1,0:T(8,128)S(1)}, u32[]{:S(2)}, u32[]{:S(2)}) collective-permute-start(f32[32,256]{1,0:T(8,128)S(1)} %slice.41), channel_id=1, source_target_pairs={{0,6},{1,7},{2,4},{3,5},{4,2},{5,3},{6,0},{7,1},{8,14},{9,15},{10,... | collective-permute-start | bytes 98312 | tf_op jit(solution)/shard_map/ppermute | solution.py:296
  67.0 1.2 %collective-permute-start.16 = (f32[32,256]{1,0:T(8,128)S(1)}, f32[32,256]{1,0:T(8,128)S(1)}, u32[]{:S(2)}, u32[]{:S(2)}) collective-permute-start(f32[32,256]{1,0:T(8,128)S(1)} %slice_select_fusion), channel_id=1, source_target_pairs={{0,1},{1,0},{2,3},{3,2},{4,5},{5,4},{6,7},{7,6},{8,9},{9,8},{10,11... | collective-permute-start | bytes 98312 | tf_op jit(solution)/shard_map/ppermute | solution.py:296
